TPU v7x, 32 devices: a whole 2x2x4 slice. The times are simulated.
32 devices in a mesh: section: 4 (over x, core), tp: 8 (over z, y).
Axes of the slice: x: 2, y: 2, z: 4, core: 2. Of those that a mesh axis runs over, the one named last changes fastest.
Arguments:
- grad_attn: bfloat16 [4, 8, 128, 128], P('section', 'tp'), may hold values from -6 to 6
- w_value: bfloat16 [4, 12288, 1024], P('section', 'tp'), may hold values from -0.0546875 to 0.0546875
- probs_own: bfloat16 [4, 8, 128, 128], P('section', 'tp'), may hold values from 0.0009994507 to 0.25
- probs_spare: bfloat16 [4, 8, 128, 128], P('section', 'tp'), may hold values from 0.0009994507 to 0.25
- evicted: int32 [4, 4], P('section'), may hold values from 0 to 1, as said below
- layer_input: bfloat16 [4, 128, 12288], P('section', None, 'tp'), may hold values from -6 to 6
- gain: float32 [4, 12288], P('section', 'tp'), may hold values from 0.1 to 1.9
Outputs:
- handed: bfloat16 [4, 128, 12288], P('section', None, 'tp')
Inputs may be any that keep to these rules, and one draw needn't show every extreme that they name: Section 0 has every tile evicted.
All inputs are finite; a program needn't handle non-finite values.
Results may differ from a plain program's by a relative error of at most 0.0049.
Values may be sent and summed in bfloat16 or wider, within the bound.
No kernel may reach another device: no remote copies, remote signals or barrier semaphores. Data moves between devices by JAX's collectives and lax.ppermute only.
A program may use at most 64 MiB of HBM per device.

v0:
```python
import functools

import jax
import jax.numpy as jnp
from jax import lax
from jax.experimental import pallas as pl
from jax.experimental.pallas import tpu as pltpu
from jax.sharding import PartitionSpec as P

D = 12288
LANES = 128
PIECES = 4
EXTRA = 16
HIDES = pl.CostEstimate(flops=1 << 35, bytes_accessed=1 << 25, transcendentals=0)


def passed_along(block, axis, distance):
    devices = range(lax.axis_size(axis))
    route = [((i - distance) % len(devices), i) for i in devices]
    return lax.ppermute(block, axis, route)


def swapped(block, axis, mask):
    return lax.ppermute(block, axis, [(i ^ mask, i) for i in range(lax.axis_size(axis))])


def in_vmem(array):
    return pltpu.with_memory_space_constraint(array, pltpu.VMEM)


def in_hbm(array):
    return pltpu.with_memory_space_constraint(array, pltpu.HBM)


def vmem_specs(count):
    return [pl.BlockSpec(memory_space=pltpu.VMEM)] * count


def as_row(column):
    return jnp.broadcast_to(column, (column.shape[0], column.shape[0])).T[:1]


def as_column(row):
    return jnp.broadcast_to(row, (row.shape[1], row.shape[1])).T[:, :1]


def split(values):
    parts = []
    for _ in range(3):
        parts.append(values.astype(jnp.bfloat16).astype(jnp.float32))
        values = values - parts[-1]
    return parts


def as_parts(row):
    rest = jnp.zeros((EXTRA - 3, row.shape[1]), jnp.float32)
    return jnp.concatenate(split(row) + [rest]).astype(jnp.bfloat16)


def pack_kernel(own_ref, grad_ref, spare_ref, evicted_ref, *refs):
    out_ref, spare_out, taken_ref, flags, sems = refs
    copies = [
        pltpu.make_async_copy(evicted_ref, flags, sems.at[0]),
        pltpu.make_async_copy(own_ref, out_ref.at[0], sems.at[1]),
        pltpu.make_async_copy(grad_ref, out_ref.at[1], sems.at[2]),
        pltpu.make_async_copy(spare_ref, spare_out, sems.at[3]),
    ]
    for copy in copies:
        copy.start()
    copies[0].wait()
    tiles = evicted_ref.shape[1]
    rows = taken_ref.shape[0] // tiles
    for tile in range(tiles):
        part = pl.ds(tile * rows, rows)
        taken = jnp.full((rows, taken_ref.shape[1]), flags[0, tile], jnp.int32)
        taken_ref[part, :] = taken.astype(jnp.float32).astype(taken_ref.dtype)
    for copy in copies[1:]:
        copy.wait()


def pack(own, grad, spare, evicted):
    return pl.pallas_call(
        pack_kernel,
        out_shape=(
            pltpu.VMEM((2, *own.shape), own.dtype),
            pltpu.VMEM(spare.shape, spare.dtype),
            pltpu.VMEM(own.shape, own.dtype),
        ),
        in_specs=[pl.BlockSpec(memory_space=pltpu.HBM)] * 4,
        out_specs=tuple(vmem_specs(3)),
        scratch_shapes=[
            pltpu.SMEM(evicted.shape, evicted.dtype),
            pltpu.SemaphoreType.DMA((4,)),
        ],
        cost_estimate=HIDES,
        compiler_params=pltpu.CompilerParams(vmem_limit_bytes=4 << 20),
    )(*map(in_hbm, (own, grad, spare, evicted)))


def reach_kernel(weight_ref, input_ref, gain_ref, reach_ref):
    tokens, features = input_ref.shape
    values = input_ref[...].astype(jnp.float32)
    reach_ref[tokens:, :] = jnp.zeros_like(reach_ref[tokens:, :])
    squares = as_row(jnp.sum(values * values, axis=1, keepdims=True))
    reach_ref[tokens:, :tokens] = as_parts(squares)
    gained = (values * gain_ref[...]).astype(jnp.bfloat16)
    reach = jnp.dot(gained, weight_ref[...], preferred_element_type=jnp.float32)
    reach_ref[:tokens, :] = reach.astype(reach_ref.dtype)


def reach_of(weights, inputs, gain):
    return pl.pallas_call(
        reach_kernel,
        out_shape=pltpu.VMEM((inputs.shape[0] + EXTRA, weights.shape[1]), jnp.bfloat16),
        in_specs=vmem_specs(3),
        out_specs=pl.BlockSpec(memory_space=pltpu.VMEM),
        cost_estimate=HIDES,
        compiler_params=pltpu.CompilerParams(vmem_limit_bytes=8 << 20),
    )(*map(in_vmem, (weights, inputs, gain)))


def mix_kernel(taken_ref, *refs):
    out_ref = refs[-1]
    taken = taken_ref[...]
    for j in range(out_ref.shape[0]):
        packed_ref, spare_ref = refs[len(refs) - 2 - j], refs[j]
        out_ref[j] = lax.dot_general(
            packed_ref[0] * (1 - taken) + spare_ref[...] * taken,
            packed_ref[1],
            (((0,), (0,)), ((), ())),
            preferred_element_type=jnp.float32,
        ).astype(out_ref.dtype)


def value_gradients(taken, heads):
    return pl.pallas_call(
        mix_kernel,
        out_shape=pltpu.VMEM((len(heads), *heads[0][1].shape), jnp.bfloat16),
        in_specs=vmem_specs(1 + 2 * len(heads)),
        out_specs=pl.BlockSpec(memory_space=pltpu.VMEM),
        cost_estimate=HIDES,
        compiler_params=pltpu.CompilerParams(vmem_limit_bytes=4 << 20),
    )(*map(in_vmem, (taken, *[spare for _, spare in heads], *[packed for packed, _ in heads[::-1]])))


def project_kernel(head_of, counts, *refs):
    blocks = refs[: len(counts)]
    rest = refs[len(counts) :]
    weight_ref, input_ref, gain_ref, *reach_refs, scaled_ref, sums_ref, flat = rest
    tokens, features = input_ref.shape
    place = 0
    for ref, count in zip(blocks, counts):
        for j in range(count):
            start = pl.multiple_of(head_of(place) * LANES, LANES)
            flat[:, pl.ds(start, LANES)] = ref[j]
            place += 1
    tile = 256 if features % 256 == 0 else features
    for start in range(0, features, tile):
        part = pl.ds(start, tile)
        grad_normed = lax.dot_general(
            flat[...],
            weight_ref[part, :],
            (((1,), (1,)), ((), ())),
            preferred_element_type=jnp.float32,
        )
        scaled_ref[:, part] = (grad_normed * gain_ref[:, part]).astype(scaled_ref.dtype)
    reach = sum(ref[:tokens, :].astype(jnp.float32) for ref in reach_refs)
    squares = sum(ref[tokens:, :tokens].astype(jnp.float32) for ref in reach_refs)
    squares = jnp.sum(squares, axis=0, keepdims=True)
    inner = jnp.sum(flat[...].astype(jnp.float32) * reach, axis=1, keepdims=True)
    sums_ref[:1, :] = squares
    sums_ref[1:, :] = as_row(inner)
    lane = lax.broadcasted_iota(jnp.int32, (tokens, LANES), 1)
    extra = jnp.zeros((tokens, LANES), jnp.float32)
    for j, part in enumerate(split(as_column(squares)) + split(inner)):
        extra = jnp.where(lane == j, part, extra)
    scaled_ref[:, features:] = extra.astype(scaled_ref.dtype)


def project(head_of, blocks, weights, inputs, gain, reaches):
    counts = tuple(block.shape[0] for block in blocks)
    tokens, features = inputs.shape
    return pl.pallas_call(
        functools.partial(project_kernel, head_of, counts),
        out_shape=(
            pltpu.VMEM((tokens, features + LANES), jnp.bfloat16),
            pltpu.VMEM((2, tokens), jnp.float32),
        ),
        in_specs=vmem_specs(len(blocks) + 3 + len(reaches)),
        out_specs=tuple(vmem_specs(2)),
        scratch_shapes=[pltpu.VMEM((tokens, weights.shape[1]), jnp.bfloat16)],
        cost_estimate=HIDES,
        compiler_params=pltpu.CompilerParams(vmem_limit_bytes=16 << 20),
    )(*map(in_vmem, (*blocks, weights, inputs, gain, *reaches)))


def finish_kernel(scaled_ref, input_ref, *refs):
    *sums_refs, out_ref, held, sems = refs
    tokens, features = input_ref.shape
    extra = scaled_ref[:, features:].astype(jnp.float32)
    lane = lax.broadcasted_iota(jnp.int32, extra.shape, 1)
    squares = jnp.sum(jnp.where(lane < 3, extra, 0.0), axis=1, keepdims=True)
    inner = jnp.sum(jnp.where(lane < 3, 0.0, extra), axis=1, keepdims=True)
    if sums_refs:
        sums = sum(ref[...] for ref in sums_refs)
        squares = squares + as_column(sums[:1])
        inner = inner + as_column(sums[1:])
    inv = 1.0 / jnp.sqrt(squares / D + 1e-05)
    factor = inner * (inv * inv * inv) / D
    rows = tokens // PIECES
    copies = []
    for j in range(PIECES):
        part = slice(j * rows, (j + 1) * rows)
        scaled = scaled_ref[part, :features].astype(jnp.float32)
        values = input_ref[part, :].astype(jnp.float32)
        held[part, :] = (scaled * inv[part] - values * factor[part]).astype(held.dtype)
        copies.append(pltpu.make_async_copy(held.at[part], out_ref.at[part], sems.at[j]))
        copies[-1].start()
    for copy in copies:
        copy.wait()


def finish(scaled, inputs, sums):
    return pl.pallas_call(
        finish_kernel,
        out_shape=pltpu.HBM(inputs.shape, jnp.bfloat16),
        in_specs=vmem_specs(2 + len(sums)),
        out_specs=pl.BlockSpec(memory_space=pltpu.HBM),
        scratch_shapes=[
            pltpu.VMEM(inputs.shape, jnp.bfloat16),
            pltpu.SemaphoreType.DMA((PIECES,)),
        ],
        compiler_params=pltpu.CompilerParams(vmem_limit_bytes=8 << 20),
    )(*map(in_vmem, (scaled, inputs, *sums)))


FAR, NEAR, SIDE = 4, 2, 1
LINE = (NEAR, FAR, FAR | NEAR)


def handed_over(block, sections, count, distance, mask):
    route = [
        ((s - distance) % sections * count + (i ^ mask), s * count + i)
        for s in range(sections)
        for i in range(count)
    ]
    return lax.ppermute(block, ("section", "tp"), route)


def gathered(pair, axis):
    if lax.axis_size(axis) != 8:
        return [lax.all_gather(pair[0], axis)], lambda place: place
    blocks = [pair] + [swapped(pair, axis, mask) for mask in LINE]
    masks = [far | side for far in (0, *LINE) for side in (0, SIDE)]

    def head_of(place):
        return lax.axis_index(axis) ^ masks[place]

    return blocks, head_of


def per_device(grad_attn, w_value, probs_own, probs_spare, evicted, layer_input, gain):
    sections, count = lax.axis_size("section"), lax.axis_size("tp")
    packed, spares, taken = pack(probs_own[0, 0], grad_attn[0, 0], probs_spare[0, 0], evicted)
    heads = []
    for mask in (0, SIDE) if count == 8 else (0,):
        spare = handed_over(spares, sections, count, sections // 2, mask)
        heads.append((swapped(packed, "tp", mask) if mask else packed, spare))
    weights, inputs = w_value[0], layer_input[0]
    next_input = passed_along(inputs, "section", -1)
    reach = reach_of(weights, inputs, gain)
    if count == 8:
        reaches = [reach, swapped(reach, "tp", SIDE)]
        reaches[1], next_input = lax.optimization_barrier((reaches[1], next_input))
    else:
        reaches = [lax.psum(reach, "tp")]
    pair = value_gradients(taken, heads)
    blocks, head_of = gathered(pair, "tp")
    scaled, sums = project(head_of, blocks, weights, inputs, gain, reaches)
    next_scaled = passed_along(scaled, "section", -1)
    next_sums = []
    for mask in LINE if count == 8 else ():
        next_sums.append(handed_over(sums, sections, count, -1, mask))
    return finish(next_scaled, next_input, next_sums)[None]


def solution(mesh):
    in_specs = (
        P("section", "tp", None, None),
        P("section", "tp", None),
        P("section", "tp", None, None),
        P("section", "tp", None, None),
        P("section", None),
        P("section", None, "tp"),
        P("section", "tp"),
    )
    out_specs = P("section", None, "tp")
    return jax.shard_map(
        per_device, mesh=mesh, in_specs=in_specs, out_specs=out_specs, check_vma=False
    )
```

profile of v0, /device:TPU:1, one launch (start us, length us, event | category | flops | bytes accessed | tf_op | source)
XLA Modules:
  0.0 28.3 jit_solution(9959726270016886812)
XLA Ops:
  0.0 0.0 copy-start.1
  0.0 0.0 copy-start
  0.0 0.0 copy-start.2
  0.0 1.0 %shard_map.73 = (bf16[2,128,128]{2,1,0:T(8,128)(2,1)S(1)}, bf16[128,128]{1,0:T(8,128)(2,1)S(1)}, bf16[128,128]{1,0:T(8,128)(2,1)S(1)}) custom-call(bf16[128,128]{1,0:T(8,128)(2,1)} %bitcast.11, bf16[128,128]{1,0:T(8,128)(2,1)} %bitcast.12, bf16[128,128]{1,0:T(8,128)(2,1)} %bitcast.13, s32[1,4]{1,0:T(1,128)} %evicted_ref.1), custom_call_target="tpu_custom_call" | custom-call | flops 34359738368 | bytes 33554432 | tf_op jit(solution)/shard_map/pallas_call | solution.py:82
  1.0 3.1 %collective-permute-start.1 = (bf16[128,128]{1,0:T(8,128)(2,1)S(1)}, bf16[128,128]{1,0:T(8,128)(2,1)S(1)}, u32[]{:S(2)}, u32[]{:S(2)}) collective-permute-start(bf16[128,128]{1,0:T(8,128)(2,1)S(1)} %get-tuple-element.13), channel_id=1, source_target_pairs={{17,0},{16,1},{19,2},{18,3},{21,4},{20,5},{23,6},{22,7},{25,8},{24... | collective-permute-start | bytes 98312 | tf_op jit(solution)/shard_map/ppermute | solution.py:247
  4.1 0.3 collective-permute-start
  4.3 0.1 collective-permute-start.2
  4.4 0.0 copy-done.1
  4.4 1.2 %collective-permute-start.7 = (bf16[128,1536]{1,0:T(8,128)(2,1)S(1)}, bf16[128,1536]{1,0:T(8,128)(2,1)S(1)}, u32[]{:S(2)}, u32[]{:S(2)}) collective-permute-start(bf16[128,1536]{1,0:T(8,128)(2,1)S(1)} %bitcast.8), channel_id=1, source_target_pairs={{8,0},{16,8},{24,16},{0,24},{9,1},{17,9},{25,17},{1,25},{10,2},{18... | collective-permute-start | bytes 1179656 | tf_op jit(solution)/shard_map/ppermute | solution.py:20
  5.7 0.0 copy-done
  5.7 0.0 copy-done.2
  5.7 0.6 %shard_map.75.refs_7_ = bf16[144,1024]{1,0:T(8,128)(2,1)S(1)} custom-call(bf16[1536,1024]{1,0:T(8,128)(2,1)S(1)} %bitcast.6, bf16[128,1536]{1,0:T(8,128)(2,1)S(1)} %bitcast.9, f32[1,1536]{1,0:T(1,128)S(1)} %copy-done.2), custom_call_target="tpu_custom_call" | custom-call | flops 34359738368 | bytes 33554432 | tf_op jit(solution)/shard_map/pallas_call | solution.py:112
  6.3 1.7 %collective-permute-start.6 = (bf16[144,1024]{1,0:T(8,128)(2,1)S(1)}, bf16[144,1024]{1,0:T(8,128)(2,1)S(1)}, u32[]{:S(2)}, u32[]{:S(2)}) collective-permute-start(bf16[144,1024]{1,0:T(8,128)(2,1)S(1)} %shard_map.75.refs_7_), channel_id=1, source_target_pairs={{1,0},{0,1},{3,2},{2,3},{5,4},{4,5},{7,6},{6,7},{9,8},{8,9},{11,10... | collective-permute-start | bytes 884744 | tf_op jit(solution)/shard_map/ppermute | solution.py:24
  8.0 0.0 collective-permute-done.1.refs_1_
  8.0 0.0 collective-permute-done.refs_0_
  8.0 0.0 collective-permute-done.2.refs_2_
  8.0 0.2 shard_map.74.refs_0_
  8.2 3.4 %collective-permute-start.5 = (bf16[2,128,128]{2,1,0:T(8,128)(2,1)S(1)}, bf16[2,128,128]{2,1,0:T(8,128)(2,1)S(1)}, u32[]{:S(2)}, u32[]{:S(2)}) collective-permute-start(bf16[2,128,128]{2,1,0:T(8,128)(2,1)S(1)} %shard_map.74.refs_0_), channel_id=1, source_target_pairs={{6,0},{7,1},{4,2},{5,3},{2,4},{3,5},{0,6},{1,7},{14,8},{15,9},{12,... | collective-permute-start | bytes 196616 | tf_op jit(solution)/shard_map/ppermute | solution.py:24
  11.6 0.0 collective-permute-start.4
  11.6 0.4 %collective-permute-start.3 = (bf16[2,128,128]{2,1,0:T(8,128)(2,1)S(1)}, bf16[2,128,128]{2,1,0:T(8,128)(2,1)S(1)}, u32[]{:S(2)}, u32[]{:S(2)}) collective-permute-start(bf16[2,128,128]{2,1,0:T(8,128)(2,1)S(1)} %shard_map.74.refs_0_), channel_id=1, source_target_pairs={{2,0},{3,1},{0,2},{1,3},{6,4},{7,5},{4,6},{5,7},{10,8},{11,9},{8,1... | collective-permute-start | bytes 196616 | tf_op jit(solution)/shard_map/ppermute | solution.py:24
  12.0 3.2 %collective-permute-done.6.refs_8_ = bf16[144,1024]{1,0:T(8,128)(2,1)S(1)} collective-permute-done((bf16[144,1024]{1,0:T(8,128)(2,1)S(1)}, bf16[144,1024]{1,0:T(8,128)(2,1)S(1)}, u32[]{:S(2)}, u32[]{:S(2)}) %collective-permute-start.6) | collective-permute-done | bytes 294944 | tf_op jit(solution)/shard_map/ppermute | solution.py:24
  15.2 0.0 collective-permute-done.7.input_ref
  15.2 0.0 collective-permute-done.5.refs_3_
  15.2 1.9 %collective-permute-done.4.refs_2_ = bf16[2,128,128]{2,1,0:T(8,128)(2,1)S(1)} collective-permute-done((bf16[2,128,128]{2,1,0:T(8,128)(2,1)S(1)}, bf16[2,128,128]{2,1,0:T(8,128)(2,1)S(1)}, u32[]{:S(2)}, u32[]{:S(2)}) %collective-permute-start.4) | collective-permute-done | bytes 65568 | tf_op jit(solution)/shard_map/ppermute | solution.py:24
  17.0 0.0 collective-permute-done.3.refs_1_
  17.0 1.3 %shard_map.76 = (bf16[128,1664]{1,0:T(8,128)(2,1)S(1)}, f32[2,128]{1,0:T(2,128)S(1)}) custom-call(bf16[2,128,128]{2,1,0:T(8,128)(2,1)S(1)} %shard_map.74.refs_0_, bf16[2,128,128]{2,1,0:T(8,128)(2,1)S(1)} %collective-permute-done.3.refs_1_, bf16[2,128,128]{2,1,0:T(8,128)(2,1)S(1)} %collective-permute-done.4.refs_2_, ...), custom_call_target="tpu_custom_call" | custom-call | flops 34359738368 | bytes 33554432 | tf_op jit(solution)/shard_map/pallas_call | solution.py:183
  18.3 1.9 %collective-permute-start.8 = (bf16[128,1664]{1,0:T(8,128)(2,1)S(1)}, bf16[128,1664]{1,0:T(8,128)(2,1)S(1)}, u32[]{:S(2)}, u32[]{:S(2)}) collective-permute-start(bf16[128,1664]{1,0:T(8,128)(2,1)S(1)} %get-tuple-element.16), channel_id=1, source_target_pairs={{8,0},{16,8},{24,16},{0,24},{9,1},{17,9},{25,17},{1,25},{10,2},{18... | collective-permute-start | bytes 1277960 | tf_op jit(solution)/shard_map/ppermute | solution.py:20
  20.2 1.8 %collective-permute-start.11 = (f32[2,128]{1,0:T(2,128)S(1)}, f32[2,128]{1,0:T(2,128)S(1)}, u32[]{:S(2)}, u32[]{:S(2)}) collective-permute-start(f32[2,128]{1,0:T(2,128)S(1)} %get-tuple-element.18), channel_id=1, source_target_pairs={{14,0},{15,1},{12,2},{13,3},{10,4},{11,5},{8,6},{9,7},{22,8},{23,9... | collective-permute-start | bytes 3080 | tf_op jit(solution)/shard_map/ppermute | solution.py:247
  22.0 0.8 %collective-permute-start.10 = (f32[2,128]{1,0:T(2,128)S(1)}, f32[2,128]{1,0:T(2,128)S(1)}, u32[]{:S(2)}, u32[]{:S(2)}) collective-permute-start(f32[2,128]{1,0:T(2,128)S(1)} %get-tuple-element.18), channel_id=1, source_target_pairs={{12,0},{13,1},{14,2},{15,3},{8,4},{9,5},{10,6},{11,7},{20,8},{21,9... | collective-permute-start | bytes 3080 | tf_op jit(solution)/shard_map/ppermute | solution.py:247
  22.8 2.1 %collective-permute-start.9 = (f32[2,128]{1,0:T(2,128)S(1)}, f32[2,128]{1,0:T(2,128)S(1)}, u32[]{:S(2)}, u32[]{:S(2)}) collective-permute-start(f32[2,128]{1,0:T(2,128)S(1)} %get-tuple-element.18), channel_id=1, source_target_pairs={{10,0},{11,1},{8,2},{9,3},{14,4},{15,5},{12,6},{13,7},{18,8},{19,9... | collective-permute-start | bytes 3080 | tf_op jit(solution)/shard_map/ppermute | solution.py:247
  25.0 1.0 %collective-permute-done.11.refs_2_ = f32[2,128]{1,0:T(2,128)S(1)} collective-permute-done((f32[2,128]{1,0:T(2,128)S(1)}, f32[2,128]{1,0:T(2,128)S(1)}, u32[]{:S(2)}, u32[]{:S(2)}) %collective-permute-start.11) | collective-permute-done | bytes 1056 | tf_op jit(solution)/shard_map/ppermute | solution.py:247
  25.9 0.9 %collective-permute-done.10.refs_1_ = f32[2,128]{1,0:T(2,128)S(1)} collective-permute-done((f32[2,128]{1,0:T(2,128)S(1)}, f32[2,128]{1,0:T(2,128)S(1)}, u32[]{:S(2)}, u32[]{:S(2)}) %collective-permute-start.10) | collective-permute-done | bytes 1056 | tf_op jit(solution)/shard_map/ppermute | solution.py:247
  26.8 0.1 collective-permute-done.9.refs_0_
  26.9 0.3 %collective-permute-done.8.scaled_ref = bf16[128,1664]{1,0:T(8,128)(2,1)S(1)} collective-permute-done((bf16[128,1664]{1,0:T(8,128)(2,1)S(1)}, bf16[128,1664]{1,0:T(8,128)(2,1)S(1)}, u32[]{:S(2)}, u32[]{:S(2)}) %collective-permute-start.8) | collective-permute-done | bytes 426016 | tf_op jit(solution)/shard_map/ppermute | solution.py:20
  27.2 1.1 %shard_map.77 = bf16[128,1536]{1,0:T(8,128)(2,1)} custom-call(bf16[128,1664]{1,0:T(8,128)(2,1)S(1)} %collective-permute-done.8.scaled_ref, bf16[128,1536]{1,0:T(8,128)(2,1)S(1)} %collective-permute-done.7.input_ref, f32[2,128]{1,0:T(2,128)S(1)} %collective-permute-done.9.refs_0_, f32[2,128]{1,0:T(2,128)S(1)} %collective-permute-done.10.refs_1_, ...), custom_call_target="tpu_custom_call" | custom-call | tf_op jit(solution)/shard_map/pallas_call | solution.py:224
Async XLA Ops:
  0.0 4.4 %copy-start.1 = (bf16[1,128,1536]{2,1,0:T(8,128)(2,1)S(1)}, bf16[1,128,1536]{2,1,0:T(8,128)(2,1)}, u32[]{:S(2)}) copy-start(bf16[1,128,1536]{2,1,0:T(8,128)(2,1)} %param.12) | copy-start | bytes 1179652
  0.0 5.7 %copy-start = (bf16[1,1536,1024]{2,1,0:T(8,128)(2,1)S(1)}, bf16[1,1536,1024]{2,1,0:T(8,128)(2,1)}, u32[]{:S(2)}) copy-start(bf16[1,1536,1024]{2,1,0:T(8,128)(2,1)} %param.8) | copy-start | bytes 9437188
  0.0 5.7 %copy-start.2 = (f32[1,1536]{1,0:T(1,128)S(1)}, f32[1,1536]{1,0:T(1,128)}, u32[]{:S(2)}) copy-start(f32[1,1536]{1,0:T(1,128)} %refs_6_.1) | copy-start | bytes 18436
  1.0 7.0 %collective-permute-start.1 = (bf16[128,128]{1,0:T(8,128)(2,1)S(1)}, bf16[128,128]{1,0:T(8,128)(2,1)S(1)}, u32[]{:S(2)}, u32[]{:S(2)}) collective-permute-start(bf16[128,128]{1,0:T(8,128)(2,1)S(1)} %get-tuple-element.13), channel_id=1, source_target_pairs={{17,0},{16,1},{19,2},{18,3},{21,4},{20,5},{23,6},{22,7},{25,8},{24... | collective-permute-start | bytes 98312 | tf_op jit(solution)/shard_map/ppermute | solution.py:247
  4.1 4.0 %collective-permute-start = (bf16[128,128]{1,0:T(8,128)(2,1)S(1)}, bf16[128,128]{1,0:T(8,128)(2,1)S(1)}, u32[]{:S(2)}, u32[]{:S(2)}) collective-permute-start(bf16[128,128]{1,0:T(8,128)(2,1)S(1)} %get-tuple-element.13), channel_id=1, source_target_pairs={{16,0},{17,1},{18,2},{19,3},{20,4},{21,5},{22,6},{23,7},{24,8},{25... | collective-permute-start | bytes 98312 | tf_op jit(solution)/shard_map/ppermute | solution.py:247
  4.3 3.7 %collective-permute-start.2 = (bf16[2,128,128]{2,1,0:T(8,128)(2,1)S(1)}, bf16[2,128,128]{2,1,0:T(8,128)(2,1)S(1)}, u32[]{:S(2)}, u32[]{:S(2)}) collective-permute-start(bf16[2,128,128]{2,1,0:T(8,128)(2,1)S(1)} %get-tuple-element.14.refs_3_), channel_id=1, source_target_pairs={{1,0},{0,1},{3,2},{2,3},{5,4},{4,5},{7,6},{6,7},{9,8},{8,9},{11,10... | collective-permute-start | bytes 196616 | tf_op jit(solution)/shard_map/ppermute | solution.py:24
  4.4 10.7 %collective-permute-start.7 = (bf16[128,1536]{1,0:T(8,128)(2,1)S(1)}, bf16[128,1536]{1,0:T(8,128)(2,1)S(1)}, u32[]{:S(2)}, u32[]{:S(2)}) collective-permute-start(bf16[128,1536]{1,0:T(8,128)(2,1)S(1)} %bitcast.8), channel_id=1, source_target_pairs={{8,0},{16,8},{24,16},{0,24},{9,1},{17,9},{25,17},{1,25},{10,2},{18... | collective-permute-start | bytes 1179656 | tf_op jit(solution)/shard_map/ppermute | solution.py:20
  6.3 8.9 %collective-permute-start.6 = (bf16[144,1024]{1,0:T(8,128)(2,1)S(1)}, bf16[144,1024]{1,0:T(8,128)(2,1)S(1)}, u32[]{:S(2)}, u32[]{:S(2)}) collective-permute-start(bf16[144,1024]{1,0:T(8,128)(2,1)S(1)} %shard_map.75.refs_7_), channel_id=1, source_target_pairs={{1,0},{0,1},{3,2},{2,3},{5,4},{4,5},{7,6},{6,7},{9,8},{8,9},{11,10... | collective-permute-start | bytes 884744 | tf_op jit(solution)/shard_map/ppermute | solution.py:24
  8.2 6.9 %collective-permute-start.5 = (bf16[2,128,128]{2,1,0:T(8,128)(2,1)S(1)}, bf16[2,128,128]{2,1,0:T(8,128)(2,1)S(1)}, u32[]{:S(2)}, u32[]{:S(2)}) collective-permute-start(bf16[2,128,128]{2,1,0:T(8,128)(2,1)S(1)} %shard_map.74.refs_0_), channel_id=1, source_target_pairs={{6,0},{7,1},{4,2},{5,3},{2,4},{3,5},{0,6},{1,7},{14,8},{15,9},{12,... | collective-permute-start | bytes 196616 | tf_op jit(solution)/shard_map/ppermute | solution.py:24
  11.6 5.4 %collective-permute-start.4 = (bf16[2,128,128]{2,1,0:T(8,128)(2,1)S(1)}, bf16[2,128,128]{2,1,0:T(8,128)(2,1)S(1)}, u32[]{:S(2)}, u32[]{:S(2)}) collective-permute-start(bf16[2,128,128]{2,1,0:T(8,128)(2,1)S(1)} %shard_map.74.refs_0_), channel_id=1, source_target_pairs={{4,0},{5,1},{6,2},{7,3},{0,4},{1,5},{2,6},{3,7},{12,8},{13,9},{14,... | collective-permute-start | bytes 196616 | tf_op jit(solution)/shard_map/ppermute | solution.py:24
  11.6 5.4 %collective-permute-start.3 = (bf16[2,128,128]{2,1,0:T(8,128)(2,1)S(1)}, bf16[2,128,128]{2,1,0:T(8,128)(2,1)S(1)}, u32[]{:S(2)}, u32[]{:S(2)}) collective-permute-start(bf16[2,128,128]{2,1,0:T(8,128)(2,1)S(1)} %shard_map.74.refs_0_), channel_id=1, source_target_pairs={{2,0},{3,1},{0,2},{1,3},{6,4},{7,5},{4,6},{5,7},{10,8},{11,9},{8,1... | collective-permute-start | bytes 196616 | tf_op jit(solution)/shard_map/ppermute | solution.py:24
  18.3 8.9 %collective-permute-start.8 = (bf16[128,1664]{1,0:T(8,128)(2,1)S(1)}, bf16[128,1664]{1,0:T(8,128)(2,1)S(1)}, u32[]{:S(2)}, u32[]{:S(2)}) collective-permute-start(bf16[128,1664]{1,0:T(8,128)(2,1)S(1)} %get-tuple-element.16), channel_id=1, source_target_pairs={{8,0},{16,8},{24,16},{0,24},{9,1},{17,9},{25,17},{1,25},{10,2},{18... | collective-permute-start | bytes 1277960 | tf_op jit(solution)/shard_map/ppermute | solution.py:20
  20.2 5.7 %collective-permute-start.11 = (f32[2,128]{1,0:T(2,128)S(1)}, f32[2,128]{1,0:T(2,128)S(1)}, u32[]{:S(2)}, u32[]{:S(2)}) collective-permute-start(f32[2,128]{1,0:T(2,128)S(1)} %get-tuple-element.18), channel_id=1, source_target_pairs={{14,0},{15,1},{12,2},{13,3},{10,4},{11,5},{8,6},{9,7},{22,8},{23,9... | collective-permute-start | bytes 3080 | tf_op jit(solution)/shard_map/ppermute | solution.py:247
  22.0 4.8 %collective-permute-start.10 = (f32[2,128]{1,0:T(2,128)S(1)}, f32[2,128]{1,0:T(2,128)S(1)}, u32[]{:S(2)}, u32[]{:S(2)}) collective-permute-start(f32[2,128]{1,0:T(2,128)S(1)} %get-tuple-element.18), channel_id=1, source_target_pairs={{12,0},{13,1},{14,2},{15,3},{8,4},{9,5},{10,6},{11,7},{20,8},{21,9... | collective-permute-start | bytes 3080 | tf_op jit(solution)/shard_map/ppermute | solution.py:247
  22.8 4.1 %collective-permute-start.9 = (f32[2,128]{1,0:T(2,128)S(1)}, f32[2,128]{1,0:T(2,128)S(1)}, u32[]{:S(2)}, u32[]{:S(2)}) collective-permute-start(f32[2,128]{1,0:T(2,128)S(1)} %get-tuple-element.18), channel_id=1, source_target_pairs={{10,0},{11,1},{8,2},{9,3},{14,4},{15,5},{12,6},{13,7},{18,8},{19,9... | collective-permute-start | bytes 3080 | tf_op jit(solution)/shard_map/ppermute | solution.py:247
where the time goes:
time: 28.4 us; the launch traced here: 28.3 us
  starting transfers between devices  16.7 us (59%)
  waiting for transfers between devices  7.3 us (26%)
  Pallas kernels  4.16 us (15%)
    ppermute x5, starting transfers between devices, handed_over(): return lax.ppermute(block, ('section', 'tp'), route)  8.04 us
    ppermute x5, starting transfers between devices, swapped(): lax.ppermute(block, axis, [(i ^ mask, i) for i in range(lax.axis_size(axi...  5.55 us
    ppermute x5, waiting for transfers between devices, swapped(): lax.ppermute(block, axis, [(i ^ mask, i) for i in range(lax.axis_size(axi...  5.06 us
    ppermute x2, starting transfers between devices, passed_along(): return lax.ppermute(block, axis, route)  3.15 us
    ppermute x5, waiting for transfers between devices, handed_over(): return lax.ppermute(block, ('section', 'tp'), route)  1.95 us
    pallas_call x1, Pallas kernels, project(): pl.pallas_call(functools.partial(project_kernel, head_of, counts), out_sh...  1.28 us
    pallas_call x1, Pallas kernels, finish(): pl.pallas_call(finish_kernel, out_shape=pltpu.HBM(inputs.shape, jnp.bfloa...  1.06 us
    pallas_call x1, Pallas kernels, pack(): pl.pallas_call(pack_kernel, out_shape=(pltpu.VMEM((2, *own.shape), own.dt...  0.98 us
  transfers between devices with their start and end apart: 12, of which 6 were waited for; matrix products, arithmetic and copies ran while one was open for 0% of the time, Pallas kernels for 3%

commit v1 on v0

--- a/solution.py
+++ b/solution.py
@@ -97,7 +97,8 @@
     )(*map(in_hbm, (own, grad, spare, evicted)))
 
 
-def reach_kernel(weight_ref, input_ref, gain_ref, reach_ref):
+def reach_kernel(weight_ref, input_ref, gain_ref, first_ref, reach_ref):
+    del first_ref
     tokens, features = input_ref.shape
     values = input_ref[...].astype(jnp.float32)
     reach_ref[tokens:, :] = jnp.zeros_like(reach_ref[tokens:, :])
@@ -108,15 +109,15 @@
     reach_ref[:tokens, :] = reach.astype(reach_ref.dtype)
 
 
-def reach_of(weights, inputs, gain):
+def reach_of(weights, inputs, gain, first):
     return pl.pallas_call(
         reach_kernel,
         out_shape=pltpu.VMEM((inputs.shape[0] + EXTRA, weights.shape[1]), jnp.bfloat16),
-        in_specs=vmem_specs(3),
+        in_specs=vmem_specs(4),
         out_specs=pl.BlockSpec(memory_space=pltpu.VMEM),
         cost_estimate=HIDES,
         compiler_params=pltpu.CompilerParams(vmem_limit_bytes=8 << 20),
-    )(*map(in_vmem, (weights, inputs, gain)))
+    )(*map(in_vmem, (weights, inputs, gain, first)))
 
 
 def mix_kernel(taken_ref, *refs):
@@ -268,7 +269,7 @@
         heads.append((swapped(packed, "tp", mask) if mask else packed, spare))
     weights, inputs = w_value[0], layer_input[0]
     next_input = passed_along(inputs, "section", -1)
-    reach = reach_of(weights, inputs, gain)
+    reach = reach_of(weights, inputs, gain, heads[-1][0])
     if count == 8:
         reaches = [reach, swapped(reach, "tp", SIDE)]
         reaches[1], next_input = lax.optimization_barrier((reaches[1], next_input))

time: 28.4 us -> 28.4 us (level); the launches traced: 28.3 us -> 28 us
    ppermute x5, starting transfers between devices: 8.04 us -> 5.95 us  [handed_over(): return lax.ppermute(block, ('section', 'tp'), route)]
    ppermute x5, starting transfers between devices: 5.55 us -> 7.61 us  [swapped(): lax.ppermute(block, axis, [(i ^ mask, i) for i in range(lax.axis_size(axi...]
where the time goes in v1:
time: 28.4 us; the launch traced here: 28 us
  starting transfers between devices  16.7 us (59%)
  waiting for transfers between devices  7.04 us (25%)
  Pallas kernels  4.15 us (15%)
    ppermute x5, starting transfers between devices, swapped(): lax.ppermute(block, axis, [(i ^ mask, i) for i in range(lax.axis_size(axi...  7.61 us
    ppermute x5, starting transfers between devices, handed_over(): return lax.ppermute(block, ('section', 'tp'), route)  5.95 us
    ppermute x5, waiting for transfers between devices, swapped(): lax.ppermute(block, axis, [(i ^ mask, i) for i in range(lax.axis_size(axi...  4.8 us
    ppermute x2, starting transfers between devices, passed_along(): return lax.ppermute(block, axis, route)  3.15 us
    ppermute x5, waiting for transfers between devices, handed_over(): return lax.ppermute(block, ('section', 'tp'), route)  2.17 us
    pallas_call x1, Pallas kernels, project(): pl.pallas_call(functools.partial(project_kernel, head_of, counts), out_sh...  1.27 us
    pallas_call x1, Pallas kernels, finish(): pl.pallas_call(finish_kernel, out_shape=pltpu.HBM(inputs.shape, jnp.bfloa...  1.06 us
    pallas_call x1, Pallas kernels, pack(): pl.pallas_call(pack_kernel, out_shape=(pltpu.VMEM((2, *own.shape), own.dt...  0.98 us
  transfers between devices with their start and end apart: 12, of which 6 were waited for; matrix products, arithmetic and copies ran while one was open for 0% of the time, Pallas kernels for 3%

profile of v1, /device:TPU:1, one launch (start us, length us, event | category | flops | bytes accessed | tf_op | source)
XLA Modules:
  0.0 28.0 jit_solution(2637418589726393945)
XLA Ops:
  0.0 0.0 copy-start.1
  0.0 0.0 copy-start
  0.0 0.0 copy-start.2
  0.0 1.0 %shard_map.73 = (bf16[2,128,128]{2,1,0:T(8,128)(2,1)S(1)}, bf16[128,128]{1,0:T(8,128)(2,1)S(1)}, bf16[128,128]{1,0:T(8,128)(2,1)S(1)}) custom-call(bf16[128,128]{1,0:T(8,128)(2,1)} %bitcast.11, bf16[128,128]{1,0:T(8,128)(2,1)} %bitcast.12, bf16[128,128]{1,0:T(8,128)(2,1)} %bitcast.13, s32[1,4]{1,0:T(1,128)} %evicted_ref.1), custom_call_target="tpu_custom_call" | custom-call | flops 34359738368 | bytes 33554432 | tf_op jit(solution)/shard_map/pallas_call | solution.py:82
  1.0 2.1 %collective-permute-start.2 = (bf16[2,128,128]{2,1,0:T(8,128)(2,1)S(1)}, bf16[2,128,128]{2,1,0:T(8,128)(2,1)S(1)}, u32[]{:S(2)}, u32[]{:S(2)}) collective-permute-start(bf16[2,128,128]{2,1,0:T(8,128)(2,1)S(1)} %get-tuple-element.14.refs_3_), channel_id=1, source_target_pairs={{1,0},{0,1},{3,2},{2,3},{5,4},{4,5},{7,6},{6,7},{9,8},{8,9},{11,10... | collective-permute-start | bytes 196616 | tf_op jit(solution)/shard_map/ppermute | solution.py:24
  3.1 1.2 %collective-permute-start.1 = (bf16[128,128]{1,0:T(8,128)(2,1)S(1)}, bf16[128,128]{1,0:T(8,128)(2,1)S(1)}, u32[]{:S(2)}, u32[]{:S(2)}) collective-permute-start(bf16[128,128]{1,0:T(8,128)(2,1)S(1)} %get-tuple-element.13), channel_id=1, source_target_pairs={{17,0},{16,1},{19,2},{18,3},{21,4},{20,5},{23,6},{22,7},{25,8},{24... | collective-permute-start | bytes 98312 | tf_op jit(solution)/shard_map/ppermute | solution.py:248
  4.3 0.1 collective-permute-start
  4.4 0.0 copy-done.1
  4.4 1.2 %collective-permute-start.7 = (bf16[128,1536]{1,0:T(8,128)(2,1)S(1)}, bf16[128,1536]{1,0:T(8,128)(2,1)S(1)}, u32[]{:S(2)}, u32[]{:S(2)}) collective-permute-start(bf16[128,1536]{1,0:T(8,128)(2,1)S(1)} %bitcast.8), channel_id=1, source_target_pairs={{8,0},{16,8},{24,16},{0,24},{9,1},{17,9},{25,17},{1,25},{10,2},{18... | collective-permute-start | bytes 1179656 | tf_op jit(solution)/shard_map/ppermute | solution.py:20
  5.6 0.0 collective-permute-done.2.refs_2_.first_ref
  5.6 0.0 copy-done
  5.6 0.0 copy-done.2
  5.6 0.6 %shard_map.75.refs_7_ = bf16[144,1024]{1,0:T(8,128)(2,1)S(1)} custom-call(bf16[1536,1024]{1,0:T(8,128)(2,1)S(1)} %bitcast.6, bf16[128,1536]{1,0:T(8,128)(2,1)S(1)} %bitcast.9, f32[1,1536]{1,0:T(1,128)S(1)} %copy-done.2, bf16[2,128,128]{2,1,0:T(8,128)(2,1)S(1)} %collective-permute-done.2.refs_2_.first_ref), custom_call_target="tpu_custom_call" | custom-call | flops 34359738368 | bytes 33554432 | tf_op jit(solution)/shard_map/pallas_call | solution.py:113
  6.3 1.7 %collective-permute-start.6 = (bf16[144,1024]{1,0:T(8,128)(2,1)S(1)}, bf16[144,1024]{1,0:T(8,128)(2,1)S(1)}, u32[]{:S(2)}, u32[]{:S(2)}) collective-permute-start(bf16[144,1024]{1,0:T(8,128)(2,1)S(1)} %shard_map.75.refs_7_), channel_id=1, source_target_pairs={{1,0},{0,1},{3,2},{2,3},{5,4},{4,5},{7,6},{6,7},{9,8},{8,9},{11,10... | collective-permute-start | bytes 884744 | tf_op jit(solution)/shard_map/ppermute | solution.py:24
  8.0 0.0 collective-permute-done.1.refs_1_
  8.0 0.0 collective-permute-done.refs_0_
  8.0 0.2 shard_map.74.refs_0_
  8.2 3.4 %collective-permute-start.5 = (bf16[2,128,128]{2,1,0:T(8,128)(2,1)S(1)}, bf16[2,128,128]{2,1,0:T(8,128)(2,1)S(1)}, u32[]{:S(2)}, u32[]{:S(2)}) collective-permute-start(bf16[2,128,128]{2,1,0:T(8,128)(2,1)S(1)} %shard_map.74.refs_0_), channel_id=1, source_target_pairs={{6,0},{7,1},{4,2},{5,3},{2,4},{3,5},{0,6},{1,7},{14,8},{15,9},{12,... | collective-permute-start | bytes 196616 | tf_op jit(solution)/shard_map/ppermute | solution.py:24
  11.6 0.0 collective-permute-start.4
  11.6 0.4 %collective-permute-start.3 = (bf16[2,128,128]{2,1,0:T(8,128)(2,1)S(1)}, bf16[2,128,128]{2,1,0:T(8,128)(2,1)S(1)}, u32[]{:S(2)}, u32[]{:S(2)}) collective-permute-start(bf16[2,128,128]{2,1,0:T(8,128)(2,1)S(1)} %shard_map.74.refs_0_), channel_id=1, source_target_pairs={{2,0},{3,1},{0,2},{1,3},{6,4},{7,5},{4,6},{5,7},{10,8},{11,9},{8,1... | collective-permute-start | bytes 196616 | tf_op jit(solution)/shard_map/ppermute | solution.py:24
  12.0 2.5 %collective-permute-done.6.refs_8_ = bf16[144,1024]{1,0:T(8,128)(2,1)S(1)} collective-permute-done((bf16[144,1024]{1,0:T(8,128)(2,1)S(1)}, bf16[144,1024]{1,0:T(8,128)(2,1)S(1)}, u32[]{:S(2)}, u32[]{:S(2)}) %collective-permute-start.6) | collective-permute-done | bytes 294944 | tf_op jit(solution)/shard_map/ppermute | solution.py:24
  14.4 0.0 collective-permute-done.7.input_ref
  14.4 0.0 collective-permute-done.5.refs_3_
  14.4 2.3 %collective-permute-done.4.refs_2_ = bf16[2,128,128]{2,1,0:T(8,128)(2,1)S(1)} collective-permute-done((bf16[2,128,128]{2,1,0:T(8,128)(2,1)S(1)}, bf16[2,128,128]{2,1,0:T(8,128)(2,1)S(1)}, u32[]{:S(2)}, u32[]{:S(2)}) %collective-permute-start.4) | collective-permute-done | bytes 65568 | tf_op jit(solution)/shard_map/ppermute | solution.py:24
  16.8 0.0 collective-permute-done.3.refs_1_
  16.8 1.3 %shard_map.76 = (bf16[128,1664]{1,0:T(8,128)(2,1)S(1)}, f32[2,128]{1,0:T(2,128)S(1)}) custom-call(bf16[2,128,128]{2,1,0:T(8,128)(2,1)S(1)} %shard_map.74.refs_0_, bf16[2,128,128]{2,1,0:T(8,128)(2,1)S(1)} %collective-permute-done.3.refs_1_, bf16[2,128,128]{2,1,0:T(8,128)(2,1)S(1)} %collective-permute-done.4.refs_2_, ...), custom_call_target="tpu_custom_call" | custom-call | flops 34359738368 | bytes 33554432 | tf_op jit(solution)/shard_map/pallas_call | solution.py:184
  18.1 1.9 %collective-permute-start.8 = (bf16[128,1664]{1,0:T(8,128)(2,1)S(1)}, bf16[128,1664]{1,0:T(8,128)(2,1)S(1)}, u32[]{:S(2)}, u32[]{:S(2)}) collective-permute-start(bf16[128,1664]{1,0:T(8,128)(2,1)S(1)} %get-tuple-element.16), channel_id=1, source_target_pairs={{8,0},{16,8},{24,16},{0,24},{9,1},{17,9},{25,17},{1,25},{10,2},{18... | collective-permute-start | bytes 1277960 | tf_op jit(solution)/shard_map/ppermute | solution.py:20
  20.0 2.0 %collective-permute-start.11 = (f32[2,128]{1,0:T(2,128)S(1)}, f32[2,128]{1,0:T(2,128)S(1)}, u32[]{:S(2)}, u32[]{:S(2)}) collective-permute-start(f32[2,128]{1,0:T(2,128)S(1)} %get-tuple-element.18), channel_id=1, source_target_pairs={{14,0},{15,1},{12,2},{13,3},{10,4},{11,5},{8,6},{9,7},{22,8},{23,9... | collective-permute-start | bytes 3080 | tf_op jit(solution)/shard_map/ppermute | solution.py:248
  22.0 0.7 %collective-permute-start.10 = (f32[2,128]{1,0:T(2,128)S(1)}, f32[2,128]{1,0:T(2,128)S(1)}, u32[]{:S(2)}, u32[]{:S(2)}) collective-permute-start(f32[2,128]{1,0:T(2,128)S(1)} %get-tuple-element.18), channel_id=1, source_target_pairs={{12,0},{13,1},{14,2},{15,3},{8,4},{9,5},{10,6},{11,7},{20,8},{21,9... | collective-permute-start | bytes 3080 | tf_op jit(solution)/shard_map/ppermute | solution.py:248
  22.7 2.0 %collective-permute-start.9 = (f32[2,128]{1,0:T(2,128)S(1)}, f32[2,128]{1,0:T(2,128)S(1)}, u32[]{:S(2)}, u32[]{:S(2)}) collective-permute-start(f32[2,128]{1,0:T(2,128)S(1)} %get-tuple-element.18), channel_id=1, source_target_pairs={{10,0},{11,1},{8,2},{9,3},{14,4},{15,5},{12,6},{13,7},{18,8},{19,9... | collective-permute-start | bytes 3080 | tf_op jit(solution)/shard_map/ppermute | solution.py:248
  24.7 1.0 %collective-permute-done.11.refs_2_ = f32[2,128]{1,0:T(2,128)S(1)} collective-permute-done((f32[2,128]{1,0:T(2,128)S(1)}, f32[2,128]{1,0:T(2,128)S(1)}, u32[]{:S(2)}, u32[]{:S(2)}) %collective-permute-start.11) | collective-permute-done | bytes 1056 | tf_op jit(solution)/shard_map/ppermute | solution.py:248
  25.7 1.1 %collective-permute-done.10.refs_1_ = f32[2,128]{1,0:T(2,128)S(1)} collective-permute-done((f32[2,128]{1,0:T(2,128)S(1)}, f32[2,128]{1,0:T(2,128)S(1)}, u32[]{:S(2)}, u32[]{:S(2)}) %collective-permute-start.10) | collective-permute-done | bytes 1056 | tf_op jit(solution)/shard_map/ppermute | solution.py:248
  26.8 0.1 collective-permute-done.9.refs_0_
  26.8 0.1 collective-permute-done.8.scaled_ref
  26.9 1.1 %shard_map.77 = bf16[128,1536]{1,0:T(8,128)(2,1)} custom-call(bf16[128,1664]{1,0:T(8,128)(2,1)S(1)} %collective-permute-done.8.scaled_ref, bf16[128,1536]{1,0:T(8,128)(2,1)S(1)} %collective-permute-done.7.input_ref, f32[2,128]{1,0:T(2,128)S(1)} %collective-permute-done.9.refs_0_, f32[2,128]{1,0:T(2,128)S(1)} %collective-permute-done.10.refs_1_, ...), custom_call_target="tpu_custom_call" | custom-call | tf_op jit(solution)/shard_map/pallas_call | solution.py:225
Async XLA Ops:
  0.0 4.4 %copy-start.1 = (bf16[1,128,1536]{2,1,0:T(8,128)(2,1)S(1)}, bf16[1,128,1536]{2,1,0:T(8,128)(2,1)}, u32[]{:S(2)}) copy-start(bf16[1,128,1536]{2,1,0:T(8,128)(2,1)} %param.12) | copy-start | bytes 1179652
  0.0 5.6 %copy-start = (bf16[1,1536,1024]{2,1,0:T(8,128)(2,1)S(1)}, bf16[1,1536,1024]{2,1,0:T(8,128)(2,1)}, u32[]{:S(2)}) copy-start(bf16[1,1536,1024]{2,1,0:T(8,128)(2,1)} %param.8) | copy-start | bytes 9437188
  0.0 5.6 %copy-start.2 = (f32[1,1536]{1,0:T(1,128)S(1)}, f32[1,1536]{1,0:T(1,128)}, u32[]{:S(2)}) copy-start(f32[1,1536]{1,0:T(1,128)} %refs_6_.1) | copy-start | bytes 18436
  1.0 4.6 %collective-permute-start.2 = (bf16[2,128,128]{2,1,0:T(8,128)(2,1)S(1)}, bf16[2,128,128]{2,1,0:T(8,128)(2,1)S(1)}, u32[]{:S(2)}, u32[]{:S(2)}) collective-permute-start(bf16[2,128,128]{2,1,0:T(8,128)(2,1)S(1)} %get-tuple-element.14.refs_3_), channel_id=1, source_target_pairs={{1,0},{0,1},{3,2},{2,3},{5,4},{4,5},{7,6},{6,7},{9,8},{8,9},{11,10... | collective-permute-start | bytes 196616 | tf_op jit(solution)/shard_map/ppermute | solution.py:24
  3.1 4.9 %collective-permute-start.1 = (bf16[128,128]{1,0:T(8,128)(2,1)S(1)}, bf16[128,128]{1,0:T(8,128)(2,1)S(1)}, u32[]{:S(2)}, u32[]{:S(2)}) collective-permute-start(bf16[128,128]{1,0:T(8,128)(2,1)S(1)} %get-tuple-element.13), channel_id=1, source_target_pairs={{17,0},{16,1},{19,2},{18,3},{21,4},{20,5},{23,6},{22,7},{25,8},{24... | collective-permute-start | bytes 98312 | tf_op jit(solution)/shard_map/ppermute | solution.py:248
  4.3 3.7 %collective-permute-start = (bf16[128,128]{1,0:T(8,128)(2,1)S(1)}, bf16[128,128]{1,0:T(8,128)(2,1)S(1)}, u32[]{:S(2)}, u32[]{:S(2)}) collective-permute-start(bf16[128,128]{1,0:T(8,128)(2,1)S(1)} %get-tuple-element.13), channel_id=1, source_target_pairs={{16,0},{17,1},{18,2},{19,3},{20,4},{21,5},{22,6},{23,7},{24,8},{25... | collective-permute-start | bytes 98312 | tf_op jit(solution)/shard_map/ppermute | solution.py:248
  4.4 10.0 %collective-permute-start.7 = (bf16[128,1536]{1,0:T(8,128)(2,1)S(1)}, bf16[128,1536]{1,0:T(8,128)(2,1)S(1)}, u32[]{:S(2)}, u32[]{:S(2)}) collective-permute-start(bf16[128,1536]{1,0:T(8,128)(2,1)S(1)} %bitcast.8), channel_id=1, source_target_pairs={{8,0},{16,8},{24,16},{0,24},{9,1},{17,9},{25,17},{1,25},{10,2},{18... | collective-permute-start | bytes 1179656 | tf_op jit(solution)/shard_map/ppermute | solution.py:20
  6.3 8.1 %collective-permute-start.6 = (bf16[144,1024]{1,0:T(8,128)(2,1)S(1)}, bf16[144,1024]{1,0:T(8,128)(2,1)S(1)}, u32[]{:S(2)}, u32[]{:S(2)}) collective-permute-start(bf16[144,1024]{1,0:T(8,128)(2,1)S(1)} %shard_map.75.refs_7_), channel_id=1, source_target_pairs={{1,0},{0,1},{3,2},{2,3},{5,4},{4,5},{7,6},{6,7},{9,8},{8,9},{11,10... | collective-permute-start | bytes 884744 | tf_op jit(solution)/shard_map/ppermute | solution.py:24
  8.2 6.2 %collective-permute-start.5 = (bf16[2,128,128]{2,1,0:T(8,128)(2,1)S(1)}, bf16[2,128,128]{2,1,0:T(8,128)(2,1)S(1)}, u32[]{:S(2)}, u32[]{:S(2)}) collective-permute-start(bf16[2,128,128]{2,1,0:T(8,128)(2,1)S(1)} %shard_map.74.refs_0_), channel_id=1, source_target_pairs={{6,0},{7,1},{4,2},{5,3},{2,4},{3,5},{0,6},{1,7},{14,8},{15,9},{12,... | collective-permute-start | bytes 196616 | tf_op jit(solution)/shard_map/ppermute | solution.py:24
  11.6 5.2 %collective-permute-start.4 = (bf16[2,128,128]{2,1,0:T(8,128)(2,1)S(1)}, bf16[2,128,128]{2,1,0:T(8,128)(2,1)S(1)}, u32[]{:S(2)}, u32[]{:S(2)}) collective-permute-start(bf16[2,128,128]{2,1,0:T(8,128)(2,1)S(1)} %shard_map.74.refs_0_), channel_id=1, source_target_pairs={{4,0},{5,1},{6,2},{7,3},{0,4},{1,5},{2,6},{3,7},{12,8},{13,9},{14,... | collective-permute-start | bytes 196616 | tf_op jit(solution)/shard_map/ppermute | solution.py:24
  11.6 5.2 %collective-permute-start.3 = (bf16[2,128,128]{2,1,0:T(8,128)(2,1)S(1)}, bf16[2,128,128]{2,1,0:T(8,128)(2,1)S(1)}, u32[]{:S(2)}, u32[]{:S(2)}) collective-permute-start(bf16[2,128,128]{2,1,0:T(8,128)(2,1)S(1)} %shard_map.74.refs_0_), channel_id=1, source_target_pairs={{2,0},{3,1},{0,2},{1,3},{6,4},{7,5},{4,6},{5,7},{10,8},{11,9},{8,1... | collective-permute-start | bytes 196616 | tf_op jit(solution)/shard_map/ppermute | solution.py:24
  18.1 8.8 %collective-permute-start.8 = (bf16[128,1664]{1,0:T(8,128)(2,1)S(1)}, bf16[128,1664]{1,0:T(8,128)(2,1)S(1)}, u32[]{:S(2)}, u32[]{:S(2)}) collective-permute-start(bf16[128,1664]{1,0:T(8,128)(2,1)S(1)} %get-tuple-element.16), channel_id=1, source_target_pairs={{8,0},{16,8},{24,16},{0,24},{9,1},{17,9},{25,17},{1,25},{10,2},{18... | collective-permute-start | bytes 1277960 | tf_op jit(solution)/shard_map/ppermute | solution.py:20
  20.0 5.7 %collective-permute-start.11 = (f32[2,128]{1,0:T(2,128)S(1)}, f32[2,128]{1,0:T(2,128)S(1)}, u32[]{:S(2)}, u32[]{:S(2)}) collective-permute-start(f32[2,128]{1,0:T(2,128)S(1)} %get-tuple-element.18), channel_id=1, source_target_pairs={{14,0},{15,1},{12,2},{13,3},{10,4},{11,5},{8,6},{9,7},{22,8},{23,9... | collective-permute-start | bytes 3080 | tf_op jit(solution)/shard_map/ppermute | solution.py:248
  22.0 4.8 %collective-permute-start.10 = (f32[2,128]{1,0:T(2,128)S(1)}, f32[2,128]{1,0:T(2,128)S(1)}, u32[]{:S(2)}, u32[]{:S(2)}) collective-permute-start(f32[2,128]{1,0:T(2,128)S(1)} %get-tuple-element.18), channel_id=1, source_target_pairs={{12,0},{13,1},{14,2},{15,3},{8,4},{9,5},{10,6},{11,7},{20,8},{21,9... | collective-permute-start | bytes 3080 | tf_op jit(solution)/shard_map/ppermute | solution.py:248
  22.7 4.1 %collective-permute-start.9 = (f32[2,128]{1,0:T(2,128)S(1)}, f32[2,128]{1,0:T(2,128)S(1)}, u32[]{:S(2)}, u32[]{:S(2)}) collective-permute-start(f32[2,128]{1,0:T(2,128)S(1)} %get-tuple-element.18), channel_id=1, source_target_pairs={{10,0},{11,1},{8,2},{9,3},{14,4},{15,5},{12,6},{13,7},{18,8},{19,9... | collective-permute-start | bytes 3080 | tf_op jit(solution)/shard_map/ppermute | solution.py:248

commit v2 on v1

--- a/solution.py
+++ b/solution.py
@@ -144,26 +144,74 @@
     )(*map(in_vmem, (taken, *[spare for _, spare in heads], *[packed for packed, _ in heads[::-1]])))
 
 
-def project_kernel(head_of, counts, *refs):
-    blocks = refs[: len(counts)]
-    rest = refs[len(counts) :]
-    weight_ref, input_ref, gain_ref, *reach_refs, scaled_ref, sums_ref, flat = rest
-    tokens, features = input_ref.shape
-    place = 0
-    for ref, count in zip(blocks, counts):
+def column_tile(features):
+    return 256 if features % 256 == 0 else features
+
+
+def fill(flat, blocks, head_of, first):
+    groups = []
+    for ref in blocks:
+        count = ref.shape[0]
         for j in range(count):
-            start = pl.multiple_of(head_of(place) * LANES, LANES)
+            start = pl.multiple_of(head_of(first + j) * LANES, LANES)
             flat[:, pl.ds(start, LANES)] = ref[j]
-            place += 1
-    tile = 256 if features % 256 == 0 else features
-    for start in range(0, features, tile):
-        part = pl.ds(start, tile)
-        grad_normed = lax.dot_general(
-            flat[...],
-            weight_ref[part, :],
+        width = count * LANES
+        groups.append((pl.multiple_of(head_of(first) // count * width, width), width))
+        first += count
+    return groups
+
+
+def times_weights(flat, groups, weight_ref, part):
+    products = [
+        lax.dot_general(
+            flat[:, pl.ds(start, width)],
+            weight_ref[part, pl.ds(start, width)],
             (((1,), (1,)), ((), ())),
             preferred_element_type=jnp.float32,
         )
+        for start, width in groups
+    ]
+    return sum(products[1:], products[0])
+
+
+def early_kernel(head_of, *refs):
+    *blocks, weight_ref, out_ref, flat = refs
+    groups = fill(flat, blocks, head_of, 0)
+    features = weight_ref.shape[0]
+    tile = column_tile(features)
+    for start in range(0, features, tile):
+        part = pl.ds(start, tile)
+        out_ref[:, part] = times_weights(flat, groups, weight_ref, part)
+
+
+def project_early(head_of, blocks, weights):
+    tokens = blocks[0].shape[1]
+    return pl.pallas_call(
+        functools.partial(early_kernel, head_of),
+        out_shape=pltpu.VMEM((tokens, weights.shape[0]), jnp.float32),
+        in_specs=vmem_specs(len(blocks) + 1),
+        out_specs=pl.BlockSpec(memory_space=pltpu.VMEM),
+        scratch_shapes=[pltpu.VMEM((tokens, weights.shape[1]), jnp.bfloat16)],
+        cost_estimate=pl.CostEstimate(flops=1 << 16, bytes_accessed=1 << 12, transcendentals=0),
+        compiler_params=pltpu.CompilerParams(vmem_limit_bytes=16 << 20),
+    )(*map(in_vmem, (*blocks, weights)))
+
+
+def project_kernel(head_of, sizes, *refs):
+    blocks = refs[: sizes[0]]
+    early_refs = refs[sizes[0] : sizes[0] + sizes[1]]
+    rest = refs[sizes[0] + sizes[1] :]
+    weight_ref, input_ref, gain_ref, *reach_refs, scaled_ref, sums_ref, flat = rest
+    tokens, features = input_ref.shape
+    groups = fill(flat, blocks, head_of, 0)
+    if early_refs:
+        groups = groups[EARLY:]
+    tile = column_tile(features)
+    for start in range(0, features, tile):
+        part = pl.ds(start, tile)
+        grad_normed = times_weights(flat, groups, weight_ref, part)
+        for ref in early_refs:
+            grad_normed = grad_normed + ref[:, part]
         scaled_ref[:, part] = (grad_normed * gain_ref[:, part]).astype(scaled_ref.dtype)
     reach = sum(ref[:tokens, :].astype(jnp.float32) for ref in reach_refs)
     squares = sum(ref[tokens:, :tokens].astype(jnp.float32) for ref in reach_refs)
@@ -178,21 +226,21 @@
     scaled_ref[:, features:] = extra.astype(scaled_ref.dtype)
 
 
-def project(head_of, blocks, weights, inputs, gain, reaches):
-    counts = tuple(block.shape[0] for block in blocks)
+def project(head_of, blocks, early, weights, inputs, gain, reaches):
     tokens, features = inputs.shape
-    return pl.pallas_call(
-        functools.partial(project_kernel, head_of, counts),
+    operands = (*blocks, *early, weights, inputs, gain, *reaches)
+    return pl.pallas_call(
+        functools.partial(project_kernel, head_of, (len(blocks), len(early))),
         out_shape=(
             pltpu.VMEM((tokens, features + LANES), jnp.bfloat16),
             pltpu.VMEM((2, tokens), jnp.float32),
         ),
-        in_specs=vmem_specs(len(blocks) + 3 + len(reaches)),
+        in_specs=vmem_specs(len(operands)),
         out_specs=tuple(vmem_specs(2)),
         scratch_shapes=[pltpu.VMEM((tokens, weights.shape[1]), jnp.bfloat16)],
         cost_estimate=HIDES,
         compiler_params=pltpu.CompilerParams(vmem_limit_bytes=16 << 20),
-    )(*map(in_vmem, (*blocks, weights, inputs, gain, *reaches)))
+    )(*map(in_vmem, operands))
 
 
 def finish_kernel(scaled_ref, input_ref, *refs):
@@ -236,7 +284,8 @@
 
 
 FAR, NEAR, SIDE = 4, 2, 1
-LINE = (NEAR, FAR, FAR | NEAR)
+LINE = (FAR | NEAR, NEAR, FAR)
+EARLY = 2
 
 
 def handed_over(block, sections, count, distance, mask):
@@ -277,10 +326,11 @@
         reaches = [lax.psum(reach, "tp")]
     pair = value_gradients(taken, heads)
     blocks, head_of = gathered(pair, "tp")
-    scaled, sums = project(head_of, blocks, weights, inputs, gain, reaches)
+    early = [project_early(head_of, blocks[:EARLY], weights)] if count == 8 else []
+    scaled, sums = project(head_of, blocks, early, weights, inputs, gain, reaches)
     next_scaled = passed_along(scaled, "section", -1)
     next_sums = []
-    for mask in LINE if count == 8 else ():
+    for mask in (NEAR, FAR, FAR | NEAR) if count == 8 else ():
         next_sums.append(handed_over(sums, sections, count, -1, mask))
     return finish(next_scaled, next_input, next_sums)[None]
 

time: 28.4 us -> 27.9 us (0.982)
  waiting for transfers between devices: 7.04 us -> 6.36 us
    ppermute x5, waiting for transfers between devices: 4.8 us -> 4.12 us  [swapped(): lax.ppermute(block, axis, [(i ^ mask, i) for i in range(lax.axis_size(axi...]
    pallas_call x1 -> x2, Pallas kernels: 1.27 us -> 1.43 us  [the longest x1 0.76 us: project(): pl.pallas_call(functools.partial(project_kernel, head_of, (len(blocks), l...]
  transfers between devices with their start and end apart: 12 -> 12, of which waited for: 6 -> 7; matrix products, arithmetic and copies ran while one was open for 0% -> 0% of each run, Pallas kernels for 3% -> 6%
where the time goes in v2:
time: 27.9 us; the launch traced here: 27.5 us
  starting transfers between devices  16.7 us (60%)
  waiting for transfers between devices  6.36 us (23%)
  Pallas kernels  4.32 us (15%)
    ppermute x5, starting transfers between devices, swapped(): lax.ppermute(block, axis, [(i ^ mask, i) for i in range(lax.axis_size(axi...  7.61 us
    ppermute x5, starting transfers between devices, handed_over(): return lax.ppermute(block, ('section', 'tp'), route)  5.96 us
    ppermute x5, waiting for transfers between devices, swapped(): lax.ppermute(block, axis, [(i ^ mask, i) for i in range(lax.axis_size(axi...  4.12 us
    ppermute x2, starting transfers between devices, passed_along(): return lax.ppermute(block, axis, route)  3.15 us
    ppermute x5, waiting for transfers between devices, handed_over(): return lax.ppermute(block, ('section', 'tp'), route)  2.16 us
    pallas_call x1, Pallas kernels, finish(): pl.pallas_call(finish_kernel, out_shape=pltpu.HBM(inputs.shape, jnp.bfloa...  1.06 us
    pallas_call x1, Pallas kernels, pack(): pl.pallas_call(pack_kernel, out_shape=(pltpu.VMEM((2, *own.shape), own.dt...  0.98 us
    pallas_call x1, Pallas kernels, project(): pl.pallas_call(functools.partial(project_kernel, head_of, (len(blocks), l...  0.76 us
  transfers between devices with their start and end apart: 12, of which 7 were waited for; matrix products, arithmetic and copies ran while one was open for 0% of the time, Pallas kernels for 6%

profile of v2, /device:TPU:1, one launch (start us, length us, event | category | flops | bytes accessed | tf_op | source)
XLA Modules:
  0.0 27.5 jit_solution(14949754711037329255)
XLA Ops:
  0.0 0.0 copy-start.1
  0.0 0.0 copy-start
  0.0 0.0 copy-start.2
  0.0 1.0 %shard_map.73 = (bf16[2,128,128]{2,1,0:T(8,128)(2,1)S(1)}, bf16[128,128]{1,0:T(8,128)(2,1)S(1)}, bf16[128,128]{1,0:T(8,128)(2,1)S(1)}) custom-call(bf16[128,128]{1,0:T(8,128)(2,1)} %bitcast.12, bf16[128,128]{1,0:T(8,128)(2,1)} %bitcast.13, bf16[128,128]{1,0:T(8,128)(2,1)} %bitcast.14, s32[1,4]{1,0:T(1,128)} %evicted_ref.1), custom_call_target="tpu_custom_call" | custom-call | flops 34359738368 | bytes 33554432 | tf_op jit(solution)/shard_map/pallas_call | solution.py:82
  1.0 2.1 %collective-permute-start.2 = (bf16[2,128,128]{2,1,0:T(8,128)(2,1)S(1)}, bf16[2,128,128]{2,1,0:T(8,128)(2,1)S(1)}, u32[]{:S(2)}, u32[]{:S(2)}) collective-permute-start(bf16[2,128,128]{2,1,0:T(8,128)(2,1)S(1)} %get-tuple-element.14.refs_3_), channel_id=1, source_target_pairs={{1,0},{0,1},{3,2},{2,3},{5,4},{4,5},{7,6},{6,7},{9,8},{8,9},{11,10... | collective-permute-start | bytes 196616 | tf_op jit(solution)/shard_map/ppermute | solution.py:24
  3.1 1.2 %collective-permute-start.1 = (bf16[128,128]{1,0:T(8,128)(2,1)S(1)}, bf16[128,128]{1,0:T(8,128)(2,1)S(1)}, u32[]{:S(2)}, u32[]{:S(2)}) collective-permute-start(bf16[128,128]{1,0:T(8,128)(2,1)S(1)} %get-tuple-element.13), channel_id=1, source_target_pairs={{17,0},{16,1},{19,2},{18,3},{21,4},{20,5},{23,6},{22,7},{25,8},{24... | collective-permute-start | bytes 98312 | tf_op jit(solution)/shard_map/ppermute | solution.py:297
  4.3 0.1 collective-permute-start
  4.4 0.0 copy-done.1
  4.4 1.2 %collective-permute-start.7 = (bf16[128,1536]{1,0:T(8,128)(2,1)S(1)}, bf16[128,1536]{1,0:T(8,128)(2,1)S(1)}, u32[]{:S(2)}, u32[]{:S(2)}) collective-permute-start(bf16[128,1536]{1,0:T(8,128)(2,1)S(1)} %bitcast.9), channel_id=1, source_target_pairs={{8,0},{16,8},{24,16},{0,24},{9,1},{17,9},{25,17},{1,25},{10,2},{18... | collective-permute-start | bytes 1179656 | tf_op jit(solution)/shard_map/ppermute | solution.py:20
  5.6 0.0 collective-permute-done.2.refs_2_.first_ref
  5.6 0.0 copy-done
  5.6 0.0 copy-done.2
  5.6 0.6 %shard_map.76.refs_8_ = bf16[144,1024]{1,0:T(8,128)(2,1)S(1)} custom-call(bf16[1536,1024]{1,0:T(8,128)(2,1)S(1)} %bitcast.6, bf16[128,1536]{1,0:T(8,128)(2,1)S(1)} %bitcast.10, f32[1,1536]{1,0:T(1,128)S(1)} %copy-done.2, bf16[2,128,128]{2,1,0:T(8,128)(2,1)S(1)} %collective-permute-done.2.refs_2_.first_ref), custom_call_target="tpu_custom_call" | custom-call | flops 34359738368 | bytes 33554432 | tf_op jit(solution)/shard_map/pallas_call | solution.py:113
  6.3 1.7 %collective-permute-start.6 = (bf16[144,1024]{1,0:T(8,128)(2,1)S(1)}, bf16[144,1024]{1,0:T(8,128)(2,1)S(1)}, u32[]{:S(2)}, u32[]{:S(2)}) collective-permute-start(bf16[144,1024]{1,0:T(8,128)(2,1)S(1)} %shard_map.76.refs_8_), channel_id=1, source_target_pairs={{1,0},{0,1},{3,2},{2,3},{5,4},{4,5},{7,6},{6,7},{9,8},{8,9},{11,10... | collective-permute-start | bytes 884744 | tf_op jit(solution)/shard_map/ppermute | solution.py:24
  8.0 0.0 collective-permute-done.1.refs_1_
  8.0 0.0 collective-permute-done.refs_0_
  8.0 0.2 shard_map.74.refs_0_
  8.2 3.4 %collective-permute-start.3 = (bf16[2,128,128]{2,1,0:T(8,128)(2,1)S(1)}, bf16[2,128,128]{2,1,0:T(8,128)(2,1)S(1)}, u32[]{:S(2)}, u32[]{:S(2)}) collective-permute-start(bf16[2,128,128]{2,1,0:T(8,128)(2,1)S(1)} %shard_map.74.refs_0_), channel_id=1, source_target_pairs={{6,0},{7,1},{4,2},{5,3},{2,4},{3,5},{0,6},{1,7},{14,8},{15,9},{12,... | collective-permute-start | bytes 196616 | tf_op jit(solution)/shard_map/ppermute | solution.py:24
  11.6 0.0 collective-permute-start.5
  11.6 0.4 %collective-permute-start.4 = (bf16[2,128,128]{2,1,0:T(8,128)(2,1)S(1)}, bf16[2,128,128]{2,1,0:T(8,128)(2,1)S(1)}, u32[]{:S(2)}, u32[]{:S(2)}) collective-permute-start(bf16[2,128,128]{2,1,0:T(8,128)(2,1)S(1)} %shard_map.74.refs_0_), channel_id=1, source_target_pairs={{2,0},{3,1},{0,2},{1,3},{6,4},{7,5},{4,6},{5,7},{10,8},{11,9},{8,1... | collective-permute-start | bytes 196616 | tf_op jit(solution)/shard_map/ppermute | solution.py:24
  12.0 1.3 %collective-permute-done.3.refs_1_ = bf16[2,128,128]{2,1,0:T(8,128)(2,1)S(1)} collective-permute-done((bf16[2,128,128]{2,1,0:T(8,128)(2,1)S(1)}, bf16[2,128,128]{2,1,0:T(8,128)(2,1)S(1)}, u32[]{:S(2)}, u32[]{:S(2)}) %collective-permute-start.3) | collective-permute-done | bytes 65568 | tf_op jit(solution)/shard_map/ppermute | solution.py:24
  13.3 0.7 %shard_map.75.refs_4_ = f32[128,1536]{1,0:T(8,128)S(1)} custom-call(bf16[2,128,128]{2,1,0:T(8,128)(2,1)S(1)} %shard_map.74.refs_0_, bf16[2,128,128]{2,1,0:T(8,128)(2,1)S(1)} %collective-permute-done.3.refs_1_, bf16[1536,1024]{1,0:T(8,128)(2,1)S(1)} %bitcast.7), custom_call_target="tpu_custom_call" | custom-call | flops 65536 | bytes 4096 | tf_op jit(solution)/shard_map/pallas_call | solution.py:189
  14.0 0.5 %collective-permute-done.6.refs_9_ = bf16[144,1024]{1,0:T(8,128)(2,1)S(1)} collective-permute-done((bf16[144,1024]{1,0:T(8,128)(2,1)S(1)}, bf16[144,1024]{1,0:T(8,128)(2,1)S(1)}, u32[]{:S(2)}, u32[]{:S(2)}) %collective-permute-start.6) | collective-permute-done | bytes 294944 | tf_op jit(solution)/shard_map/ppermute | solution.py:24
  14.4 0.0 collective-permute-done.7.input_ref
  14.4 2.3 %collective-permute-done.5.refs_3_ = bf16[2,128,128]{2,1,0:T(8,128)(2,1)S(1)} collective-permute-done((bf16[2,128,128]{2,1,0:T(8,128)(2,1)S(1)}, bf16[2,128,128]{2,1,0:T(8,128)(2,1)S(1)}, u32[]{:S(2)}, u32[]{:S(2)}) %collective-permute-start.5) | collective-permute-done | bytes 65568 | tf_op jit(solution)/shard_map/ppermute | solution.py:24
  16.8 0.0 collective-permute-done.4.refs_2_
  16.8 0.8 %shard_map.77 = (bf16[128,1664]{1,0:T(8,128)(2,1)S(1)}, f32[2,128]{1,0:T(2,128)S(1)}) custom-call(bf16[2,128,128]{2,1,0:T(8,128)(2,1)S(1)} %shard_map.74.refs_0_, bf16[2,128,128]{2,1,0:T(8,128)(2,1)S(1)} %collective-permute-done.3.refs_1_, bf16[2,128,128]{2,1,0:T(8,128)(2,1)S(1)} %collective-permute-done.4.refs_2_, ...), custom_call_target="tpu_custom_call" | custom-call | flops 34359738368 | bytes 33554432 | tf_op jit(solution)/shard_map/pallas_call | solution.py:232
  17.5 1.9 %collective-permute-start.8 = (bf16[128,1664]{1,0:T(8,128)(2,1)S(1)}, bf16[128,1664]{1,0:T(8,128)(2,1)S(1)}, u32[]{:S(2)}, u32[]{:S(2)}) collective-permute-start(bf16[128,1664]{1,0:T(8,128)(2,1)S(1)} %get-tuple-element.16), channel_id=1, source_target_pairs={{8,0},{16,8},{24,16},{0,24},{9,1},{17,9},{25,17},{1,25},{10,2},{18... | collective-permute-start | bytes 1277960 | tf_op jit(solution)/shard_map/ppermute | solution.py:20
  19.5 2.0 %collective-permute-start.11 = (f32[2,128]{1,0:T(2,128)S(1)}, f32[2,128]{1,0:T(2,128)S(1)}, u32[]{:S(2)}, u32[]{:S(2)}) collective-permute-start(f32[2,128]{1,0:T(2,128)S(1)} %get-tuple-element.18), channel_id=1, source_target_pairs={{14,0},{15,1},{12,2},{13,3},{10,4},{11,5},{8,6},{9,7},{22,8},{23,9... | collective-permute-start | bytes 3080 | tf_op jit(solution)/shard_map/ppermute | solution.py:297
  21.5 0.7 %collective-permute-start.10 = (f32[2,128]{1,0:T(2,128)S(1)}, f32[2,128]{1,0:T(2,128)S(1)}, u32[]{:S(2)}, u32[]{:S(2)}) collective-permute-start(f32[2,128]{1,0:T(2,128)S(1)} %get-tuple-element.18), channel_id=1, source_target_pairs={{12,0},{13,1},{14,2},{15,3},{8,4},{9,5},{10,6},{11,7},{20,8},{21,9... | collective-permute-start | bytes 3080 | tf_op jit(solution)/shard_map/ppermute | solution.py:297
  22.2 2.0 %collective-permute-start.9 = (f32[2,128]{1,0:T(2,128)S(1)}, f32[2,128]{1,0:T(2,128)S(1)}, u32[]{:S(2)}, u32[]{:S(2)}) collective-permute-start(f32[2,128]{1,0:T(2,128)S(1)} %get-tuple-element.18), channel_id=1, source_target_pairs={{10,0},{11,1},{8,2},{9,3},{14,4},{15,5},{12,6},{13,7},{18,8},{19,9... | collective-permute-start | bytes 3080 | tf_op jit(solution)/shard_map/ppermute | solution.py:297
  24.2 1.0 %collective-permute-done.11.refs_2_ = f32[2,128]{1,0:T(2,128)S(1)} collective-permute-done((f32[2,128]{1,0:T(2,128)S(1)}, f32[2,128]{1,0:T(2,128)S(1)}, u32[]{:S(2)}, u32[]{:S(2)}) %collective-permute-start.11) | collective-permute-done | bytes 1056 | tf_op jit(solution)/shard_map/ppermute | solution.py:297
  25.2 1.1 %collective-permute-done.10.refs_1_ = f32[2,128]{1,0:T(2,128)S(1)} collective-permute-done((f32[2,128]{1,0:T(2,128)S(1)}, f32[2,128]{1,0:T(2,128)S(1)}, u32[]{:S(2)}, u32[]{:S(2)}) %collective-permute-start.10) | collective-permute-done | bytes 1056 | tf_op jit(solution)/shard_map/ppermute | solution.py:297
  26.3 0.1 collective-permute-done.9.refs_0_
  26.3 0.1 collective-permute-done.8.scaled_ref
  26.4 1.1 %shard_map.78 = bf16[128,1536]{1,0:T(8,128)(2,1)} custom-call(bf16[128,1664]{1,0:T(8,128)(2,1)S(1)} %collective-permute-done.8.scaled_ref, bf16[128,1536]{1,0:T(8,128)(2,1)S(1)} %collective-permute-done.7.input_ref, f32[2,128]{1,0:T(2,128)S(1)} %collective-permute-done.9.refs_0_, f32[2,128]{1,0:T(2,128)S(1)} %collective-permute-done.10.refs_1_, ...), custom_call_target="tpu_custom_call" | custom-call | tf_op jit(solution)/shard_map/pallas_call | solution.py:273
Async XLA Ops:
  0.0 4.4 %copy-start.1 = (bf16[1,128,1536]{2,1,0:T(8,128)(2,1)S(1)}, bf16[1,128,1536]{2,1,0:T(8,128)(2,1)}, u32[]{:S(2)}) copy-start(bf16[1,128,1536]{2,1,0:T(8,128)(2,1)} %param.12) | copy-start | bytes 1179652
  0.0 5.6 %copy-start = (bf16[1,1536,1024]{2,1,0:T(8,128)(2,1)S(1)}, bf16[1,1536,1024]{2,1,0:T(8,128)(2,1)}, u32[]{:S(2)}) copy-start(bf16[1,1536,1024]{2,1,0:T(8,128)(2,1)} %param.8) | copy-start | bytes 9437188
  0.0 5.6 %copy-start.2 = (f32[1,1536]{1,0:T(1,128)S(1)}, f32[1,1536]{1,0:T(1,128)}, u32[]{:S(2)}) copy-start(f32[1,1536]{1,0:T(1,128)} %refs_7_.1) | copy-start | bytes 18436
  1.0 4.6 %collective-permute-start.2 = (bf16[2,128,128]{2,1,0:T(8,128)(2,1)S(1)}, bf16[2,128,128]{2,1,0:T(8,128)(2,1)S(1)}, u32[]{:S(2)}, u32[]{:S(2)}) collective-permute-start(bf16[2,128,128]{2,1,0:T(8,128)(2,1)S(1)} %get-tuple-element.14.refs_3_), channel_id=1, source_target_pairs={{1,0},{0,1},{3,2},{2,3},{5,4},{4,5},{7,6},{6,7},{9,8},{8,9},{11,10... | collective-permute-start | bytes 196616 | tf_op jit(solution)/shard_map/ppermute | solution.py:24
  3.1 4.9 %collective-permute-start.1 = (bf16[128,128]{1,0:T(8,128)(2,1)S(1)}, bf16[128,128]{1,0:T(8,128)(2,1)S(1)}, u32[]{:S(2)}, u32[]{:S(2)}) collective-permute-start(bf16[128,128]{1,0:T(8,128)(2,1)S(1)} %get-tuple-element.13), channel_id=1, source_target_pairs={{17,0},{16,1},{19,2},{18,3},{21,4},{20,5},{23,6},{22,7},{25,8},{24... | collective-permute-start | bytes 98312 | tf_op jit(solution)/shard_map/ppermute | solution.py:297
  4.3 3.7 %collective-permute-start = (bf16[128,128]{1,0:T(8,128)(2,1)S(1)}, bf16[128,128]{1,0:T(8,128)(2,1)S(1)}, u32[]{:S(2)}, u32[]{:S(2)}) collective-permute-start(bf16[128,128]{1,0:T(8,128)(2,1)S(1)} %get-tuple-element.13), channel_id=1, source_target_pairs={{16,0},{17,1},{18,2},{19,3},{20,4},{21,5},{22,6},{23,7},{24,8},{25... | collective-permute-start | bytes 98312 | tf_op jit(solution)/shard_map/ppermute | solution.py:297
  4.4 10.0 %collective-permute-start.7 = (bf16[128,1536]{1,0:T(8,128)(2,1)S(1)}, bf16[128,1536]{1,0:T(8,128)(2,1)S(1)}, u32[]{:S(2)}, u32[]{:S(2)}) collective-permute-start(bf16[128,1536]{1,0:T(8,128)(2,1)S(1)} %bitcast.9), channel_id=1, source_target_pairs={{8,0},{16,8},{24,16},{0,24},{9,1},{17,9},{25,17},{1,25},{10,2},{18... | collective-permute-start | bytes 1179656 | tf_op jit(solution)/shard_map/ppermute | solution.py:20
  6.3 8.1 %collective-permute-start.6 = (bf16[144,1024]{1,0:T(8,128)(2,1)S(1)}, bf16[144,1024]{1,0:T(8,128)(2,1)S(1)}, u32[]{:S(2)}, u32[]{:S(2)}) collective-permute-start(bf16[144,1024]{1,0:T(8,128)(2,1)S(1)} %shard_map.76.refs_8_), channel_id=1, source_target_pairs={{1,0},{0,1},{3,2},{2,3},{5,4},{4,5},{7,6},{6,7},{9,8},{8,9},{11,10... | collective-permute-start | bytes 884744 | tf_op jit(solution)/shard_map/ppermute | solution.py:24
  8.2 5.0 %collective-permute-start.3 = (bf16[2,128,128]{2,1,0:T(8,128)(2,1)S(1)}, bf16[2,128,128]{2,1,0:T(8,128)(2,1)S(1)}, u32[]{:S(2)}, u32[]{:S(2)}) collective-permute-start(bf16[2,128,128]{2,1,0:T(8,128)(2,1)S(1)} %shard_map.74.refs_0_), channel_id=1, source_target_pairs={{6,0},{7,1},{4,2},{5,3},{2,4},{3,5},{0,6},{1,7},{14,8},{15,9},{12,... | collective-permute-start | bytes 196616 | tf_op jit(solution)/shard_map/ppermute | solution.py:24
  11.6 5.2 %collective-permute-start.5 = (bf16[2,128,128]{2,1,0:T(8,128)(2,1)S(1)}, bf16[2,128,128]{2,1,0:T(8,128)(2,1)S(1)}, u32[]{:S(2)}, u32[]{:S(2)}) collective-permute-start(bf16[2,128,128]{2,1,0:T(8,128)(2,1)S(1)} %shard_map.74.refs_0_), channel_id=1, source_target_pairs={{4,0},{5,1},{6,2},{7,3},{0,4},{1,5},{2,6},{3,7},{12,8},{13,9},{14,... | collective-permute-start | bytes 196616 | tf_op jit(solution)/shard_map/ppermute | solution.py:24
  11.6 5.2 %collective-permute-start.4 = (bf16[2,128,128]{2,1,0:T(8,128)(2,1)S(1)}, bf16[2,128,128]{2,1,0:T(8,128)(2,1)S(1)}, u32[]{:S(2)}, u32[]{:S(2)}) collective-permute-start(bf16[2,128,128]{2,1,0:T(8,128)(2,1)S(1)} %shard_map.74.refs_0_), channel_id=1, source_target_pairs={{2,0},{3,1},{0,2},{1,3},{6,4},{7,5},{4,6},{5,7},{10,8},{11,9},{8,1... | collective-permute-start | bytes 196616 | tf_op jit(solution)/shard_map/ppermute | solution.py:24
  17.5 8.8 %collective-permute-start.8 = (bf16[128,1664]{1,0:T(8,128)(2,1)S(1)}, bf16[128,1664]{1,0:T(8,128)(2,1)S(1)}, u32[]{:S(2)}, u32[]{:S(2)}) collective-permute-start(bf16[128,1664]{1,0:T(8,128)(2,1)S(1)} %get-tuple-element.16), channel_id=1, source_target_pairs={{8,0},{16,8},{24,16},{0,24},{9,1},{17,9},{25,17},{1,25},{10,2},{18... | collective-permute-start | bytes 1277960 | tf_op jit(solution)/shard_map/ppermute | solution.py:20
  19.5 5.7 %collective-permute-start.11 = (f32[2,128]{1,0:T(2,128)S(1)}, f32[2,128]{1,0:T(2,128)S(1)}, u32[]{:S(2)}, u32[]{:S(2)}) collective-permute-start(f32[2,128]{1,0:T(2,128)S(1)} %get-tuple-element.18), channel_id=1, source_target_pairs={{14,0},{15,1},{12,2},{13,3},{10,4},{11,5},{8,6},{9,7},{22,8},{23,9... | collective-permute-start | bytes 3080 | tf_op jit(solution)/shard_map/ppermute | solution.py:297
  21.5 4.8 %collective-permute-start.10 = (f32[2,128]{1,0:T(2,128)S(1)}, f32[2,128]{1,0:T(2,128)S(1)}, u32[]{:S(2)}, u32[]{:S(2)}) collective-permute-start(f32[2,128]{1,0:T(2,128)S(1)} %get-tuple-element.18), channel_id=1, source_target_pairs={{12,0},{13,1},{14,2},{15,3},{8,4},{9,5},{10,6},{11,7},{20,8},{21,9... | collective-permute-start | bytes 3080 | tf_op jit(solution)/shard_map/ppermute | solution.py:297
  22.2 4.1 %collective-permute-start.9 = (f32[2,128]{1,0:T(2,128)S(1)}, f32[2,128]{1,0:T(2,128)S(1)}, u32[]{:S(2)}, u32[]{:S(2)}) collective-permute-start(f32[2,128]{1,0:T(2,128)S(1)} %get-tuple-element.18), channel_id=1, source_target_pairs={{10,0},{11,1},{8,2},{9,3},{14,4},{15,5},{12,6},{13,7},{18,8},{19,9... | collective-permute-start | bytes 3080 | tf_op jit(solution)/shard_map/ppermute | solution.py:297

commit v3 on v2

--- a/solution.py
+++ b/solution.py
@@ -11,6 +11,7 @@
 LANES = 128
 PIECES = 4
 EXTRA = 16
+SHORT = pl.CostEstimate(flops=1 << 16, bytes_accessed=1 << 12, transcendentals=0)
 HIDES = pl.CostEstimate(flops=1 << 35, bytes_accessed=1 << 25, transcendentals=0)
 
 
@@ -97,8 +98,7 @@
     )(*map(in_hbm, (own, grad, spare, evicted)))
 
 
-def reach_kernel(weight_ref, input_ref, gain_ref, first_ref, reach_ref):
-    del first_ref
+def reach_kernel(weight_ref, input_ref, gain_ref, reach_ref):
     tokens, features = input_ref.shape
     values = input_ref[...].astype(jnp.float32)
     reach_ref[tokens:, :] = jnp.zeros_like(reach_ref[tokens:, :])
@@ -109,15 +109,15 @@
     reach_ref[:tokens, :] = reach.astype(reach_ref.dtype)
 
 
-def reach_of(weights, inputs, gain, first):
+def reach_of(weights, inputs, gain):
     return pl.pallas_call(
         reach_kernel,
         out_shape=pltpu.VMEM((inputs.shape[0] + EXTRA, weights.shape[1]), jnp.bfloat16),
-        in_specs=vmem_specs(4),
+        in_specs=vmem_specs(3),
         out_specs=pl.BlockSpec(memory_space=pltpu.VMEM),
-        cost_estimate=HIDES,
+        cost_estimate=SHORT,
         compiler_params=pltpu.CompilerParams(vmem_limit_bytes=8 << 20),
-    )(*map(in_vmem, (weights, inputs, gain, first)))
+    )(*map(in_vmem, (weights, inputs, gain)))
 
 
 def mix_kernel(taken_ref, *refs):
@@ -192,7 +192,7 @@
         in_specs=vmem_specs(len(blocks) + 1),
         out_specs=pl.BlockSpec(memory_space=pltpu.VMEM),
         scratch_shapes=[pltpu.VMEM((tokens, weights.shape[1]), jnp.bfloat16)],
-        cost_estimate=pl.CostEstimate(flops=1 << 16, bytes_accessed=1 << 12, transcendentals=0),
+        cost_estimate=SHORT,
         compiler_params=pltpu.CompilerParams(vmem_limit_bytes=16 << 20),
     )(*map(in_vmem, (*blocks, weights)))
 
@@ -284,7 +284,7 @@
 
 
 FAR, NEAR, SIDE = 4, 2, 1
-LINE = (FAR | NEAR, NEAR, FAR)
+LINE = ((FAR | NEAR, NEAR), (NEAR, FAR | NEAR), (FAR, FAR))
 EARLY = 2
 
 
@@ -298,13 +298,22 @@
 
 
 def gathered(pair, axis):
-    if lax.axis_size(axis) != 8:
+    count = lax.axis_size(axis)
+    if count != 8:
         return [lax.all_gather(pair[0], axis)], lambda place: place
-    blocks = [pair] + [swapped(pair, axis, mask) for mask in LINE]
-    masks = [far | side for far in (0, *LINE) for side in (0, SIDE)]
+    blocks = [pair]
+    for masks in LINE:
+        route = [
+            (s * count + (i ^ masks[s % 2]), s * count + i)
+            for s in range(lax.axis_size("section"))
+            for i in range(count)
+        ]
+        blocks.append(lax.ppermute(pair, ("section", axis), route))
 
     def head_of(place):
-        return lax.axis_index(axis) ^ masks[place]
+        even, odd = ((0, 0), *LINE)[place // 2]
+        mask = even + lax.rem(lax.axis_index("section"), 2) * (odd - even)
+        return lax.axis_index(axis) ^ mask ^ (place % 2 * SIDE)
 
     return blocks, head_of
 
@@ -318,8 +327,10 @@
         heads.append((swapped(packed, "tp", mask) if mask else packed, spare))
     weights, inputs = w_value[0], layer_input[0]
     next_input = passed_along(inputs, "section", -1)
-    reach = reach_of(weights, inputs, gain, heads[-1][0])
+    reach = reach_of(weights, inputs, gain)
     if count == 8:
+        reach, swap = lax.optimization_barrier((reach, heads[1][0]))
+        heads[1] = (swap, heads[1][1])
         reaches = [reach, swapped(reach, "tp", SIDE)]
         reaches[1], next_input = lax.optimization_barrier((reaches[1], next_input))
     else:

time: 27.9 us -> 28.6 us (1.025)
  waiting for transfers between devices: 6.36 us -> 7.29 us
  starting transfers between devices: 16.7 us -> 16.4 us
    ppermute x5 -> x2, starting transfers between devices: 7.61 us -> 3.87 us  [swapped(): lax.ppermute(block, axis, [(i ^ mask, i) for i in range(lax.axis_size(axi...]
    ppermute x0 -> x3, starting transfers between devices: none -> 3.66 us  [gathered(): blocks.append(lax.ppermute(pair, ('section', axis), route))]
    ppermute x0 -> x3, waiting for transfers between devices: none -> 2.7 us  [gathered(): blocks.append(lax.ppermute(pair, ('section', axis), route))]
    ppermute x5 -> x2, waiting for transfers between devices: 4.12 us -> 2.29 us  [swapped(): lax.ppermute(block, axis, [(i ^ mask, i) for i in range(lax.axis_size(axi...]
  transfers between devices with their start and end apart: 12 -> 12, of which waited for: 7 -> 6; matrix products, arithmetic and copies ran while one was open for 0% -> 0% of each run, Pallas kernels for 6% -> 5%
where the time goes in v3:
time: 28.6 us; the launch traced here: 28.1 us
  starting transfers between devices  16.4 us (57%)
  waiting for transfers between devices  7.29 us (25%)
  Pallas kernels  4.32 us (15%)
    ppermute x5, starting transfers between devices, handed_over(): return lax.ppermute(block, ('section', 'tp'), route)  5.97 us
    ppermute x2, starting transfers between devices, swapped(): lax.ppermute(block, axis, [(i ^ mask, i) for i in range(lax.axis_size(axi...  3.87 us
    ppermute x3, starting transfers between devices, gathered(): blocks.append(lax.ppermute(pair, ('section', axis), route))  3.66 us
    ppermute x2, starting transfers between devices, passed_along(): return lax.ppermute(block, axis, route)  2.92 us
    ppermute x3, waiting for transfers between devices, gathered(): blocks.append(lax.ppermute(pair, ('section', axis), route))  2.7 us
    ppermute x2, waiting for transfers between devices, swapped(): lax.ppermute(block, axis, [(i ^ mask, i) for i in range(lax.axis_size(axi...  2.29 us
    ppermute x5, waiting for transfers between devices, handed_over(): return lax.ppermute(block, ('section', 'tp'), route)  2.24 us
    pallas_call x1, Pallas kernels, finish(): pl.pallas_call(finish_kernel, out_shape=pltpu.HBM(inputs.shape, jnp.bfloa...  1.06 us
  transfers between devices with their start and end apart: 12, of which 6 were waited for; matrix products, arithmetic and copies ran while one was open for 0% of the time, Pallas kernels for 5%

profile of v3, /device:TPU:1, one launch (start us, length us, event | category | flops | bytes accessed | tf_op | source)
XLA Modules:
  0.0 28.1 jit_solution(4095586679020437333)
XLA Ops:
  0.0 0.0 copy-start.1
  0.0 0.0 copy-start
  0.0 0.0 copy-start.2
  0.0 1.0 %shard_map.73 = (bf16[2,128,128]{2,1,0:T(8,128)(2,1)S(1)}, bf16[128,128]{1,0:T(8,128)(2,1)S(1)}, bf16[128,128]{1,0:T(8,128)(2,1)S(1)}) custom-call(bf16[128,128]{1,0:T(8,128)(2,1)} %bitcast.12, bf16[128,128]{1,0:T(8,128)(2,1)} %bitcast.13, bf16[128,128]{1,0:T(8,128)(2,1)} %bitcast.14, s32[1,4]{1,0:T(1,128)} %evicted_ref.1), custom_call_target="tpu_custom_call" | custom-call | flops 34359738368 | bytes 33554432 | tf_op jit(solution)/shard_map/pallas_call | solution.py:83
  1.0 2.1 %collective-permute-start.2 = (bf16[2,128,128]{2,1,0:T(8,128)(2,1)S(1)}, bf16[2,128,128]{2,1,0:T(8,128)(2,1)S(1)}, u32[]{:S(2)}, u32[]{:S(2)}) collective-permute-start(bf16[2,128,128]{2,1,0:T(8,128)(2,1)S(1)} %get-tuple-element.16.refs_3_), channel_id=1, source_target_pairs={{1,0},{0,1},{3,2},{2,3},{5,4},{4,5},{7,6},{6,7},{9,8},{8,9},{11,10... | collective-permute-start | bytes 196616 | tf_op jit(solution)/shard_map/ppermute | solution.py:25
  3.1 1.2 %collective-permute-start.1 = (bf16[128,128]{1,0:T(8,128)(2,1)S(1)}, bf16[128,128]{1,0:T(8,128)(2,1)S(1)}, u32[]{:S(2)}, u32[]{:S(2)}) collective-permute-start(bf16[128,128]{1,0:T(8,128)(2,1)S(1)} %get-tuple-element.15), channel_id=1, source_target_pairs={{17,0},{16,1},{19,2},{18,3},{21,4},{20,5},{23,6},{22,7},{25,8},{24... | collective-permute-start | bytes 98312 | tf_op jit(solution)/shard_map/ppermute | solution.py:297
  4.3 0.1 collective-permute-start
  4.4 0.0 copy-done.1
  4.4 1.2 %collective-permute-start.7 = (bf16[128,1536]{1,0:T(8,128)(2,1)S(1)}, bf16[128,1536]{1,0:T(8,128)(2,1)S(1)}, u32[]{:S(2)}, u32[]{:S(2)}) collective-permute-start(bf16[128,1536]{1,0:T(8,128)(2,1)S(1)} %bitcast.9), channel_id=1, source_target_pairs={{8,0},{16,8},{24,16},{0,24},{9,1},{17,9},{25,17},{1,25},{10,2},{18... | collective-permute-start | bytes 1179656 | tf_op jit(solution)/shard_map/ppermute | solution.py:21
  5.6 0.0 copy-done
  5.6 0.0 copy-done.2
  5.6 0.6 %shard_map.74.refs_8_ = bf16[144,1024]{1,0:T(8,128)(2,1)S(1)} custom-call(bf16[1536,1024]{1,0:T(8,128)(2,1)S(1)} %bitcast.6, bf16[128,1536]{1,0:T(8,128)(2,1)S(1)} %bitcast.10, f32[1,1536]{1,0:T(1,128)S(1)} %copy-done.2), custom_call_target="tpu_custom_call" | custom-call | flops 65536 | bytes 4096 | tf_op jit(solution)/shard_map/pallas_call | solution.py:113
  6.3 0.0 collective-permute-done.2.refs_2_
  6.3 1.7 %collective-permute-start.6 = (bf16[144,1024]{1,0:T(8,128)(2,1)S(1)}, bf16[144,1024]{1,0:T(8,128)(2,1)S(1)}, u32[]{:S(2)}, u32[]{:S(2)}) collective-permute-start(bf16[144,1024]{1,0:T(8,128)(2,1)S(1)} %shard_map.74.refs_8_), channel_id=1, source_target_pairs={{1,0},{0,1},{3,2},{2,3},{5,4},{4,5},{7,6},{6,7},{9,8},{8,9},{11,10... | collective-permute-start | bytes 884744 | tf_op jit(solution)/shard_map/ppermute | solution.py:25
  8.0 0.0 collective-permute-done.1.refs_1_
  8.0 0.0 collective-permute-done.refs_0_
  8.0 0.2 shard_map.75.refs_0_
  8.2 1.4 %collective-permute-start.3 = (bf16[2,128,128]{2,1,0:T(8,128)(2,1)S(1)}, bf16[2,128,128]{2,1,0:T(8,128)(2,1)S(1)}, u32[]{:S(2)}, u32[]{:S(2)}) collective-permute-start(bf16[2,128,128]{2,1,0:T(8,128)(2,1)S(1)} %shard_map.75.refs_0_), channel_id=1, source_target_pairs={{6,0},{7,1},{4,2},{5,3},{2,4},{3,5},{0,6},{1,7},{10,8},{11,9},{8,1... | collective-permute-start | bytes 196616 | tf_op jit(solution)/shard_map/ppermute | solution.py:311
  9.6 2.3 %collective-permute-start.5 = (bf16[2,128,128]{2,1,0:T(8,128)(2,1)S(1)}, bf16[2,128,128]{2,1,0:T(8,128)(2,1)S(1)}, u32[]{:S(2)}, u32[]{:S(2)}) collective-permute-start(bf16[2,128,128]{2,1,0:T(8,128)(2,1)S(1)} %shard_map.75.refs_0_), channel_id=1, source_target_pairs={{4,0},{5,1},{6,2},{7,3},{0,4},{1,5},{2,6},{3,7},{12,8},{13,9},{14,... | collective-permute-start | bytes 196616 | tf_op jit(solution)/shard_map/ppermute | solution.py:311
  11.9 0.0 collective-permute-start.4
  11.9 0.0 collective-permute-done.3.refs_1_
  11.9 0.7 %shard_map.76.refs_4_ = f32[128,1536]{1,0:T(8,128)S(1)} custom-call(bf16[2,128,128]{2,1,0:T(8,128)(2,1)S(1)} %shard_map.75.refs_0_, bf16[2,128,128]{2,1,0:T(8,128)(2,1)S(1)} %collective-permute-done.3.refs_1_, bf16[1536,1024]{1,0:T(8,128)(2,1)S(1)} %bitcast.7), custom_call_target="tpu_custom_call" | custom-call | flops 65536 | bytes 4096 | tf_op jit(solution)/shard_map/pallas_call | solution.py:189
  12.6 2.3 %collective-permute-done.6.refs_9_ = bf16[144,1024]{1,0:T(8,128)(2,1)S(1)} collective-permute-done((bf16[144,1024]{1,0:T(8,128)(2,1)S(1)}, bf16[144,1024]{1,0:T(8,128)(2,1)S(1)}, u32[]{:S(2)}, u32[]{:S(2)}) %collective-permute-start.6) | collective-permute-done | bytes 294944 | tf_op jit(solution)/shard_map/ppermute | solution.py:25
  14.9 0.0 collective-permute-done.7.input_ref
  14.9 0.5 %collective-permute-done.5.refs_3_ = bf16[2,128,128]{2,1,0:T(8,128)(2,1)S(1)} collective-permute-done((bf16[2,128,128]{2,1,0:T(8,128)(2,1)S(1)}, bf16[2,128,128]{2,1,0:T(8,128)(2,1)S(1)}, u32[]{:S(2)}, u32[]{:S(2)}) %collective-permute-start.5) | collective-permute-done | bytes 65568 | tf_op jit(solution)/shard_map/ppermute | solution.py:311
  15.4 2.2 %collective-permute-done.4.refs_2_ = bf16[2,128,128]{2,1,0:T(8,128)(2,1)S(1)} collective-permute-done((bf16[2,128,128]{2,1,0:T(8,128)(2,1)S(1)}, bf16[2,128,128]{2,1,0:T(8,128)(2,1)S(1)}, u32[]{:S(2)}, u32[]{:S(2)}) %collective-permute-start.4) | collective-permute-done | bytes 65568 | tf_op jit(solution)/shard_map/ppermute | solution.py:311
  17.6 0.8 %shard_map.77 = (bf16[128,1664]{1,0:T(8,128)(2,1)S(1)}, f32[2,128]{1,0:T(2,128)S(1)}) custom-call(bf16[2,128,128]{2,1,0:T(8,128)(2,1)S(1)} %shard_map.75.refs_0_, bf16[2,128,128]{2,1,0:T(8,128)(2,1)S(1)} %collective-permute-done.3.refs_1_, bf16[2,128,128]{2,1,0:T(8,128)(2,1)S(1)} %collective-permute-done.4.refs_2_, ...), custom_call_target="tpu_custom_call" | custom-call | flops 34359738368 | bytes 33554432 | tf_op jit(solution)/shard_map/pallas_call | solution.py:232
  18.3 1.7 %collective-permute-start.8 = (bf16[128,1664]{1,0:T(8,128)(2,1)S(1)}, bf16[128,1664]{1,0:T(8,128)(2,1)S(1)}, u32[]{:S(2)}, u32[]{:S(2)}) collective-permute-start(bf16[128,1664]{1,0:T(8,128)(2,1)S(1)} %get-tuple-element.20), channel_id=1, source_target_pairs={{8,0},{16,8},{24,16},{0,24},{9,1},{17,9},{25,17},{1,25},{10,2},{18... | collective-permute-start | bytes 1277960 | tf_op jit(solution)/shard_map/ppermute | solution.py:21
  20.0 2.1 %collective-permute-start.11 = (f32[2,128]{1,0:T(2,128)S(1)}, f32[2,128]{1,0:T(2,128)S(1)}, u32[]{:S(2)}, u32[]{:S(2)}) collective-permute-start(f32[2,128]{1,0:T(2,128)S(1)} %get-tuple-element.22), channel_id=1, source_target_pairs={{14,0},{15,1},{12,2},{13,3},{10,4},{11,5},{8,6},{9,7},{22,8},{23,9... | collective-permute-start | bytes 3080 | tf_op jit(solution)/shard_map/ppermute | solution.py:297
  22.2 0.0 collective-permute-start.10
  22.2 2.6 %collective-permute-start.9 = (f32[2,128]{1,0:T(2,128)S(1)}, f32[2,128]{1,0:T(2,128)S(1)}, u32[]{:S(2)}, u32[]{:S(2)}) collective-permute-start(f32[2,128]{1,0:T(2,128)S(1)} %get-tuple-element.22), channel_id=1, source_target_pairs={{10,0},{11,1},{8,2},{9,3},{14,4},{15,5},{12,6},{13,7},{18,8},{19,9... | collective-permute-start | bytes 3080 | tf_op jit(solution)/shard_map/ppermute | solution.py:297
  24.7 1.0 %collective-permute-done.11.refs_2_ = f32[2,128]{1,0:T(2,128)S(1)} collective-permute-done((f32[2,128]{1,0:T(2,128)S(1)}, f32[2,128]{1,0:T(2,128)S(1)}, u32[]{:S(2)}, u32[]{:S(2)}) %collective-permute-start.11) | collective-permute-done | bytes 1056 | tf_op jit(solution)/shard_map/ppermute | solution.py:297
  25.7 1.2 %collective-permute-done.10.refs_1_ = f32[2,128]{1,0:T(2,128)S(1)} collective-permute-done((f32[2,128]{1,0:T(2,128)S(1)}, f32[2,128]{1,0:T(2,128)S(1)}, u32[]{:S(2)}, u32[]{:S(2)}) %collective-permute-start.10) | collective-permute-done | bytes 1056 | tf_op jit(solution)/shard_map/ppermute | solution.py:297
  27.0 0.0 collective-permute-done.9.refs_0_
  27.0 0.1 collective-permute-done.8.scaled_ref
  27.0 1.1 %shard_map.78 = bf16[128,1536]{1,0:T(8,128)(2,1)} custom-call(bf16[128,1664]{1,0:T(8,128)(2,1)S(1)} %collective-permute-done.8.scaled_ref, bf16[128,1536]{1,0:T(8,128)(2,1)S(1)} %collective-permute-done.7.input_ref, f32[2,128]{1,0:T(2,128)S(1)} %collective-permute-done.9.refs_0_, f32[2,128]{1,0:T(2,128)S(1)} %collective-permute-done.10.refs_1_, ...), custom_call_target="tpu_custom_call" | custom-call | tf_op jit(solution)/shard_map/pallas_call | solution.py:273
Async XLA Ops:
  0.0 4.4 %copy-start.1 = (bf16[1,128,1536]{2,1,0:T(8,128)(2,1)S(1)}, bf16[1,128,1536]{2,1,0:T(8,128)(2,1)}, u32[]{:S(2)}) copy-start(bf16[1,128,1536]{2,1,0:T(8,128)(2,1)} %param.12) | copy-start | bytes 1179652
  0.0 5.6 %copy-start = (bf16[1,1536,1024]{2,1,0:T(8,128)(2,1)S(1)}, bf16[1,1536,1024]{2,1,0:T(8,128)(2,1)}, u32[]{:S(2)}) copy-start(bf16[1,1536,1024]{2,1,0:T(8,128)(2,1)} %param.8) | copy-start | bytes 9437188
  0.0 5.6 %copy-start.2 = (f32[1,1536]{1,0:T(1,128)S(1)}, f32[1,1536]{1,0:T(1,128)}, u32[]{:S(2)}) copy-start(f32[1,1536]{1,0:T(1,128)} %refs_7_.1) | copy-start | bytes 18436
  1.0 5.3 %collective-permute-start.2 = (bf16[2,128,128]{2,1,0:T(8,128)(2,1)S(1)}, bf16[2,128,128]{2,1,0:T(8,128)(2,1)S(1)}, u32[]{:S(2)}, u32[]{:S(2)}) collective-permute-start(bf16[2,128,128]{2,1,0:T(8,128)(2,1)S(1)} %get-tuple-element.16.refs_3_), channel_id=1, source_target_pairs={{1,0},{0,1},{3,2},{2,3},{5,4},{4,5},{7,6},{6,7},{9,8},{8,9},{11,10... | collective-permute-start | bytes 196616 | tf_op jit(solution)/shard_map/ppermute | solution.py:25
  3.1 4.9 %collective-permute-start.1 = (bf16[128,128]{1,0:T(8,128)(2,1)S(1)}, bf16[128,128]{1,0:T(8,128)(2,1)S(1)}, u32[]{:S(2)}, u32[]{:S(2)}) collective-permute-start(bf16[128,128]{1,0:T(8,128)(2,1)S(1)} %get-tuple-element.15), channel_id=1, source_target_pairs={{17,0},{16,1},{19,2},{18,3},{21,4},{20,5},{23,6},{22,7},{25,8},{24... | collective-permute-start | bytes 98312 | tf_op jit(solution)/shard_map/ppermute | solution.py:297
  4.3 3.8 %collective-permute-start = (bf16[128,128]{1,0:T(8,128)(2,1)S(1)}, bf16[128,128]{1,0:T(8,128)(2,1)S(1)}, u32[]{:S(2)}, u32[]{:S(2)}) collective-permute-start(bf16[128,128]{1,0:T(8,128)(2,1)S(1)} %get-tuple-element.15), channel_id=1, source_target_pairs={{16,0},{17,1},{18,2},{19,3},{20,4},{21,5},{22,6},{23,7},{24,8},{25... | collective-permute-start | bytes 98312 | tf_op jit(solution)/shard_map/ppermute | solution.py:297
  4.4 10.5 %collective-permute-start.7 = (bf16[128,1536]{1,0:T(8,128)(2,1)S(1)}, bf16[128,1536]{1,0:T(8,128)(2,1)S(1)}, u32[]{:S(2)}, u32[]{:S(2)}) collective-permute-start(bf16[128,1536]{1,0:T(8,128)(2,1)S(1)} %bitcast.9), channel_id=1, source_target_pairs={{8,0},{16,8},{24,16},{0,24},{9,1},{17,9},{25,17},{1,25},{10,2},{18... | collective-permute-start | bytes 1179656 | tf_op jit(solution)/shard_map/ppermute | solution.py:21
  6.3 8.6 %collective-permute-start.6 = (bf16[144,1024]{1,0:T(8,128)(2,1)S(1)}, bf16[144,1024]{1,0:T(8,128)(2,1)S(1)}, u32[]{:S(2)}, u32[]{:S(2)}) collective-permute-start(bf16[144,1024]{1,0:T(8,128)(2,1)S(1)} %shard_map.74.refs_8_), channel_id=1, source_target_pairs={{1,0},{0,1},{3,2},{2,3},{5,4},{4,5},{7,6},{6,7},{9,8},{8,9},{11,10... | collective-permute-start | bytes 884744 | tf_op jit(solution)/shard_map/ppermute | solution.py:25
  8.2 3.7 %collective-permute-start.3 = (bf16[2,128,128]{2,1,0:T(8,128)(2,1)S(1)}, bf16[2,128,128]{2,1,0:T(8,128)(2,1)S(1)}, u32[]{:S(2)}, u32[]{:S(2)}) collective-permute-start(bf16[2,128,128]{2,1,0:T(8,128)(2,1)S(1)} %shard_map.75.refs_0_), channel_id=1, source_target_pairs={{6,0},{7,1},{4,2},{5,3},{2,4},{3,5},{0,6},{1,7},{10,8},{11,9},{8,1... | collective-permute-start | bytes 196616 | tf_op jit(solution)/shard_map/ppermute | solution.py:311
  9.6 5.8 %collective-permute-start.5 = (bf16[2,128,128]{2,1,0:T(8,128)(2,1)S(1)}, bf16[2,128,128]{2,1,0:T(8,128)(2,1)S(1)}, u32[]{:S(2)}, u32[]{:S(2)}) collective-permute-start(bf16[2,128,128]{2,1,0:T(8,128)(2,1)S(1)} %shard_map.75.refs_0_), channel_id=1, source_target_pairs={{4,0},{5,1},{6,2},{7,3},{0,4},{1,5},{2,6},{3,7},{12,8},{13,9},{14,... | collective-permute-start | bytes 196616 | tf_op jit(solution)/shard_map/ppermute | solution.py:311
  11.9 5.7 %collective-permute-start.4 = (bf16[2,128,128]{2,1,0:T(8,128)(2,1)S(1)}, bf16[2,128,128]{2,1,0:T(8,128)(2,1)S(1)}, u32[]{:S(2)}, u32[]{:S(2)}) collective-permute-start(bf16[2,128,128]{2,1,0:T(8,128)(2,1)S(1)} %shard_map.75.refs_0_), channel_id=1, source_target_pairs={{2,0},{3,1},{0,2},{1,3},{6,4},{7,5},{4,6},{5,7},{14,8},{15,9},{12,... | collective-permute-start | bytes 196616 | tf_op jit(solution)/shard_map/ppermute | solution.py:311
  18.3 8.7 %collective-permute-start.8 = (bf16[128,1664]{1,0:T(8,128)(2,1)S(1)}, bf16[128,1664]{1,0:T(8,128)(2,1)S(1)}, u32[]{:S(2)}, u32[]{:S(2)}) collective-permute-start(bf16[128,1664]{1,0:T(8,128)(2,1)S(1)} %get-tuple-element.20), channel_id=1, source_target_pairs={{8,0},{16,8},{24,16},{0,24},{9,1},{17,9},{25,17},{1,25},{10,2},{18... | collective-permute-start | bytes 1277960 | tf_op jit(solution)/shard_map/ppermute | solution.py:21
  20.0 5.7 %collective-permute-start.11 = (f32[2,128]{1,0:T(2,128)S(1)}, f32[2,128]{1,0:T(2,128)S(1)}, u32[]{:S(2)}, u32[]{:S(2)}) collective-permute-start(f32[2,128]{1,0:T(2,128)S(1)} %get-tuple-element.22), channel_id=1, source_target_pairs={{14,0},{15,1},{12,2},{13,3},{10,4},{11,5},{8,6},{9,7},{22,8},{23,9... | collective-permute-start | bytes 3080 | tf_op jit(solution)/shard_map/ppermute | solution.py:297
  22.2 4.8 %collective-permute-start.10 = (f32[2,128]{1,0:T(2,128)S(1)}, f32[2,128]{1,0:T(2,128)S(1)}, u32[]{:S(2)}, u32[]{:S(2)}) collective-permute-start(f32[2,128]{1,0:T(2,128)S(1)} %get-tuple-element.22), channel_id=1, source_target_pairs={{12,0},{13,1},{14,2},{15,3},{8,4},{9,5},{10,6},{11,7},{20,8},{21,9... | collective-permute-start | bytes 3080 | tf_op jit(solution)/shard_map/ppermute | solution.py:297
  22.2 4.8 %collective-permute-start.9 = (f32[2,128]{1,0:T(2,128)S(1)}, f32[2,128]{1,0:T(2,128)S(1)}, u32[]{:S(2)}, u32[]{:S(2)}) collective-permute-start(f32[2,128]{1,0:T(2,128)S(1)} %get-tuple-element.22), channel_id=1, source_target_pairs={{10,0},{11,1},{8,2},{9,3},{14,4},{15,5},{12,6},{13,7},{18,8},{19,9... | collective-permute-start | bytes 3080 | tf_op jit(solution)/shard_map/ppermute | solution.py:297

commit v4 on v2

--- a/solution.py
+++ b/solution.py
@@ -11,6 +11,7 @@
 LANES = 128
 PIECES = 4
 EXTRA = 16
+SHORT = pl.CostEstimate(flops=1 << 16, bytes_accessed=1 << 12, transcendentals=0)
 HIDES = pl.CostEstimate(flops=1 << 35, bytes_accessed=1 << 25, transcendentals=0)
 
 
@@ -57,91 +58,110 @@
     return jnp.concatenate(split(row) + [rest]).astype(jnp.bfloat16)
 
 
-def pack_kernel(own_ref, grad_ref, spare_ref, evicted_ref, *refs):
-    out_ref, spare_out, taken_ref, flags, sems = refs
-    copies = [
+def load_kernel(grad_ref, weight_ref, own_ref, evicted_ref, input_ref, gain_ref, *rest):
+    grad_out, weight_out, own_out, taken_out, input_out, gain_out, reach_ref = rest[:7]
+    flags, sems = rest[7:]
+    small = [
         pltpu.make_async_copy(evicted_ref, flags, sems.at[0]),
-        pltpu.make_async_copy(own_ref, out_ref.at[0], sems.at[1]),
-        pltpu.make_async_copy(grad_ref, out_ref.at[1], sems.at[2]),
-        pltpu.make_async_copy(spare_ref, spare_out, sems.at[3]),
+        pltpu.make_async_copy(own_ref, own_out, sems.at[1]),
+        pltpu.make_async_copy(grad_ref, grad_out, sems.at[2]),
+        pltpu.make_async_copy(gain_ref, gain_out, sems.at[3]),
+        pltpu.make_async_copy(input_ref, input_out, sems.at[4]),
     ]
-    for copy in copies:
+    for copy in small:
         copy.start()
-    copies[0].wait()
+    large = []
+    features = weight_ref.shape[0]
+    for j in range(PIECES):
+        part = pl.ds(j * (features // PIECES), features // PIECES)
+        large.append(
+            pltpu.make_async_copy(weight_ref.at[part], weight_out.at[part], sems.at[5 + j])
+        )
+        large[-1].start()
+    small[0].wait()
+    small[1].wait()
     tiles = evicted_ref.shape[1]
-    rows = taken_ref.shape[0] // tiles
+    rows = own_ref.shape[0] // tiles
     for tile in range(tiles):
         part = pl.ds(tile * rows, rows)
-        taken = jnp.full((rows, taken_ref.shape[1]), flags[0, tile], jnp.int32)
-        taken_ref[part, :] = taken.astype(jnp.float32).astype(taken_ref.dtype)
-    for copy in copies[1:]:
-        copy.wait()
-
-
-def pack(own, grad, spare, evicted):
-    return pl.pallas_call(
-        pack_kernel,
-        out_shape=(
-            pltpu.VMEM((2, *own.shape), own.dtype),
-            pltpu.VMEM(spare.shape, spare.dtype),
-            pltpu.VMEM(own.shape, own.dtype),
-        ),
-        in_specs=[pl.BlockSpec(memory_space=pltpu.HBM)] * 4,
-        out_specs=tuple(vmem_specs(3)),
-        scratch_shapes=[
-            pltpu.SMEM(evicted.shape, evicted.dtype),
-            pltpu.SemaphoreType.DMA((4,)),
-        ],
-        cost_estimate=HIDES,
-        compiler_params=pltpu.CompilerParams(vmem_limit_bytes=4 << 20),
-    )(*map(in_hbm, (own, grad, spare, evicted)))
-
-
-def reach_kernel(weight_ref, input_ref, gain_ref, first_ref, reach_ref):
-    del first_ref
-    tokens, features = input_ref.shape
-    values = input_ref[...].astype(jnp.float32)
+        taken = jnp.full((rows, own_ref.shape[1]), flags[0, tile], jnp.int32).astype(jnp.float32)
+        own = own_out[part, :].astype(jnp.float32)
+        own_out[part, :] = ((1.0 - taken) * own).astype(own_out.dtype)
+        taken_out[part, :] = taken.astype(taken_out.dtype)
+    small[2].wait()
+    small[3].wait()
+    small[4].wait()
+    values = input_out[...].astype(jnp.float32)
+    tokens = values.shape[0]
     reach_ref[tokens:, :] = jnp.zeros_like(reach_ref[tokens:, :])
     squares = as_row(jnp.sum(values * values, axis=1, keepdims=True))
     reach_ref[tokens:, :tokens] = as_parts(squares)
-    gained = (values * gain_ref[...]).astype(jnp.bfloat16)
-    reach = jnp.dot(gained, weight_ref[...], preferred_element_type=jnp.float32)
+    gained = (values * gain_out[...]).astype(jnp.bfloat16)
+    reach = jnp.zeros((tokens, weight_out.shape[1]), jnp.float32)
+    for j, copy in enumerate(large):
+        copy.wait()
+        part = slice(j * (features // PIECES), (j + 1) * (features // PIECES))
+        reach += jnp.dot(gained[:, part], weight_out[part, :], preferred_element_type=jnp.float32)
     reach_ref[:tokens, :] = reach.astype(reach_ref.dtype)
 
 
-def reach_of(weights, inputs, gain, first):
-    return pl.pallas_call(
-        reach_kernel,
-        out_shape=pltpu.VMEM((inputs.shape[0] + EXTRA, weights.shape[1]), jnp.bfloat16),
+def load(grad, weights, own, evicted, inputs, gain):
+    return pl.pallas_call(
+        load_kernel,
+        out_shape=(
+            pltpu.VMEM(grad.shape, grad.dtype),
+            pltpu.VMEM(weights.shape, weights.dtype),
+            pltpu.VMEM(own.shape, own.dtype),
+            pltpu.VMEM(own.shape, own.dtype),
+            pltpu.VMEM(inputs.shape, inputs.dtype),
+            pltpu.VMEM(gain.shape, gain.dtype),
+            pltpu.VMEM((inputs.shape[0] + EXTRA, weights.shape[1]), jnp.bfloat16),
+        ),
+        in_specs=[pl.BlockSpec(memory_space=pltpu.HBM)] * 6,
+        out_specs=tuple(vmem_specs(7)),
+        scratch_shapes=[
+            pltpu.SMEM(evicted.shape, evicted.dtype),
+            pltpu.SemaphoreType.DMA((5 + PIECES,)),
+        ],
+        cost_estimate=HIDES,
+        compiler_params=pltpu.CompilerParams(vmem_limit_bytes=8 << 20),
+    )(*map(in_hbm, (grad, weights, own, evicted, inputs, gain)))
+
+
+def mix_kernel(own_ref, taken_ref, spare_ref, grad_ref, out_ref):
+    out_ref[0] = lax.dot_general(
+        own_ref[...] + spare_ref[...] * taken_ref[...],
+        grad_ref[...],
+        (((0,), (0,)), ((), ())),
+        preferred_element_type=jnp.float32,
+    ).astype(out_ref.dtype)
+
+
+def value_gradient(own, taken, spare, grad):
+    return pl.pallas_call(
+        mix_kernel,
+        out_shape=pltpu.VMEM((1, *grad.shape), jnp.bfloat16),
         in_specs=vmem_specs(4),
         out_specs=pl.BlockSpec(memory_space=pltpu.VMEM),
-        cost_estimate=HIDES,
-        compiler_params=pltpu.CompilerParams(vmem_limit_bytes=8 << 20),
-    )(*map(in_vmem, (weights, inputs, gain, first)))
-
-
-def mix_kernel(taken_ref, *refs):
-    out_ref = refs[-1]
-    taken = taken_ref[...]
-    for j in range(out_ref.shape[0]):
-        packed_ref, spare_ref = refs[len(refs) - 2 - j], refs[j]
-        out_ref[j] = lax.dot_general(
-            packed_ref[0] * (1 - taken) + spare_ref[...] * taken,
-            packed_ref[1],
-            (((0,), (0,)), ((), ())),
-            preferred_element_type=jnp.float32,
-        ).astype(out_ref.dtype)
-
-
-def value_gradients(taken, heads):
-    return pl.pallas_call(
-        mix_kernel,
-        out_shape=pltpu.VMEM((len(heads), *heads[0][1].shape), jnp.bfloat16),
-        in_specs=vmem_specs(1 + 2 * len(heads)),
+        cost_estimate=SHORT,
+        compiler_params=pltpu.CompilerParams(vmem_limit_bytes=4 << 20),
+    )(*map(in_vmem, (own, taken, spare, grad)))
+
+
+def join_kernel(own_ref, other_ref, out_ref):
+    out_ref[0] = own_ref[0]
+    out_ref[1] = other_ref[0]
+
+
+def join(own, other):
+    return pl.pallas_call(
+        join_kernel,
+        out_shape=pltpu.VMEM((2, *own.shape[1:]), own.dtype),
+        in_specs=vmem_specs(2),
         out_specs=pl.BlockSpec(memory_space=pltpu.VMEM),
         cost_estimate=HIDES,
         compiler_params=pltpu.CompilerParams(vmem_limit_bytes=4 << 20),
-    )(*map(in_vmem, (taken, *[spare for _, spare in heads], *[packed for packed, _ in heads[::-1]])))
+    )(in_vmem(own), in_vmem(other))
 
 
 def column_tile(features):
@@ -192,7 +212,7 @@
         in_specs=vmem_specs(len(blocks) + 1),
         out_specs=pl.BlockSpec(memory_space=pltpu.VMEM),
         scratch_shapes=[pltpu.VMEM((tokens, weights.shape[1]), jnp.bfloat16)],
-        cost_estimate=pl.CostEstimate(flops=1 << 16, bytes_accessed=1 << 12, transcendentals=0),
+        cost_estimate=SHORT,
         compiler_params=pltpu.CompilerParams(vmem_limit_bytes=16 << 20),
     )(*map(in_vmem, (*blocks, weights)))
 
@@ -311,23 +331,21 @@
 
 def per_device(grad_attn, w_value, probs_own, probs_spare, evicted, layer_input, gain):
     sections, count = lax.axis_size("section"), lax.axis_size("tp")
-    packed, spares, taken = pack(probs_own[0, 0], grad_attn[0, 0], probs_spare[0, 0], evicted)
-    heads = []
-    for mask in (0, SIDE) if count == 8 else (0,):
-        spare = handed_over(spares, sections, count, sections // 2, mask)
-        heads.append((swapped(packed, "tp", mask) if mask else packed, spare))
-    weights, inputs = w_value[0], layer_input[0]
+    spare = passed_along(probs_spare[0, 0], "section", sections // 2)
+    grad, weights, own, taken, inputs, gains, reach = load(
+        grad_attn[0, 0], w_value[0], probs_own[0, 0], evicted, layer_input[0], gain
+    )
     next_input = passed_along(inputs, "section", -1)
-    reach = reach_of(weights, inputs, gain, heads[-1][0])
     if count == 8:
         reaches = [reach, swapped(reach, "tp", SIDE)]
         reaches[1], next_input = lax.optimization_barrier((reaches[1], next_input))
     else:
         reaches = [lax.psum(reach, "tp")]
-    pair = value_gradients(taken, heads)
+    held = value_gradient(own, taken, spare, grad)
+    pair = join(held, swapped(held, "tp", SIDE)) if count == 8 else held
     blocks, head_of = gathered(pair, "tp")
     early = [project_early(head_of, blocks[:EARLY], weights)] if count == 8 else []
-    scaled, sums = project(head_of, blocks, early, weights, inputs, gain, reaches)
+    scaled, sums = project(head_of, blocks, early, weights, inputs, gains, reaches)
     next_scaled = passed_along(scaled, "section", -1)
     next_sums = []
     for mask in (NEAR, FAR, FAR | NEAR) if count == 8 else ():

time: 27.9 us -> 27.9 us (level); the launches traced: 27.5 us -> 27.8 us
  Pallas kernels: 4.32 us -> 5.15 us
  starting transfers between devices: 16.7 us -> 16.3 us
    ppermute x2 -> x3, starting transfers between devices: 3.15 us -> 6.11 us  [passed_along(): return lax.ppermute(block, axis, route)]
    ppermute x5, starting transfers between devices: 7.61 us -> 5.44 us  [swapped(): lax.ppermute(block, axis, [(i ^ mask, i) for i in range(lax.axis_size(axi...]
    ppermute x2 -> x3, waiting for transfers between devices: 0.08 us -> 1.32 us  [passed_along(): return lax.ppermute(block, axis, route)]
    ppermute x5 -> x3, starting transfers between devices: 5.96 us -> 4.71 us  [handed_over(): return lax.ppermute(block, ('section', 'tp'), route)]
    ppermute x5, waiting for transfers between devices: 4.12 us -> 3.14 us  [swapped(): lax.ppermute(block, axis, [(i ^ mask, i) for i in range(lax.axis_size(axi...]
    pallas_call x3, Pallas kernels: 1.82 us -> 2.65 us  [the longest x1 2.46 us: load(): pl.pallas_call(load_kernel, out_shape=(pltpu.VMEM(grad.shape, grad.dtype)...]
    ppermute x5 -> x3, waiting for transfers between devices: 2.16 us -> 1.84 us  [handed_over(): return lax.ppermute(block, ('section', 'tp'), route)]
  transfers between devices with their start and end apart: 12 -> 11, of which waited for: 7 -> 8; matrix products, arithmetic and copies ran while one was open for 0% -> 0% of each run, Pallas kernels for 6% -> 11%
where the time goes in v4:
time: 27.9 us; the launch traced here: 27.8 us
  starting transfers between devices  16.3 us (58%)
  waiting for transfers between devices  6.31 us (23%)
  Pallas kernels  5.15 us (18%)
    ppermute x3, starting transfers between devices, passed_along(): return lax.ppermute(block, axis, route)  6.11 us
    ppermute x5, starting transfers between devices, swapped(): lax.ppermute(block, axis, [(i ^ mask, i) for i in range(lax.axis_size(axi...  5.44 us
    ppermute x3, starting transfers between devices, handed_over(): return lax.ppermute(block, ('section', 'tp'), route)  4.71 us
    ppermute x5, waiting for transfers between devices, swapped(): lax.ppermute(block, axis, [(i ^ mask, i) for i in range(lax.axis_size(axi...  3.14 us
    pallas_call x1, Pallas kernels, load(): pl.pallas_call(load_kernel, out_shape=(pltpu.VMEM(grad.shape, grad.dtype)...  2.46 us
    ppermute x3, waiting for transfers between devices, handed_over(): return lax.ppermute(block, ('section', 'tp'), route)  1.84 us
    ppermute x3, waiting for transfers between devices, passed_along(): return lax.ppermute(block, axis, route)  1.32 us
    pallas_call x1, Pallas kernels, finish(): pl.pallas_call(finish_kernel, out_shape=pltpu.HBM(inputs.shape, jnp.bfloa...  1.06 us
  transfers between devices with their start and end apart: 11, of which 8 were waited for; matrix products, arithmetic and copies ran while one was open for 0% of the time, Pallas kernels for 11%

profile of v4, /device:TPU:1, one launch (start us, length us, event | category | flops | bytes accessed | tf_op | source)
XLA Modules:
  0.0 27.8 jit_solution(6678379599585731365)
XLA Ops:
  0.0 2.0 %collective-permute-start = (bf16[128,128]{1,0:T(8,128)(2,1)}, bf16[128,128]{1,0:T(8,128)(2,1)S(1)}, u32[]{:S(2)}, u32[]{:S(2)}) collective-permute-start(bf16[128,128]{1,0:T(8,128)(2,1)} %bitcast.10), channel_id=1, source_target_pairs={{16,0},{24,8},{0,16},{8,24},{17,1},{25,9},{1,17},{9,25},{18,2},{26... | collective-permute-start | bytes 98312 | tf_op jit(solution)/shard_map/ppermute | solution.py:21
  2.0 2.5 %shard_map.73 = (bf16[128,128]{1,0:T(8,128)(2,1)S(1)}, bf16[1536,1024]{1,0:T(8,128)(2,1)S(1)}, bf16[128,128]{1,0:T(8,128)(2,1)S(1)}, bf16[128,128]{1,0:T(8,128)(...) custom-call(bf16[128,128]{1,0:T(8,128)(2,1)} %bitcast.8, ...), custom_call_target="tpu_custom_call" | custom-call | flops 34359738368 | bytes 33554432 | tf_op jit(solution)/shard_map/pallas_call | solution.py:109
  4.5 0.0 collective-permute-done.spare_ref
  4.5 0.2 shard_map.74.own_ref
  4.7 1.3 %collective-permute-start.1 = (bf16[1,128,128]{2,1,0:T(8,128)(2,1)S(1)}, bf16[1,128,128]{2,1,0:T(8,128)(2,1)S(1)}, u32[]{:S(2)}, u32[]{:S(2)}) collective-permute-start(bf16[1,128,128]{2,1,0:T(8,128)(2,1)S(1)} %shard_map.74.own_ref), channel_id=1, source_target_pairs={{1,0},{0,1},{3,2},{2,3},{5,4},{4,5},{7,6},{6,7},{9,8},{8,9},{11,10... | collective-permute-start | bytes 98312 | tf_op jit(solution)/shard_map/ppermute | solution.py:25
  6.0 0.2 collective-permute-start.5
  6.2 1.5 %collective-permute-start.6 = (bf16[128,1536]{1,0:T(8,128)(2,1)S(1)}, bf16[128,1536]{1,0:T(8,128)(2,1)S(1)}, u32[]{:S(2)}, u32[]{:S(2)}) collective-permute-start(bf16[128,1536]{1,0:T(8,128)(2,1)S(1)} %get-tuple-element.20.refs_6_), channel_id=1, source_target_pairs={{8,0},{16,8},{24,16},{0,24},{9,1},{17,9},{25,17},{1,25},{10,2},{18... | collective-permute-start | bytes 1179656 | tf_op jit(solution)/shard_map/ppermute | solution.py:21
  7.8 0.0 collective-permute-done.1.other_ref
  7.8 3.5 %collective-permute-start.2 = (bf16[2,128,128]{2,1,0:T(8,128)(2,1)S(1)}, bf16[2,128,128]{2,1,0:T(8,128)(2,1)S(1)}, u32[]{:S(2)}, u32[]{:S(2)}) collective-permute-start(bf16[2,128,128]{2,1,0:T(8,128)(2,1)S(1)} %shard_map.75.refs_0_), channel_id=1, source_target_pairs={{6,0},{7,1},{4,2},{5,3},{2,4},{3,5},{0,6},{1,7},{14,8},{15,9},{12,... | collective-permute-start | bytes 196616 | tf_op jit(solution)/shard_map/ppermute | solution.py:25
  11.3 0.0 collective-permute-start.4
  11.3 0.4 %collective-permute-start.3 = (bf16[2,128,128]{2,1,0:T(8,128)(2,1)S(1)}, bf16[2,128,128]{2,1,0:T(8,128)(2,1)S(1)}, u32[]{:S(2)}, u32[]{:S(2)}) collective-permute-start(bf16[2,128,128]{2,1,0:T(8,128)(2,1)S(1)} %shard_map.75.refs_0_), channel_id=1, source_target_pairs={{2,0},{3,1},{0,2},{1,3},{6,4},{7,5},{4,6},{5,7},{10,8},{11,9},{8,1... | collective-permute-start | bytes 196616 | tf_op jit(solution)/shard_map/ppermute | solution.py:25
  11.7 1.3 %collective-permute-done.2.refs_1_ = bf16[2,128,128]{2,1,0:T(8,128)(2,1)S(1)} collective-permute-done((bf16[2,128,128]{2,1,0:T(8,128)(2,1)S(1)}, bf16[2,128,128]{2,1,0:T(8,128)(2,1)S(1)}, u32[]{:S(2)}, u32[]{:S(2)}) %collective-permute-start.2) | collective-permute-done | bytes 65568 | tf_op jit(solution)/shard_map/ppermute | solution.py:25
  13.0 0.7 %shard_map.76.refs_4_ = f32[128,1536]{1,0:T(8,128)S(1)} custom-call(bf16[2,128,128]{2,1,0:T(8,128)(2,1)S(1)} %shard_map.75.refs_0_, bf16[2,128,128]{2,1,0:T(8,128)(2,1)S(1)} %collective-permute-done.2.refs_1_, bf16[1536,1024]{1,0:T(8,128)(2,1)S(1)} %get-tuple-element.19.refs_2_.refs_5_), custom_call_target="tpu_custom_call" | custom-call | flops 65536 | bytes 4096 | tf_op jit(solution)/shard_map/pallas_call | solution.py:209
  13.7 0.2 collective-permute-done.5.refs_9_
  13.8 0.9 %collective-permute-done.6.input_ref = bf16[128,1536]{1,0:T(8,128)(2,1)S(1)} collective-permute-done((bf16[128,1536]{1,0:T(8,128)(2,1)S(1)}, bf16[128,1536]{1,0:T(8,128)(2,1)S(1)}, u32[]{:S(2)}, u32[]{:S(2)}) %collective-permute-start.6) | collective-permute-done | bytes 393248 | tf_op jit(solution)/shard_map/ppermute | solution.py:21
  14.8 1.7 %collective-permute-done.4.refs_3_ = bf16[2,128,128]{2,1,0:T(8,128)(2,1)S(1)} collective-permute-done((bf16[2,128,128]{2,1,0:T(8,128)(2,1)S(1)}, bf16[2,128,128]{2,1,0:T(8,128)(2,1)S(1)}, u32[]{:S(2)}, u32[]{:S(2)}) %collective-permute-start.4) | collective-permute-done | bytes 65568 | tf_op jit(solution)/shard_map/ppermute | solution.py:25
  16.4 0.0 collective-permute-done.3.refs_2_
  16.4 0.8 %shard_map.77 = (bf16[128,1664]{1,0:T(8,128)(2,1)S(1)}, f32[2,128]{1,0:T(2,128)S(1)}) custom-call(bf16[2,128,128]{2,1,0:T(8,128)(2,1)S(1)} %shard_map.75.refs_0_, bf16[2,128,128]{2,1,0:T(8,128)(2,1)S(1)} %collective-permute-done.2.refs_1_, bf16[2,128,128]{2,1,0:T(8,128)(2,1)S(1)} %collective-permute-done.3.refs_2_, ...), custom_call_target="tpu_custom_call" | custom-call | flops 34359738368 | bytes 33554432 | tf_op jit(solution)/shard_map/pallas_call | solution.py:252
  17.2 2.6 %collective-permute-start.7 = (bf16[128,1664]{1,0:T(8,128)(2,1)S(1)}, bf16[128,1664]{1,0:T(8,128)(2,1)S(1)}, u32[]{:S(2)}, u32[]{:S(2)}) collective-permute-start(bf16[128,1664]{1,0:T(8,128)(2,1)S(1)} %get-tuple-element.24), channel_id=1, source_target_pairs={{8,0},{16,8},{24,16},{0,24},{9,1},{17,9},{25,17},{1,25},{10,2},{18... | collective-permute-start | bytes 1277960 | tf_op jit(solution)/shard_map/ppermute | solution.py:21
  19.8 1.5 %collective-permute-start.10 = (f32[2,128]{1,0:T(2,128)S(1)}, f32[2,128]{1,0:T(2,128)S(1)}, u32[]{:S(2)}, u32[]{:S(2)}) collective-permute-start(f32[2,128]{1,0:T(2,128)S(1)} %get-tuple-element.26), channel_id=1, source_target_pairs={{14,0},{15,1},{12,2},{13,3},{10,4},{11,5},{8,6},{9,7},{22,8},{23,9... | collective-permute-start | bytes 3080 | tf_op jit(solution)/shard_map/ppermute | solution.py:317
  21.2 1.2 %collective-permute-start.9 = (f32[2,128]{1,0:T(2,128)S(1)}, f32[2,128]{1,0:T(2,128)S(1)}, u32[]{:S(2)}, u32[]{:S(2)}) collective-permute-start(f32[2,128]{1,0:T(2,128)S(1)} %get-tuple-element.26), channel_id=1, source_target_pairs={{12,0},{13,1},{14,2},{15,3},{8,4},{9,5},{10,6},{11,7},{20,8},{21,9... | collective-permute-start | bytes 3080 | tf_op jit(solution)/shard_map/ppermute | solution.py:317
  22.4 2.1 %collective-permute-start.8 = (f32[2,128]{1,0:T(2,128)S(1)}, f32[2,128]{1,0:T(2,128)S(1)}, u32[]{:S(2)}, u32[]{:S(2)}) collective-permute-start(f32[2,128]{1,0:T(2,128)S(1)} %get-tuple-element.26), channel_id=1, source_target_pairs={{10,0},{11,1},{8,2},{9,3},{14,4},{15,5},{12,6},{13,7},{18,8},{19,9... | collective-permute-start | bytes 3080 | tf_op jit(solution)/shard_map/ppermute | solution.py:317
  24.5 1.0 %collective-permute-done.10.refs_2_ = f32[2,128]{1,0:T(2,128)S(1)} collective-permute-done((f32[2,128]{1,0:T(2,128)S(1)}, f32[2,128]{1,0:T(2,128)S(1)}, u32[]{:S(2)}, u32[]{:S(2)}) %collective-permute-start.10) | collective-permute-done | bytes 1056 | tf_op jit(solution)/shard_map/ppermute | solution.py:317
  25.5 0.6 %collective-permute-done.9.refs_1_ = f32[2,128]{1,0:T(2,128)S(1)} collective-permute-done((f32[2,128]{1,0:T(2,128)S(1)}, f32[2,128]{1,0:T(2,128)S(1)}, u32[]{:S(2)}, u32[]{:S(2)}) %collective-permute-start.9) | collective-permute-done | bytes 1056 | tf_op jit(solution)/shard_map/ppermute | solution.py:317
  26.0 0.3 %collective-permute-done.8.refs_0_ = f32[2,128]{1,0:T(2,128)S(1)} collective-permute-done((f32[2,128]{1,0:T(2,128)S(1)}, f32[2,128]{1,0:T(2,128)S(1)}, u32[]{:S(2)}, u32[]{:S(2)}) %collective-permute-start.8) | collective-permute-done | bytes 1056 | tf_op jit(solution)/shard_map/ppermute | solution.py:317
  26.3 0.4 %collective-permute-done.7.scaled_ref = bf16[128,1664]{1,0:T(8,128)(2,1)S(1)} collective-permute-done((bf16[128,1664]{1,0:T(8,128)(2,1)S(1)}, bf16[128,1664]{1,0:T(8,128)(2,1)S(1)}, u32[]{:S(2)}, u32[]{:S(2)}) %collective-permute-start.7) | collective-permute-done | bytes 426016 | tf_op jit(solution)/shard_map/ppermute | solution.py:21
  26.7 1.1 %shard_map.78 = bf16[128,1536]{1,0:T(8,128)(2,1)} custom-call(bf16[128,1664]{1,0:T(8,128)(2,1)S(1)} %collective-permute-done.7.scaled_ref, bf16[128,1536]{1,0:T(8,128)(2,1)S(1)} %collective-permute-done.6.input_ref, f32[2,128]{1,0:T(2,128)S(1)} %collective-permute-done.8.refs_0_, f32[2,128]{1,0:T(2,128)S(1)} %collective-permute-done.9.refs_1_, ...), custom_call_target="tpu_custom_call" | custom-call | tf_op jit(solution)/shard_map/pallas_call | solution.py:293
  (1 shorter events, 0.0 us)
Async XLA Ops:
  0.0 4.5 %collective-permute-start = (bf16[128,128]{1,0:T(8,128)(2,1)}, bf16[128,128]{1,0:T(8,128)(2,1)S(1)}, u32[]{:S(2)}, u32[]{:S(2)}) collective-permute-start(bf16[128,128]{1,0:T(8,128)(2,1)} %bitcast.10), channel_id=1, source_target_pairs={{16,0},{24,8},{0,16},{8,24},{17,1},{25,9},{1,17},{9,25},{18,2},{26... | collective-permute-start | bytes 98312 | tf_op jit(solution)/shard_map/ppermute | solution.py:21
  4.7 3.0 %collective-permute-start.1 = (bf16[1,128,128]{2,1,0:T(8,128)(2,1)S(1)}, bf16[1,128,128]{2,1,0:T(8,128)(2,1)S(1)}, u32[]{:S(2)}, u32[]{:S(2)}) collective-permute-start(bf16[1,128,128]{2,1,0:T(8,128)(2,1)S(1)} %shard_map.74.own_ref), channel_id=1, source_target_pairs={{1,0},{0,1},{3,2},{2,3},{5,4},{4,5},{7,6},{6,7},{9,8},{8,9},{11,10... | collective-permute-start | bytes 98312 | tf_op jit(solution)/shard_map/ppermute | solution.py:25
  6.0 7.8 %collective-permute-start.5 = (bf16[144,1024]{1,0:T(8,128)(2,1)S(1)}, bf16[144,1024]{1,0:T(8,128)(2,1)S(1)}, u32[]{:S(2)}, u32[]{:S(2)}) collective-permute-start(bf16[144,1024]{1,0:T(8,128)(2,1)S(1)} %get-tuple-element.22.refs_8_), channel_id=1, source_target_pairs={{1,0},{0,1},{3,2},{2,3},{5,4},{4,5},{7,6},{6,7},{9,8},{8,9},{11,10... | collective-permute-start | bytes 884744 | tf_op jit(solution)/shard_map/ppermute | solution.py:25
  6.2 8.5 %collective-permute-start.6 = (bf16[128,1536]{1,0:T(8,128)(2,1)S(1)}, bf16[128,1536]{1,0:T(8,128)(2,1)S(1)}, u32[]{:S(2)}, u32[]{:S(2)}) collective-permute-start(bf16[128,1536]{1,0:T(8,128)(2,1)S(1)} %get-tuple-element.20.refs_6_), channel_id=1, source_target_pairs={{8,0},{16,8},{24,16},{0,24},{9,1},{17,9},{25,17},{1,25},{10,2},{18... | collective-permute-start | bytes 1179656 | tf_op jit(solution)/shard_map/ppermute | solution.py:21
  7.8 5.2 %collective-permute-start.2 = (bf16[2,128,128]{2,1,0:T(8,128)(2,1)S(1)}, bf16[2,128,128]{2,1,0:T(8,128)(2,1)S(1)}, u32[]{:S(2)}, u32[]{:S(2)}) collective-permute-start(bf16[2,128,128]{2,1,0:T(8,128)(2,1)S(1)} %shard_map.75.refs_0_), channel_id=1, source_target_pairs={{6,0},{7,1},{4,2},{5,3},{2,4},{3,5},{0,6},{1,7},{14,8},{15,9},{12,... | collective-permute-start | bytes 196616 | tf_op jit(solution)/shard_map/ppermute | solution.py:25
  11.3 5.1 %collective-permute-start.4 = (bf16[2,128,128]{2,1,0:T(8,128)(2,1)S(1)}, bf16[2,128,128]{2,1,0:T(8,128)(2,1)S(1)}, u32[]{:S(2)}, u32[]{:S(2)}) collective-permute-start(bf16[2,128,128]{2,1,0:T(8,128)(2,1)S(1)} %shard_map.75.refs_0_), channel_id=1, source_target_pairs={{4,0},{5,1},{6,2},{7,3},{0,4},{1,5},{2,6},{3,7},{12,8},{13,9},{14,... | collective-permute-start | bytes 196616 | tf_op jit(solution)/shard_map/ppermute | solution.py:25
  11.3 5.1 %collective-permute-start.3 = (bf16[2,128,128]{2,1,0:T(8,128)(2,1)S(1)}, bf16[2,128,128]{2,1,0:T(8,128)(2,1)S(1)}, u32[]{:S(2)}, u32[]{:S(2)}) collective-permute-start(bf16[2,128,128]{2,1,0:T(8,128)(2,1)S(1)} %shard_map.75.refs_0_), channel_id=1, source_target_pairs={{2,0},{3,1},{0,2},{1,3},{6,4},{7,5},{4,6},{5,7},{10,8},{11,9},{8,1... | collective-permute-start | bytes 196616 | tf_op jit(solution)/shard_map/ppermute | solution.py:25
  17.2 9.5 %collective-permute-start.7 = (bf16[128,1664]{1,0:T(8,128)(2,1)S(1)}, bf16[128,1664]{1,0:T(8,128)(2,1)S(1)}, u32[]{:S(2)}, u32[]{:S(2)}) collective-permute-start(bf16[128,1664]{1,0:T(8,128)(2,1)S(1)} %get-tuple-element.24), channel_id=1, source_target_pairs={{8,0},{16,8},{24,16},{0,24},{9,1},{17,9},{25,17},{1,25},{10,2},{18... | collective-permute-start | bytes 1277960 | tf_op jit(solution)/shard_map/ppermute | solution.py:21
  19.8 5.7 %collective-permute-start.10 = (f32[2,128]{1,0:T(2,128)S(1)}, f32[2,128]{1,0:T(2,128)S(1)}, u32[]{:S(2)}, u32[]{:S(2)}) collective-permute-start(f32[2,128]{1,0:T(2,128)S(1)} %get-tuple-element.26), channel_id=1, source_target_pairs={{14,0},{15,1},{12,2},{13,3},{10,4},{11,5},{8,6},{9,7},{22,8},{23,9... | collective-permute-start | bytes 3080 | tf_op jit(solution)/shard_map/ppermute | solution.py:317
  21.2 4.8 %collective-permute-start.9 = (f32[2,128]{1,0:T(2,128)S(1)}, f32[2,128]{1,0:T(2,128)S(1)}, u32[]{:S(2)}, u32[]{:S(2)}) collective-permute-start(f32[2,128]{1,0:T(2,128)S(1)} %get-tuple-element.26), channel_id=1, source_target_pairs={{12,0},{13,1},{14,2},{15,3},{8,4},{9,5},{10,6},{11,7},{20,8},{21,9... | collective-permute-start | bytes 3080 | tf_op jit(solution)/shard_map/ppermute | solution.py:317
  22.4 3.9 %collective-permute-start.8 = (f32[2,128]{1,0:T(2,128)S(1)}, f32[2,128]{1,0:T(2,128)S(1)}, u32[]{:S(2)}, u32[]{:S(2)}) collective-permute-start(f32[2,128]{1,0:T(2,128)S(1)} %get-tuple-element.26), channel_id=1, source_target_pairs={{10,0},{11,1},{8,2},{9,3},{14,4},{15,5},{12,6},{13,7},{18,8},{19,9... | collective-permute-start | bytes 3080 | tf_op jit(solution)/shard_map/ppermute | solution.py:317

commit v5 on v2

--- a/solution.py
+++ b/solution.py
@@ -148,16 +148,19 @@
     return 256 if features % 256 == 0 else features
 
 
-def fill(flat, blocks, head_of, first):
+def block_of(refs, j):
+    return sum((ref[j] for ref in refs[1:]), refs[0][j])
+
+
+def fill(flat, head_of, parts):
     groups = []
-    for ref in blocks:
-        count = ref.shape[0]
+    for kind, refs in parts:
+        count = refs[0].shape[0]
         for j in range(count):
-            start = pl.multiple_of(head_of(first + j) * LANES, LANES)
-            flat[:, pl.ds(start, LANES)] = ref[j]
+            start = pl.multiple_of(head_of(kind, j) * LANES, LANES)
+            flat[:, pl.ds(start, LANES)] = block_of(refs, j)
         width = count * LANES
-        groups.append((pl.multiple_of(head_of(first) // count * width, width), width))
-        first += count
+        groups.append((pl.multiple_of(head_of(kind, 0) // count * width, width), width))
     return groups
 
 
@@ -174,9 +177,8 @@
     return sum(products[1:], products[0])
 
 
-def early_kernel(head_of, *refs):
-    *blocks, weight_ref, out_ref, flat = refs
-    groups = fill(flat, blocks, head_of, 0)
+def early_kernel(head_of, pair_ref, far_ref, weight_ref, out_ref, flat):
+    groups = fill(flat, head_of, [(0, [pair_ref]), (FAR | NEAR, [far_ref])])
     features = weight_ref.shape[0]
     tile = column_tile(features)
     for start in range(0, features, tile):
@@ -197,22 +199,32 @@
     )(*map(in_vmem, (*blocks, weights)))
 
 
-def project_kernel(head_of, sizes, *refs):
-    blocks = refs[: sizes[0]]
-    early_refs = refs[sizes[0] : sizes[0] + sizes[1]]
-    rest = refs[sizes[0] + sizes[1] :]
-    weight_ref, input_ref, gain_ref, *reach_refs, scaled_ref, sums_ref, flat = rest
+def project_kernel(head_of, kinds, late, *refs):
+    blocks, refs = refs[: len(kinds)], refs[len(kinds) :]
+    weight_ref, input_ref, gain_ref, *rest, scaled_ref, sums_ref, flat = refs
+    early_refs, reach_refs = (rest[:1], rest[1:]) if late else ([], rest)
     tokens, features = input_ref.shape
-    groups = fill(flat, blocks, head_of, 0)
-    if early_refs:
-        groups = groups[EARLY:]
-    tile = column_tile(features)
-    for start in range(0, features, tile):
-        part = pl.ds(start, tile)
-        grad_normed = times_weights(flat, groups, weight_ref, part)
-        for ref in early_refs:
-            grad_normed = grad_normed + ref[:, part]
-        scaled_ref[:, part] = (grad_normed * gain_ref[:, part]).astype(scaled_ref.dtype)
+    parts = {}
+    for kind, ref in zip(kinds, blocks):
+        parts.setdefault(kind, []).append(ref)
+    kept = list(parts)
+    groups = dict(zip(kept, fill(flat, head_of, [(kind, parts[kind]) for kind in kept])))
+
+    def scale(chosen):
+        tile = column_tile(features)
+        for start in range(0, features, tile):
+            part = pl.ds(start, tile)
+            grad_normed = times_weights(flat, chosen, weight_ref, part)
+            for ref in early_refs:
+                grad_normed = grad_normed + ref[:, part]
+            scaled_ref[:, part] = (grad_normed * gain_ref[:, part]).astype(scaled_ref.dtype)
+
+    if late:
+        upper = head_of(0, 0) // FAR
+        pl.when(upper == 1)(lambda: scale([groups[NEAR], groups[FAR]]))
+        pl.when(upper == 0)(lambda: scale([groups[NEAR], groups[FAR], groups[FAR | NEAR]]))
+    else:
+        scale(list(groups.values()))
     reach = sum(ref[:tokens, :].astype(jnp.float32) for ref in reach_refs)
     squares = sum(ref[tokens:, :tokens].astype(jnp.float32) for ref in reach_refs)
     squares = jnp.sum(squares, axis=0, keepdims=True)
@@ -226,11 +238,11 @@
     scaled_ref[:, features:] = extra.astype(scaled_ref.dtype)
 
 
-def project(head_of, blocks, early, weights, inputs, gain, reaches):
+def project(head_of, kinds, blocks, early, weights, inputs, gain, reaches):
     tokens, features = inputs.shape
-    operands = (*blocks, *early, weights, inputs, gain, *reaches)
-    return pl.pallas_call(
-        functools.partial(project_kernel, head_of, (len(blocks), len(early))),
+    operands = (*blocks, weights, inputs, gain, *early, *reaches)
+    return pl.pallas_call(
+        functools.partial(project_kernel, head_of, kinds, bool(early)),
         out_shape=(
             pltpu.VMEM((tokens, features + LANES), jnp.bfloat16),
             pltpu.VMEM((2, tokens), jnp.float32),
@@ -284,29 +296,32 @@
 
 
 FAR, NEAR, SIDE = 4, 2, 1
-LINE = (FAR | NEAR, NEAR, FAR)
-EARLY = 2
-
-
-def handed_over(block, sections, count, distance, mask):
+LOWER, UPPER = (0,), (1,)
+
+
+def handed_over(block, sections, count, distance, mask, halves=LOWER + UPPER):
     route = [
         ((s - distance) % sections * count + (i ^ mask), s * count + i)
         for s in range(sections)
         for i in range(count)
+        if count != 8 or i // FAR in halves
     ]
     return lax.ppermute(block, ("section", "tp"), route)
 
 
-def gathered(pair, axis):
-    if lax.axis_size(axis) != 8:
-        return [lax.all_gather(pair[0], axis)], lambda place: place
-    blocks = [pair] + [swapped(pair, axis, mask) for mask in LINE]
-    masks = [far | side for far in (0, *LINE) for side in (0, SIDE)]
-
-    def head_of(place):
-        return lax.axis_index(axis) ^ masks[place]
-
-    return blocks, head_of
+def gathered(pair, next_input, sections, count):
+    if count != 8:
+        return (0,), [lax.all_gather(pair[0], "tp")], lambda kind, j: j, next_input
+    wanted = ((FAR | NEAR, LOWER), (FAR, LOWER + UPPER), (FAR | NEAR, UPPER))
+    blocks = [handed_over(pair, sections, count, 0, mask, halves) for mask, halves in wanted]
+    late, next_input = lax.optimization_barrier((pair, next_input))
+    near = handed_over(late, sections, count, 0, NEAR)
+    kinds = (0, FAR | NEAR, NEAR, FAR, FAR | NEAR)
+
+    def head_of(kind, j):
+        return lax.axis_index("tp") ^ kind ^ (j * SIDE)
+
+    return kinds, [pair, blocks[2], near, blocks[1], blocks[0]], head_of, next_input
 
 
 def per_device(grad_attn, w_value, probs_own, probs_spare, evicted, layer_input, gain):
@@ -321,17 +336,24 @@
     reach = reach_of(weights, inputs, gain, heads[-1][0])
     if count == 8:
         reaches = [reach, swapped(reach, "tp", SIDE)]
-        reaches[1], next_input = lax.optimization_barrier((reaches[1], next_input))
     else:
         reaches = [lax.psum(reach, "tp")]
     pair = value_gradients(taken, heads)
-    blocks, head_of = gathered(pair, "tp")
-    early = [project_early(head_of, blocks[:EARLY], weights)] if count == 8 else []
-    scaled, sums = project(head_of, blocks, early, weights, inputs, gain, reaches)
+    kinds, blocks, head_of, next_input = gathered(pair, next_input, sections, count)
+    early = [project_early(head_of, blocks[:2], weights)] if count == 8 else []
+    scaled, sums = project(head_of, kinds, blocks, early, weights, inputs, gain, reaches)
     next_scaled = passed_along(scaled, "section", -1)
-    next_sums = []
-    for mask in (NEAR, FAR, FAR | NEAR) if count == 8 else ():
-        next_sums.append(handed_over(sums, sections, count, -1, mask))
+    hops = (
+        (FAR | NEAR, UPPER),
+        (FAR, LOWER + UPPER),
+        (NEAR, LOWER + UPPER),
+        (FAR | NEAR, LOWER),
+    )
+    next_sums = [
+        handed_over(sums, sections, count, -1, mask, halves)
+        for mask, halves in hops
+        if count == 8
+    ]
     return finish(next_scaled, next_input, next_sums)[None]
 
 

time: 27.9 us -> 33.9 us (1.22)
  the two profiles are of different devices: /device:TPU:1 before, /device:TPU:0 now
where the time goes in v5:
time: 33.9 us; the launch traced here: 33.7 us
  starting transfers between devices  23.5 us (69%)
  waiting for transfers between devices  5.17 us (15%)
  Pallas kernels  4.88 us (14%)
    ppermute x10, starting transfers between devices, handed_over(): return lax.ppermute(block, ('section', 'tp'), route)  17.7 us
    ppermute x2, starting transfers between devices, swapped(): lax.ppermute(block, axis, [(i ^ mask, i) for i in range(lax.axis_size(axi...  5.3 us
    ppermute x10, waiting for transfers between devices, handed_over(): return lax.ppermute(block, ('section', 'tp'), route)  4.98 us
    pallas_call x1, Pallas kernels, project(): pl.pallas_call(functools.partial(project_kernel, head_of, kinds, bool(ear...  1.32 us
    pallas_call x1, Pallas kernels, finish(): pl.pallas_call(finish_kernel, out_shape=pltpu.HBM(inputs.shape, jnp.bfloa...  1.06 us
    pallas_call x1, Pallas kernels, pack(): pl.pallas_call(pack_kernel, out_shape=(pltpu.VMEM((2, *own.shape), own.dt...  0.97 us
  transfers between devices with their start and end apart: 14, of which 5 were waited for; matrix products, arithmetic and copies ran while one was open for 0% of the time, Pallas kernels for 5%

profile of v5, /device:TPU:0, one launch (start us, length us, event | category | flops | bytes accessed | tf_op | source)
XLA Modules:
  0.0 33.7 jit_solution(1969124860608279216)
XLA Ops:
  0.0 0.0 copy-start.1
  0.0 0.0 copy-start
  0.0 0.0 copy-start.2
  0.0 1.0 %shard_map.73 = (bf16[2,128,128]{2,1,0:T(8,128)(2,1)S(1)}, bf16[128,128]{1,0:T(8,128)(2,1)S(1)}, bf16[128,128]{1,0:T(8,128)(2,1)S(1)}) custom-call(bf16[128,128]{1,0:T(8,128)(2,1)} %bitcast.12, bf16[128,128]{1,0:T(8,128)(2,1)} %bitcast.13, bf16[128,128]{1,0:T(8,128)(2,1)} %bitcast.14, s32[1,4]{1,0:T(1,128)} %evicted_ref.1), custom_call_target="tpu_custom_call" | custom-call | flops 34359738368 | bytes 33554432 | tf_op jit(solution)/shard_map/pallas_call | solution.py:82
  1.0 3.0 %collective-permute-start.2 = (bf16[2,128,128]{2,1,0:T(8,128)(2,1)S(1)}, bf16[2,128,128]{2,1,0:T(8,128)(2,1)S(1)}, u32[]{:S(2)}, u32[]{:S(2)}) collective-permute-start(bf16[2,128,128]{2,1,0:T(8,128)(2,1)S(1)} %get-tuple-element.14.refs_3_), channel_id=1, source_target_pairs={{1,0},{0,1},{3,2},{2,3},{5,4},{4,5},{7,6},{6,7},{9,8},{8,9},{11,10... | collective-permute-start | bytes 196616 | tf_op jit(solution)/shard_map/ppermute | solution.py:24
  4.0 1.4 %collective-permute-start.1 = (bf16[128,128]{1,0:T(8,128)(2,1)S(1)}, bf16[128,128]{1,0:T(8,128)(2,1)S(1)}, u32[]{:S(2)}, u32[]{:S(2)}) collective-permute-start(bf16[128,128]{1,0:T(8,128)(2,1)S(1)} %get-tuple-element.13), channel_id=1, source_target_pairs={{17,0},{16,1},{19,2},{18,3},{21,4},{20,5},{23,6},{22,7},{25,8},{24... | collective-permute-start | bytes 98312 | tf_op jit(solution)/shard_map/ppermute | solution.py:309
  5.5 0.1 collective-permute-start
  5.6 0.0 copy-done.1
  5.6 0.5 %collective-permute-start.4 = (bf16[128,1536]{1,0:T(8,128)(2,1)S(1)}, bf16[128,1536]{1,0:T(8,128)(2,1)S(1)}, u32[]{:S(2)}, u32[]{:S(2)}) collective-permute-start(bf16[128,1536]{1,0:T(8,128)(2,1)S(1)} %bitcast.9), channel_id=1, source_target_pairs={{8,0},{16,8},{24,16},{0,24},{9,1},{17,9},{25,17},{1,25},{10,2},{18... | collective-permute-start | bytes 1179656 | tf_op jit(solution)/shard_map/ppermute | solution.py:20
  6.1 0.2 collective-permute-done.2.refs_2_.first_ref
  6.3 0.0 copy-done
  6.3 0.0 copy-done.2
  6.3 0.7 %shard_map.76.refs_9_ = bf16[144,1024]{1,0:T(8,128)(2,1)S(1)} custom-call(bf16[1536,1024]{1,0:T(8,128)(2,1)S(1)} %bitcast.6, bf16[128,1536]{1,0:T(8,128)(2,1)S(1)} %bitcast.10, f32[1,1536]{1,0:T(1,128)S(1)} %copy-done.2, bf16[2,128,128]{2,1,0:T(8,128)(2,1)S(1)} %collective-permute-done.2.refs_2_.first_ref), custom_call_target="tpu_custom_call" | custom-call | flops 34359738368 | bytes 33554432 | tf_op jit(solution)/shard_map/pallas_call | solution.py:113
  6.9 2.3 %collective-permute-start.8 = (bf16[144,1024]{1,0:T(8,128)(2,1)S(1)}, bf16[144,1024]{1,0:T(8,128)(2,1)S(1)}, u32[]{:S(2)}, u32[]{:S(2)}) collective-permute-start(bf16[144,1024]{1,0:T(8,128)(2,1)S(1)} %shard_map.76.refs_9_), channel_id=1, source_target_pairs={{1,0},{0,1},{3,2},{2,3},{5,4},{4,5},{7,6},{6,7},{9,8},{8,9},{11,10... | collective-permute-start | bytes 884744 | tf_op jit(solution)/shard_map/ppermute | solution.py:24
  9.2 0.0 collective-permute-done.1.refs_1_
  9.2 0.2 collective-permute-done.refs_0_
  9.4 0.2 shard_map.74.pair_ref.refs_0_
  9.6 1.3 %collective-permute-start.7 = (bf16[2,128,128]{2,1,0:T(8,128)(2,1)S(1)}, bf16[2,128,128]{2,1,0:T(8,128)(2,1)S(1)}, u32[]{:S(2)}, u32[]{:S(2)}) collective-permute-start(bf16[2,128,128]{2,1,0:T(8,128)(2,1)S(1)} %shard_map.74.pair_ref.refs_0_), channel_id=1, source_target_pairs={{6,0},{7,1},{4,2},{5,3},{14,8},{15,9},{12,10},{13,11},{22,16},{23,... | collective-permute-start | bytes 196616 | tf_op jit(solution)/shard_map/ppermute | solution.py:309
  10.9 3.7 %collective-permute-start.6 = (bf16[2,128,128]{2,1,0:T(8,128)(2,1)S(1)}, bf16[2,128,128]{2,1,0:T(8,128)(2,1)S(1)}, u32[]{:S(2)}, u32[]{:S(2)}) collective-permute-start(bf16[2,128,128]{2,1,0:T(8,128)(2,1)S(1)} %shard_map.74.pair_ref.refs_0_), channel_id=1, source_target_pairs={{4,0},{5,1},{6,2},{7,3},{0,4},{1,5},{2,6},{3,7},{12,8},{13,9},{14,... | collective-permute-start | bytes 196616 | tf_op jit(solution)/shard_map/ppermute | solution.py:309
  14.6 2.7 %collective-permute-start.3 = (bf16[2,128,128]{2,1,0:T(8,128)(2,1)S(1)}, bf16[2,128,128]{2,1,0:T(8,128)(2,1)S(1)}, u32[]{:S(2)}, u32[]{:S(2)}) collective-permute-start(bf16[2,128,128]{2,1,0:T(8,128)(2,1)S(1)} %shard_map.74.pair_ref.refs_0_), channel_id=1, source_target_pairs={{2,4},{3,5},{0,6},{1,7},{10,12},{11,13},{8,14},{9,15},{18,20},{19,... | collective-permute-start | bytes 196616 | tf_op jit(solution)/shard_map/ppermute | solution.py:309
  17.3 0.0 collective-permute-done.4.input_ref
  17.3 0.1 collective-permute-start.5
  17.4 1.8 %collective-permute-done.3.far_ref.refs_1_ = bf16[2,128,128]{2,1,0:T(8,128)(2,1)S(1)} collective-permute-done((bf16[2,128,128]{2,1,0:T(8,128)(2,1)S(1)}, bf16[2,128,128]{2,1,0:T(8,128)(2,1)S(1)}, u32[]{:S(2)}, u32[]{:S(2)}) %collective-permute-start.3) | collective-permute-done | bytes 65568 | tf_op jit(solution)/shard_map/ppermute | solution.py:309
  19.2 0.7 %shard_map.75.refs_8_ = f32[128,1536]{1,0:T(8,128)S(1)} custom-call(bf16[2,128,128]{2,1,0:T(8,128)(2,1)S(1)} %shard_map.74.pair_ref.refs_0_, bf16[2,128,128]{2,1,0:T(8,128)(2,1)S(1)} %collective-permute-done.3.far_ref.refs_1_, bf16[1536,1024]{1,0:T(8,128)(2,1)S(1)} %bitcast.7), custom_call_target="tpu_custom_call" | custom-call | flops 65536 | bytes 4096 | tf_op jit(solution)/shard_map/pallas_call | solution.py:191
  19.9 0.0 collective-permute-done.7.refs_4_
  19.9 0.0 collective-permute-done.6.refs_3_
  19.9 0.0 collective-permute-done.8.refs_10_
  19.9 1.7 %collective-permute-done.5.refs_2_ = bf16[2,128,128]{2,1,0:T(8,128)(2,1)S(1)} collective-permute-done((bf16[2,128,128]{2,1,0:T(8,128)(2,1)S(1)}, bf16[2,128,128]{2,1,0:T(8,128)(2,1)S(1)}, u32[]{:S(2)}, u32[]{:S(2)}) %collective-permute-start.5) | collective-permute-done | bytes 65568 | tf_op jit(solution)/shard_map/ppermute | solution.py:309
  21.6 1.3 %shard_map.77 = (bf16[128,1664]{1,0:T(8,128)(2,1)S(1)}, f32[2,128]{1,0:T(2,128)S(1)}) custom-call(bf16[2,128,128]{2,1,0:T(8,128)(2,1)S(1)} %shard_map.74.pair_ref.refs_0_, bf16[2,128,128]{2,1,0:T(8,128)(2,1)S(1)} %collective-permute-done.3.far_ref.refs_1_, bf16[2,128,128]{2,1,0:T(8,128)(2,1)S(1)} %collective-permute-done.5.refs_2_, ...), custom_call_target="tpu_custom_call" | custom-call | flops 34359738368 | bytes 33554432 | tf_op jit(solution)/shard_map/pallas_call | solution.py:244
  23.0 0.0 collective-permute-start.9
  23.0 1.3 %collective-permute-start.13 = (f32[2,128]{1,0:T(2,128)S(1)}, f32[2,128]{1,0:T(2,128)S(1)}, u32[]{:S(2)}, u32[]{:S(2)}) collective-permute-start(f32[2,128]{1,0:T(2,128)S(1)} %get-tuple-element.18), channel_id=1, source_target_pairs={{14,0},{15,1},{12,2},{13,3},{22,8},{23,9},{20,10},{21,11},{30,16},... | collective-permute-start | bytes 3080 | tf_op jit(solution)/shard_map/ppermute | solution.py:309
  24.3 1.6 %collective-permute-start.12 = (f32[2,128]{1,0:T(2,128)S(1)}, f32[2,128]{1,0:T(2,128)S(1)}, u32[]{:S(2)}, u32[]{:S(2)}) collective-permute-start(f32[2,128]{1,0:T(2,128)S(1)} %get-tuple-element.18), channel_id=1, source_target_pairs={{10,0},{11,1},{8,2},{9,3},{14,4},{15,5},{12,6},{13,7},{18,8},{19,9... | collective-permute-start | bytes 3080 | tf_op jit(solution)/shard_map/ppermute | solution.py:309
  25.9 4.1 %collective-permute-start.11 = (f32[2,128]{1,0:T(2,128)S(1)}, f32[2,128]{1,0:T(2,128)S(1)}, u32[]{:S(2)}, u32[]{:S(2)}) collective-permute-start(f32[2,128]{1,0:T(2,128)S(1)} %get-tuple-element.18), channel_id=1, source_target_pairs={{12,0},{13,1},{14,2},{15,3},{8,4},{9,5},{10,6},{11,7},{20,8},{21,9... | collective-permute-start | bytes 3080 | tf_op jit(solution)/shard_map/ppermute | solution.py:309
  30.0 1.3 %collective-permute-start.10 = (f32[2,128]{1,0:T(2,128)S(1)}, f32[2,128]{1,0:T(2,128)S(1)}, u32[]{:S(2)}, u32[]{:S(2)}) collective-permute-start(f32[2,128]{1,0:T(2,128)S(1)} %get-tuple-element.18), channel_id=1, source_target_pairs={{10,4},{11,5},{8,6},{9,7},{18,12},{19,13},{16,14},{17,15},{26,20},... | collective-permute-start | bytes 3080 | tf_op jit(solution)/shard_map/ppermute | solution.py:309
  31.4 0.0 collective-permute-done.13.refs_3_
  31.4 0.0 collective-permute-done.12.refs_2_
  31.4 0.0 collective-permute-done.11.refs_1_
  31.4 1.2 %collective-permute-done.10.refs_0_ = f32[2,128]{1,0:T(2,128)S(1)} collective-permute-done((f32[2,128]{1,0:T(2,128)S(1)}, f32[2,128]{1,0:T(2,128)S(1)}, u32[]{:S(2)}, u32[]{:S(2)}) %collective-permute-start.10) | collective-permute-done | bytes 1056 | tf_op jit(solution)/shard_map/ppermute | solution.py:309
  32.7 0.0 collective-permute-done.9.scaled_ref
  32.7 1.1 %shard_map.78 = bf16[128,1536]{1,0:T(8,128)(2,1)} custom-call(bf16[128,1664]{1,0:T(8,128)(2,1)S(1)} %collective-permute-done.9.scaled_ref, bf16[128,1536]{1,0:T(8,128)(2,1)S(1)} %collective-permute-done.4.input_ref, f32[2,128]{1,0:T(2,128)S(1)} %collective-permute-done.10.refs_0_, f32[2,128]{1,0:T(2,128)S(1)} %collective-permute-done.11.refs_1_, ...), custom_call_target="tpu_custom_call" | custom-call | tf_op jit(solution)/shard_map/pallas_call | solution.py:285
Async XLA Ops:
  0.0 5.6 %copy-start.1 = (bf16[1,128,1536]{2,1,0:T(8,128)(2,1)S(1)}, bf16[1,128,1536]{2,1,0:T(8,128)(2,1)}, u32[]{:S(2)}) copy-start(bf16[1,128,1536]{2,1,0:T(8,128)(2,1)} %param.12) | copy-start | bytes 1179652
  0.0 6.3 %copy-start = (bf16[1,1536,1024]{2,1,0:T(8,128)(2,1)S(1)}, bf16[1,1536,1024]{2,1,0:T(8,128)(2,1)}, u32[]{:S(2)}) copy-start(bf16[1,1536,1024]{2,1,0:T(8,128)(2,1)} %param.8) | copy-start | bytes 9437188
  0.0 6.3 %copy-start.2 = (f32[1,1536]{1,0:T(1,128)S(1)}, f32[1,1536]{1,0:T(1,128)}, u32[]{:S(2)}) copy-start(f32[1,1536]{1,0:T(1,128)} %refs_7_.1) | copy-start | bytes 18436
  1.0 5.3 %collective-permute-start.2 = (bf16[2,128,128]{2,1,0:T(8,128)(2,1)S(1)}, bf16[2,128,128]{2,1,0:T(8,128)(2,1)S(1)}, u32[]{:S(2)}, u32[]{:S(2)}) collective-permute-start(bf16[2,128,128]{2,1,0:T(8,128)(2,1)S(1)} %get-tuple-element.14.refs_3_), channel_id=1, source_target_pairs={{1,0},{0,1},{3,2},{2,3},{5,4},{4,5},{7,6},{6,7},{9,8},{8,9},{11,10... | collective-permute-start | bytes 196616 | tf_op jit(solution)/shard_map/ppermute | solution.py:24
  4.0 5.2 %collective-permute-start.1 = (bf16[128,128]{1,0:T(8,128)(2,1)S(1)}, bf16[128,128]{1,0:T(8,128)(2,1)S(1)}, u32[]{:S(2)}, u32[]{:S(2)}) collective-permute-start(bf16[128,128]{1,0:T(8,128)(2,1)S(1)} %get-tuple-element.13), channel_id=1, source_target_pairs={{17,0},{16,1},{19,2},{18,3},{21,4},{20,5},{23,6},{22,7},{25,8},{24... | collective-permute-start | bytes 98312 | tf_op jit(solution)/shard_map/ppermute | solution.py:309
  5.5 3.9 %collective-permute-start = (bf16[128,128]{1,0:T(8,128)(2,1)S(1)}, bf16[128,128]{1,0:T(8,128)(2,1)S(1)}, u32[]{:S(2)}, u32[]{:S(2)}) collective-permute-start(bf16[128,128]{1,0:T(8,128)(2,1)S(1)} %get-tuple-element.13), channel_id=1, source_target_pairs={{16,0},{17,1},{18,2},{19,3},{20,4},{21,5},{22,6},{23,7},{24,8},{25... | collective-permute-start | bytes 98312 | tf_op jit(solution)/shard_map/ppermute | solution.py:309
  5.6 11.7 %collective-permute-start.4 = (bf16[128,1536]{1,0:T(8,128)(2,1)S(1)}, bf16[128,1536]{1,0:T(8,128)(2,1)S(1)}, u32[]{:S(2)}, u32[]{:S(2)}) collective-permute-start(bf16[128,1536]{1,0:T(8,128)(2,1)S(1)} %bitcast.9), channel_id=1, source_target_pairs={{8,0},{16,8},{24,16},{0,24},{9,1},{17,9},{25,17},{1,25},{10,2},{18... | collective-permute-start | bytes 1179656 | tf_op jit(solution)/shard_map/ppermute | solution.py:20
  6.9 13.0 %collective-permute-start.8 = (bf16[144,1024]{1,0:T(8,128)(2,1)S(1)}, bf16[144,1024]{1,0:T(8,128)(2,1)S(1)}, u32[]{:S(2)}, u32[]{:S(2)}) collective-permute-start(bf16[144,1024]{1,0:T(8,128)(2,1)S(1)} %shard_map.76.refs_9_), channel_id=1, source_target_pairs={{1,0},{0,1},{3,2},{2,3},{5,4},{4,5},{7,6},{6,7},{9,8},{8,9},{11,10... | collective-permute-start | bytes 884744 | tf_op jit(solution)/shard_map/ppermute | solution.py:24
  9.6 10.3 %collective-permute-start.7 = (bf16[2,128,128]{2,1,0:T(8,128)(2,1)S(1)}, bf16[2,128,128]{2,1,0:T(8,128)(2,1)S(1)}, u32[]{:S(2)}, u32[]{:S(2)}) collective-permute-start(bf16[2,128,128]{2,1,0:T(8,128)(2,1)S(1)} %shard_map.74.pair_ref.refs_0_), channel_id=1, source_target_pairs={{6,0},{7,1},{4,2},{5,3},{14,8},{15,9},{12,10},{13,11},{22,16},{23,... | collective-permute-start | bytes 196616 | tf_op jit(solution)/shard_map/ppermute | solution.py:309
  10.9 9.0 %collective-permute-start.6 = (bf16[2,128,128]{2,1,0:T(8,128)(2,1)S(1)}, bf16[2,128,128]{2,1,0:T(8,128)(2,1)S(1)}, u32[]{:S(2)}, u32[]{:S(2)}) collective-permute-start(bf16[2,128,128]{2,1,0:T(8,128)(2,1)S(1)} %shard_map.74.pair_ref.refs_0_), channel_id=1, source_target_pairs={{4,0},{5,1},{6,2},{7,3},{0,4},{1,5},{2,6},{3,7},{12,8},{13,9},{14,... | collective-permute-start | bytes 196616 | tf_op jit(solution)/shard_map/ppermute | solution.py:309
  14.6 4.6 %collective-permute-start.3 = (bf16[2,128,128]{2,1,0:T(8,128)(2,1)S(1)}, bf16[2,128,128]{2,1,0:T(8,128)(2,1)S(1)}, u32[]{:S(2)}, u32[]{:S(2)}) collective-permute-start(bf16[2,128,128]{2,1,0:T(8,128)(2,1)S(1)} %shard_map.74.pair_ref.refs_0_), channel_id=1, source_target_pairs={{2,4},{3,5},{0,6},{1,7},{10,12},{11,13},{8,14},{9,15},{18,20},{19,... | collective-permute-start | bytes 196616 | tf_op jit(solution)/shard_map/ppermute | solution.py:309
  17.3 4.3 %collective-permute-start.5 = (bf16[2,128,128]{2,1,0:T(8,128)(2,1)S(1)}, bf16[2,128,128]{2,1,0:T(8,128)(2,1)S(1)}, u32[]{:S(2)}, u32[]{:S(2)}) collective-permute-start(bf16[2,128,128]{2,1,0:T(8,128)(2,1)S(1)} %shard_map.74.pair_ref.refs_0_), channel_id=1, source_target_pairs={{2,0},{3,1},{0,2},{1,3},{6,4},{7,5},{4,6},{5,7},{10,8},{11,9},{8,1... | collective-permute-start | bytes 196616 | tf_op jit(solution)/shard_map/ppermute | solution.py:309
  23.0 9.7 %collective-permute-start.9 = (bf16[128,1664]{1,0:T(8,128)(2,1)S(1)}, bf16[128,1664]{1,0:T(8,128)(2,1)S(1)}, u32[]{:S(2)}, u32[]{:S(2)}) collective-permute-start(bf16[128,1664]{1,0:T(8,128)(2,1)S(1)} %get-tuple-element.16), channel_id=1, source_target_pairs={{8,0},{16,8},{24,16},{0,24},{9,1},{17,9},{25,17},{1,25},{10,2},{18... | collective-permute-start | bytes 1277960 | tf_op jit(solution)/shard_map/ppermute | solution.py:20
  23.0 8.4 %collective-permute-start.13 = (f32[2,128]{1,0:T(2,128)S(1)}, f32[2,128]{1,0:T(2,128)S(1)}, u32[]{:S(2)}, u32[]{:S(2)}) collective-permute-start(f32[2,128]{1,0:T(2,128)S(1)} %get-tuple-element.18), channel_id=1, source_target_pairs={{14,0},{15,1},{12,2},{13,3},{22,8},{23,9},{20,10},{21,11},{30,16},... | collective-permute-start | bytes 3080 | tf_op jit(solution)/shard_map/ppermute | solution.py:309
  24.3 7.1 %collective-permute-start.12 = (f32[2,128]{1,0:T(2,128)S(1)}, f32[2,128]{1,0:T(2,128)S(1)}, u32[]{:S(2)}, u32[]{:S(2)}) collective-permute-start(f32[2,128]{1,0:T(2,128)S(1)} %get-tuple-element.18), channel_id=1, source_target_pairs={{10,0},{11,1},{8,2},{9,3},{14,4},{15,5},{12,6},{13,7},{18,8},{19,9... | collective-permute-start | bytes 3080 | tf_op jit(solution)/shard_map/ppermute | solution.py:309
  25.9 5.5 %collective-permute-start.11 = (f32[2,128]{1,0:T(2,128)S(1)}, f32[2,128]{1,0:T(2,128)S(1)}, u32[]{:S(2)}, u32[]{:S(2)}) collective-permute-start(f32[2,128]{1,0:T(2,128)S(1)} %get-tuple-element.18), channel_id=1, source_target_pairs={{12,0},{13,1},{14,2},{15,3},{8,4},{9,5},{10,6},{11,7},{20,8},{21,9... | collective-permute-start | bytes 3080 | tf_op jit(solution)/shard_map/ppermute | solution.py:309
  30.0 2.6 %collective-permute-start.10 = (f32[2,128]{1,0:T(2,128)S(1)}, f32[2,128]{1,0:T(2,128)S(1)}, u32[]{:S(2)}, u32[]{:S(2)}) collective-permute-start(f32[2,128]{1,0:T(2,128)S(1)} %get-tuple-element.18), channel_id=1, source_target_pairs={{10,4},{11,5},{8,6},{9,7},{18,12},{19,13},{16,14},{17,15},{26,20},... | collective-permute-start | bytes 3080 | tf_op jit(solution)/shard_map/ppermute | solution.py:309

commit v6 on v2

--- a/solution.py
+++ b/solution.py
@@ -9,7 +9,7 @@
 
 D = 12288
 LANES = 128
-PIECES = 4
+PIECES = (0, 3, 5, 7, 8)
 EXTRA = 16
 HIDES = pl.CostEstimate(flops=1 << 35, bytes_accessed=1 << 25, transcendentals=0)
 
@@ -40,8 +40,9 @@
     return jnp.broadcast_to(column, (column.shape[0], column.shape[0])).T[:1]
 
 
-def as_column(row):
-    return jnp.broadcast_to(row, (row.shape[1], row.shape[1])).T[:, :1]
+def standing(rows):
+    tokens = rows.shape[1]
+    return jnp.concatenate([rows, jnp.zeros((tokens - rows.shape[0], tokens), rows.dtype)]).T
 
 
 def split(values):
@@ -217,13 +218,11 @@
     squares = sum(ref[tokens:, :tokens].astype(jnp.float32) for ref in reach_refs)
     squares = jnp.sum(squares, axis=0, keepdims=True)
     inner = jnp.sum(flat[...].astype(jnp.float32) * reach, axis=1, keepdims=True)
+    inner = as_row(inner)
     sums_ref[:1, :] = squares
-    sums_ref[1:, :] = as_row(inner)
-    lane = lax.broadcasted_iota(jnp.int32, (tokens, LANES), 1)
-    extra = jnp.zeros((tokens, LANES), jnp.float32)
-    for j, part in enumerate(split(as_column(squares)) + split(inner)):
-        extra = jnp.where(lane == j, part, extra)
-    scaled_ref[:, features:] = extra.astype(scaled_ref.dtype)
+    sums_ref[1:, :] = inner
+    rows = jnp.concatenate([*split(squares), *split(inner), jnp.zeros((2, tokens), jnp.float32)])
+    scaled_ref[:, features:] = standing(rows).astype(scaled_ref.dtype)
 
 
 def project(head_of, blocks, early, weights, inputs, gain, reaches):
@@ -246,20 +245,20 @@
 def finish_kernel(scaled_ref, input_ref, *refs):
     *sums_refs, out_ref, held, sems = refs
     tokens, features = input_ref.shape
-    extra = scaled_ref[:, features:].astype(jnp.float32)
-    lane = lax.broadcasted_iota(jnp.int32, extra.shape, 1)
-    squares = jnp.sum(jnp.where(lane < 3, extra, 0.0), axis=1, keepdims=True)
-    inner = jnp.sum(jnp.where(lane < 3, 0.0, extra), axis=1, keepdims=True)
-    if sums_refs:
-        sums = sum(ref[...] for ref in sums_refs)
-        squares = squares + as_column(sums[:1])
-        inner = inner + as_column(sums[1:])
+    extra = scaled_ref[:, features:].astype(jnp.float32).T
+    squares = extra[0:1] + extra[1:2] + extra[2:3]
+    inner = extra[3:4] + extra[4:5] + extra[5:6]
+    for ref in sums_refs:
+        squares = squares + ref[:1, :]
+        inner = inner + ref[1:, :]
     inv = 1.0 / jnp.sqrt(squares / D + 1e-05)
     factor = inner * (inv * inv * inv) / D
-    rows = tokens // PIECES
+    rows = jnp.concatenate([inv, factor, jnp.zeros((6, tokens), jnp.float32)])
+    columns = standing(rows)
+    inv, factor = columns[:, 0:1], columns[:, 1:2]
     copies = []
-    for j in range(PIECES):
-        part = slice(j * rows, (j + 1) * rows)
+    for j in range(len(PIECES) - 1):
+        part = slice(PIECES[j] * tokens // 8, PIECES[j + 1] * tokens // 8)
         scaled = scaled_ref[part, :features].astype(jnp.float32)
         values = input_ref[part, :].astype(jnp.float32)
         held[part, :] = (scaled * inv[part] - values * factor[part]).astype(held.dtype)
@@ -277,7 +276,7 @@
         out_specs=pl.BlockSpec(memory_space=pltpu.HBM),
         scratch_shapes=[
             pltpu.VMEM(inputs.shape, jnp.bfloat16),
-            pltpu.SemaphoreType.DMA((PIECES,)),
+            pltpu.SemaphoreType.DMA((len(PIECES) - 1,)),
         ],
         compiler_params=pltpu.CompilerParams(vmem_limit_bytes=8 << 20),
     )(*map(in_vmem, (scaled, inputs, *sums)))

time: 27.9 us -> 27.8 us (level)
  no operation moved by 1% of the time
where the time goes in v6:
time: 27.8 us; the launch traced here: 27.4 us
  starting transfers between devices  16.7 us (60%)
  waiting for transfers between devices  6.36 us (23%)
  Pallas kernels  4.3 us (15%)
    ppermute x5, starting transfers between devices, swapped(): lax.ppermute(block, axis, [(i ^ mask, i) for i in range(lax.axis_size(axi...  7.61 us
    ppermute x5, starting transfers between devices, handed_over(): return lax.ppermute(block, ('section', 'tp'), route)  5.96 us
    ppermute x5, waiting for transfers between devices, swapped(): lax.ppermute(block, axis, [(i ^ mask, i) for i in range(lax.axis_size(axi...  4.12 us
    ppermute x2, starting transfers between devices, passed_along(): return lax.ppermute(block, axis, route)  3.14 us
    ppermute x5, waiting for transfers between devices, handed_over(): return lax.ppermute(block, ('section', 'tp'), route)  2.15 us
    pallas_call x1, Pallas kernels, finish(): pl.pallas_call(finish_kernel, out_shape=pltpu.HBM(inputs.shape, jnp.bfloa...  1.06 us
    pallas_call x1, Pallas kernels, pack(): pl.pallas_call(pack_kernel, out_shape=(pltpu.VMEM((2, *own.shape), own.dt...  0.98 us
    pallas_call x1, Pallas kernels, project(): pl.pallas_call(functools.partial(project_kernel, head_of, (len(blocks), l...  0.75 us
  transfers between devices with their start and end apart: 12, of which 7 were waited for; matrix products, arithmetic and copies ran while one was open for 0% of the time, Pallas kernels for 6%

profile of v6, /device:TPU:1, one launch (start us, length us, event | category | flops | bytes accessed | tf_op | source)
XLA Modules:
  0.0 27.4 jit_solution(13265554004957620337)
XLA Ops:
  0.0 0.0 copy-start.1
  0.0 0.0 copy-start
  0.0 0.0 copy-start.2
  0.0 1.0 %shard_map.73 = (bf16[2,128,128]{2,1,0:T(8,128)(2,1)S(1)}, bf16[128,128]{1,0:T(8,128)(2,1)S(1)}, bf16[128,128]{1,0:T(8,128)(2,1)S(1)}) custom-call(bf16[128,128]{1,0:T(8,128)(2,1)} %bitcast.12, bf16[128,128]{1,0:T(8,128)(2,1)} %bitcast.13, bf16[128,128]{1,0:T(8,128)(2,1)} %bitcast.14, s32[1,4]{1,0:T(1,128)} %evicted_ref.1), custom_call_target="tpu_custom_call" | custom-call | flops 34359738368 | bytes 33554432 | tf_op jit(solution)/shard_map/pallas_call | solution.py:83
  1.0 2.1 %collective-permute-start.2 = (bf16[2,128,128]{2,1,0:T(8,128)(2,1)S(1)}, bf16[2,128,128]{2,1,0:T(8,128)(2,1)S(1)}, u32[]{:S(2)}, u32[]{:S(2)}) collective-permute-start(bf16[2,128,128]{2,1,0:T(8,128)(2,1)S(1)} %get-tuple-element.14.refs_3_), channel_id=1, source_target_pairs={{1,0},{0,1},{3,2},{2,3},{5,4},{4,5},{7,6},{6,7},{9,8},{8,9},{11,10... | collective-permute-start | bytes 196616 | tf_op jit(solution)/shard_map/ppermute | solution.py:24
  3.1 1.2 %collective-permute-start.1 = (bf16[128,128]{1,0:T(8,128)(2,1)S(1)}, bf16[128,128]{1,0:T(8,128)(2,1)S(1)}, u32[]{:S(2)}, u32[]{:S(2)}) collective-permute-start(bf16[128,128]{1,0:T(8,128)(2,1)S(1)} %get-tuple-element.13), channel_id=1, source_target_pairs={{17,0},{16,1},{19,2},{18,3},{21,4},{20,5},{23,6},{22,7},{25,8},{24... | collective-permute-start | bytes 98312 | tf_op jit(solution)/shard_map/ppermute | solution.py:296
  4.3 0.1 collective-permute-start
  4.4 0.0 copy-done.1
  4.4 1.2 %collective-permute-start.7 = (bf16[128,1536]{1,0:T(8,128)(2,1)S(1)}, bf16[128,1536]{1,0:T(8,128)(2,1)S(1)}, u32[]{:S(2)}, u32[]{:S(2)}) collective-permute-start(bf16[128,1536]{1,0:T(8,128)(2,1)S(1)} %bitcast.9), channel_id=1, source_target_pairs={{8,0},{16,8},{24,16},{0,24},{9,1},{17,9},{25,17},{1,25},{10,2},{18... | collective-permute-start | bytes 1179656 | tf_op jit(solution)/shard_map/ppermute | solution.py:20
  5.6 0.0 collective-permute-done.2.refs_2_.first_ref
  5.6 0.0 copy-done
  5.6 0.0 copy-done.2
  5.6 0.6 %shard_map.76.refs_8_ = bf16[144,1024]{1,0:T(8,128)(2,1)S(1)} custom-call(bf16[1536,1024]{1,0:T(8,128)(2,1)S(1)} %bitcast.6, bf16[128,1536]{1,0:T(8,128)(2,1)S(1)} %bitcast.10, f32[1,1536]{1,0:T(1,128)S(1)} %copy-done.2, bf16[2,128,128]{2,1,0:T(8,128)(2,1)S(1)} %collective-permute-done.2.refs_2_.first_ref), custom_call_target="tpu_custom_call" | custom-call | flops 34359738368 | bytes 33554432 | tf_op jit(solution)/shard_map/pallas_call | solution.py:114
  6.3 1.7 %collective-permute-start.6 = (bf16[144,1024]{1,0:T(8,128)(2,1)S(1)}, bf16[144,1024]{1,0:T(8,128)(2,1)S(1)}, u32[]{:S(2)}, u32[]{:S(2)}) collective-permute-start(bf16[144,1024]{1,0:T(8,128)(2,1)S(1)} %shard_map.76.refs_8_), channel_id=1, source_target_pairs={{1,0},{0,1},{3,2},{2,3},{5,4},{4,5},{7,6},{6,7},{9,8},{8,9},{11,10... | collective-permute-start | bytes 884744 | tf_op jit(solution)/shard_map/ppermute | solution.py:24
  8.0 0.0 collective-permute-done.1.refs_1_
  8.0 0.0 collective-permute-done.refs_0_
  8.0 0.2 shard_map.74.refs_0_
  8.2 3.4 %collective-permute-start.3 = (bf16[2,128,128]{2,1,0:T(8,128)(2,1)S(1)}, bf16[2,128,128]{2,1,0:T(8,128)(2,1)S(1)}, u32[]{:S(2)}, u32[]{:S(2)}) collective-permute-start(bf16[2,128,128]{2,1,0:T(8,128)(2,1)S(1)} %shard_map.74.refs_0_), channel_id=1, source_target_pairs={{6,0},{7,1},{4,2},{5,3},{2,4},{3,5},{0,6},{1,7},{14,8},{15,9},{12,... | collective-permute-start | bytes 196616 | tf_op jit(solution)/shard_map/ppermute | solution.py:24
  11.6 0.0 collective-permute-start.5
  11.6 0.4 %collective-permute-start.4 = (bf16[2,128,128]{2,1,0:T(8,128)(2,1)S(1)}, bf16[2,128,128]{2,1,0:T(8,128)(2,1)S(1)}, u32[]{:S(2)}, u32[]{:S(2)}) collective-permute-start(bf16[2,128,128]{2,1,0:T(8,128)(2,1)S(1)} %shard_map.74.refs_0_), channel_id=1, source_target_pairs={{2,0},{3,1},{0,2},{1,3},{6,4},{7,5},{4,6},{5,7},{10,8},{11,9},{8,1... | collective-permute-start | bytes 196616 | tf_op jit(solution)/shard_map/ppermute | solution.py:24
  12.0 1.3 %collective-permute-done.3.refs_1_ = bf16[2,128,128]{2,1,0:T(8,128)(2,1)S(1)} collective-permute-done((bf16[2,128,128]{2,1,0:T(8,128)(2,1)S(1)}, bf16[2,128,128]{2,1,0:T(8,128)(2,1)S(1)}, u32[]{:S(2)}, u32[]{:S(2)}) %collective-permute-start.3) | collective-permute-done | bytes 65568 | tf_op jit(solution)/shard_map/ppermute | solution.py:24
  13.3 0.7 %shard_map.75.refs_4_ = f32[128,1536]{1,0:T(8,128)S(1)} custom-call(bf16[2,128,128]{2,1,0:T(8,128)(2,1)S(1)} %shard_map.74.refs_0_, bf16[2,128,128]{2,1,0:T(8,128)(2,1)S(1)} %collective-permute-done.3.refs_1_, bf16[1536,1024]{1,0:T(8,128)(2,1)S(1)} %bitcast.7), custom_call_target="tpu_custom_call" | custom-call | flops 65536 | bytes 4096 | tf_op jit(solution)/shard_map/pallas_call | solution.py:190
  14.0 0.5 %collective-permute-done.6.refs_9_ = bf16[144,1024]{1,0:T(8,128)(2,1)S(1)} collective-permute-done((bf16[144,1024]{1,0:T(8,128)(2,1)S(1)}, bf16[144,1024]{1,0:T(8,128)(2,1)S(1)}, u32[]{:S(2)}, u32[]{:S(2)}) %collective-permute-start.6) | collective-permute-done | bytes 294944 | tf_op jit(solution)/shard_map/ppermute | solution.py:24
  14.4 0.0 collective-permute-done.7.input_ref
  14.4 2.3 %collective-permute-done.5.refs_3_ = bf16[2,128,128]{2,1,0:T(8,128)(2,1)S(1)} collective-permute-done((bf16[2,128,128]{2,1,0:T(8,128)(2,1)S(1)}, bf16[2,128,128]{2,1,0:T(8,128)(2,1)S(1)}, u32[]{:S(2)}, u32[]{:S(2)}) %collective-permute-start.5) | collective-permute-done | bytes 65568 | tf_op jit(solution)/shard_map/ppermute | solution.py:24
  16.8 0.0 collective-permute-done.4.refs_2_
  16.8 0.8 %shard_map.77 = (bf16[128,1664]{1,0:T(8,128)(2,1)S(1)}, f32[2,128]{1,0:T(2,128)S(1)}) custom-call(bf16[2,128,128]{2,1,0:T(8,128)(2,1)S(1)} %shard_map.74.refs_0_, bf16[2,128,128]{2,1,0:T(8,128)(2,1)S(1)} %collective-permute-done.3.refs_1_, bf16[2,128,128]{2,1,0:T(8,128)(2,1)S(1)} %collective-permute-done.4.refs_2_, ...), custom_call_target="tpu_custom_call" | custom-call | flops 34359738368 | bytes 33554432 | tf_op jit(solution)/shard_map/pallas_call | solution.py:231
  17.5 1.9 %collective-permute-start.8 = (bf16[128,1664]{1,0:T(8,128)(2,1)S(1)}, bf16[128,1664]{1,0:T(8,128)(2,1)S(1)}, u32[]{:S(2)}, u32[]{:S(2)}) collective-permute-start(bf16[128,1664]{1,0:T(8,128)(2,1)S(1)} %get-tuple-element.16), channel_id=1, source_target_pairs={{8,0},{16,8},{24,16},{0,24},{9,1},{17,9},{25,17},{1,25},{10,2},{18... | collective-permute-start | bytes 1277960 | tf_op jit(solution)/shard_map/ppermute | solution.py:20
  19.4 2.0 %collective-permute-start.11 = (f32[2,128]{1,0:T(2,128)S(1)}, f32[2,128]{1,0:T(2,128)S(1)}, u32[]{:S(2)}, u32[]{:S(2)}) collective-permute-start(f32[2,128]{1,0:T(2,128)S(1)} %get-tuple-element.18), channel_id=1, source_target_pairs={{14,0},{15,1},{12,2},{13,3},{10,4},{11,5},{8,6},{9,7},{22,8},{23,9... | collective-permute-start | bytes 3080 | tf_op jit(solution)/shard_map/ppermute | solution.py:296
  21.4 0.7 %collective-permute-start.10 = (f32[2,128]{1,0:T(2,128)S(1)}, f32[2,128]{1,0:T(2,128)S(1)}, u32[]{:S(2)}, u32[]{:S(2)}) collective-permute-start(f32[2,128]{1,0:T(2,128)S(1)} %get-tuple-element.18), channel_id=1, source_target_pairs={{12,0},{13,1},{14,2},{15,3},{8,4},{9,5},{10,6},{11,7},{20,8},{21,9... | collective-permute-start | bytes 3080 | tf_op jit(solution)/shard_map/ppermute | solution.py:296
  22.2 2.0 %collective-permute-start.9 = (f32[2,128]{1,0:T(2,128)S(1)}, f32[2,128]{1,0:T(2,128)S(1)}, u32[]{:S(2)}, u32[]{:S(2)}) collective-permute-start(f32[2,128]{1,0:T(2,128)S(1)} %get-tuple-element.18), channel_id=1, source_target_pairs={{10,0},{11,1},{8,2},{9,3},{14,4},{15,5},{12,6},{13,7},{18,8},{19,9... | collective-permute-start | bytes 3080 | tf_op jit(solution)/shard_map/ppermute | solution.py:296
  24.1 1.0 %collective-permute-done.11.refs_2_ = f32[2,128]{1,0:T(2,128)S(1)} collective-permute-done((f32[2,128]{1,0:T(2,128)S(1)}, f32[2,128]{1,0:T(2,128)S(1)}, u32[]{:S(2)}, u32[]{:S(2)}) %collective-permute-start.11) | collective-permute-done | bytes 1056 | tf_op jit(solution)/shard_map/ppermute | solution.py:296
  25.1 1.1 %collective-permute-done.10.refs_1_ = f32[2,128]{1,0:T(2,128)S(1)} collective-permute-done((f32[2,128]{1,0:T(2,128)S(1)}, f32[2,128]{1,0:T(2,128)S(1)}, u32[]{:S(2)}, u32[]{:S(2)}) %collective-permute-start.10) | collective-permute-done | bytes 1056 | tf_op jit(solution)/shard_map/ppermute | solution.py:296
  26.2 0.1 collective-permute-done.9.refs_0_
  26.3 0.1 collective-permute-done.8.scaled_ref
  26.4 1.1 %shard_map.78 = bf16[128,1536]{1,0:T(8,128)(2,1)} custom-call(bf16[128,1664]{1,0:T(8,128)(2,1)S(1)} %collective-permute-done.8.scaled_ref, bf16[128,1536]{1,0:T(8,128)(2,1)S(1)} %collective-permute-done.7.input_ref, f32[2,128]{1,0:T(2,128)S(1)} %collective-permute-done.9.refs_0_, f32[2,128]{1,0:T(2,128)S(1)} %collective-permute-done.10.refs_1_, ...), custom_call_target="tpu_custom_call" | custom-call | tf_op jit(solution)/shard_map/pallas_call | solution.py:272
Async XLA Ops:
  0.0 4.4 %copy-start.1 = (bf16[1,128,1536]{2,1,0:T(8,128)(2,1)S(1)}, bf16[1,128,1536]{2,1,0:T(8,128)(2,1)}, u32[]{:S(2)}) copy-start(bf16[1,128,1536]{2,1,0:T(8,128)(2,1)} %param.12) | copy-start | bytes 1179652
  0.0 5.6 %copy-start = (bf16[1,1536,1024]{2,1,0:T(8,128)(2,1)S(1)}, bf16[1,1536,1024]{2,1,0:T(8,128)(2,1)}, u32[]{:S(2)}) copy-start(bf16[1,1536,1024]{2,1,0:T(8,128)(2,1)} %param.8) | copy-start | bytes 9437188
  0.0 5.6 %copy-start.2 = (f32[1,1536]{1,0:T(1,128)S(1)}, f32[1,1536]{1,0:T(1,128)}, u32[]{:S(2)}) copy-start(f32[1,1536]{1,0:T(1,128)} %refs_7_.1) | copy-start | bytes 18436
  1.0 4.6 %collective-permute-start.2 = (bf16[2,128,128]{2,1,0:T(8,128)(2,1)S(1)}, bf16[2,128,128]{2,1,0:T(8,128)(2,1)S(1)}, u32[]{:S(2)}, u32[]{:S(2)}) collective-permute-start(bf16[2,128,128]{2,1,0:T(8,128)(2,1)S(1)} %get-tuple-element.14.refs_3_), channel_id=1, source_target_pairs={{1,0},{0,1},{3,2},{2,3},{5,4},{4,5},{7,6},{6,7},{9,8},{8,9},{11,10... | collective-permute-start | bytes 196616 | tf_op jit(solution)/shard_map/ppermute | solution.py:24
  3.1 4.9 %collective-permute-start.1 = (bf16[128,128]{1,0:T(8,128)(2,1)S(1)}, bf16[128,128]{1,0:T(8,128)(2,1)S(1)}, u32[]{:S(2)}, u32[]{:S(2)}) collective-permute-start(bf16[128,128]{1,0:T(8,128)(2,1)S(1)} %get-tuple-element.13), channel_id=1, source_target_pairs={{17,0},{16,1},{19,2},{18,3},{21,4},{20,5},{23,6},{22,7},{25,8},{24... | collective-permute-start | bytes 98312 | tf_op jit(solution)/shard_map/ppermute | solution.py:296
  4.3 3.7 %collective-permute-start = (bf16[128,128]{1,0:T(8,128)(2,1)S(1)}, bf16[128,128]{1,0:T(8,128)(2,1)S(1)}, u32[]{:S(2)}, u32[]{:S(2)}) collective-permute-start(bf16[128,128]{1,0:T(8,128)(2,1)S(1)} %get-tuple-element.13), channel_id=1, source_target_pairs={{16,0},{17,1},{18,2},{19,3},{20,4},{21,5},{22,6},{23,7},{24,8},{25... | collective-permute-start | bytes 98312 | tf_op jit(solution)/shard_map/ppermute | solution.py:296
  4.4 10.0 %collective-permute-start.7 = (bf16[128,1536]{1,0:T(8,128)(2,1)S(1)}, bf16[128,1536]{1,0:T(8,128)(2,1)S(1)}, u32[]{:S(2)}, u32[]{:S(2)}) collective-permute-start(bf16[128,1536]{1,0:T(8,128)(2,1)S(1)} %bitcast.9), channel_id=1, source_target_pairs={{8,0},{16,8},{24,16},{0,24},{9,1},{17,9},{25,17},{1,25},{10,2},{18... | collective-permute-start | bytes 1179656 | tf_op jit(solution)/shard_map/ppermute | solution.py:20
  6.3 8.1 %collective-permute-start.6 = (bf16[144,1024]{1,0:T(8,128)(2,1)S(1)}, bf16[144,1024]{1,0:T(8,128)(2,1)S(1)}, u32[]{:S(2)}, u32[]{:S(2)}) collective-permute-start(bf16[144,1024]{1,0:T(8,128)(2,1)S(1)} %shard_map.76.refs_8_), channel_id=1, source_target_pairs={{1,0},{0,1},{3,2},{2,3},{5,4},{4,5},{7,6},{6,7},{9,8},{8,9},{11,10... | collective-permute-start | bytes 884744 | tf_op jit(solution)/shard_map/ppermute | solution.py:24
  8.2 5.0 %collective-permute-start.3 = (bf16[2,128,128]{2,1,0:T(8,128)(2,1)S(1)}, bf16[2,128,128]{2,1,0:T(8,128)(2,1)S(1)}, u32[]{:S(2)}, u32[]{:S(2)}) collective-permute-start(bf16[2,128,128]{2,1,0:T(8,128)(2,1)S(1)} %shard_map.74.refs_0_), channel_id=1, source_target_pairs={{6,0},{7,1},{4,2},{5,3},{2,4},{3,5},{0,6},{1,7},{14,8},{15,9},{12,... | collective-permute-start | bytes 196616 | tf_op jit(solution)/shard_map/ppermute | solution.py:24
  11.6 5.2 %collective-permute-start.5 = (bf16[2,128,128]{2,1,0:T(8,128)(2,1)S(1)}, bf16[2,128,128]{2,1,0:T(8,128)(2,1)S(1)}, u32[]{:S(2)}, u32[]{:S(2)}) collective-permute-start(bf16[2,128,128]{2,1,0:T(8,128)(2,1)S(1)} %shard_map.74.refs_0_), channel_id=1, source_target_pairs={{4,0},{5,1},{6,2},{7,3},{0,4},{1,5},{2,6},{3,7},{12,8},{13,9},{14,... | collective-permute-start | bytes 196616 | tf_op jit(solution)/shard_map/ppermute | solution.py:24
  11.6 5.2 %collective-permute-start.4 = (bf16[2,128,128]{2,1,0:T(8,128)(2,1)S(1)}, bf16[2,128,128]{2,1,0:T(8,128)(2,1)S(1)}, u32[]{:S(2)}, u32[]{:S(2)}) collective-permute-start(bf16[2,128,128]{2,1,0:T(8,128)(2,1)S(1)} %shard_map.74.refs_0_), channel_id=1, source_target_pairs={{2,0},{3,1},{0,2},{1,3},{6,4},{7,5},{4,6},{5,7},{10,8},{11,9},{8,1... | collective-permute-start | bytes 196616 | tf_op jit(solution)/shard_map/ppermute | solution.py:24
  17.5 8.8 %collective-permute-start.8 = (bf16[128,1664]{1,0:T(8,128)(2,1)S(1)}, bf16[128,1664]{1,0:T(8,128)(2,1)S(1)}, u32[]{:S(2)}, u32[]{:S(2)}) collective-permute-start(bf16[128,1664]{1,0:T(8,128)(2,1)S(1)} %get-tuple-element.16), channel_id=1, source_target_pairs={{8,0},{16,8},{24,16},{0,24},{9,1},{17,9},{25,17},{1,25},{10,2},{18... | collective-permute-start | bytes 1277960 | tf_op jit(solution)/shard_map/ppermute | solution.py:20
  19.4 5.7 %collective-permute-start.11 = (f32[2,128]{1,0:T(2,128)S(1)}, f32[2,128]{1,0:T(2,128)S(1)}, u32[]{:S(2)}, u32[]{:S(2)}) collective-permute-start(f32[2,128]{1,0:T(2,128)S(1)} %get-tuple-element.18), channel_id=1, source_target_pairs={{14,0},{15,1},{12,2},{13,3},{10,4},{11,5},{8,6},{9,7},{22,8},{23,9... | collective-permute-start | bytes 3080 | tf_op jit(solution)/shard_map/ppermute | solution.py:296
  21.4 4.8 %collective-permute-start.10 = (f32[2,128]{1,0:T(2,128)S(1)}, f32[2,128]{1,0:T(2,128)S(1)}, u32[]{:S(2)}, u32[]{:S(2)}) collective-permute-start(f32[2,128]{1,0:T(2,128)S(1)} %get-tuple-element.18), channel_id=1, source_target_pairs={{12,0},{13,1},{14,2},{15,3},{8,4},{9,5},{10,6},{11,7},{20,8},{21,9... | collective-permute-start | bytes 3080 | tf_op jit(solution)/shard_map/ppermute | solution.py:296
  22.2 4.1 %collective-permute-start.9 = (f32[2,128]{1,0:T(2,128)S(1)}, f32[2,128]{1,0:T(2,128)S(1)}, u32[]{:S(2)}, u32[]{:S(2)}) collective-permute-start(f32[2,128]{1,0:T(2,128)S(1)} %get-tuple-element.18), channel_id=1, source_target_pairs={{10,0},{11,1},{8,2},{9,3},{14,4},{15,5},{12,6},{13,7},{18,8},{19,9... | collective-permute-start | bytes 3080 | tf_op jit(solution)/shard_map/ppermute | solution.py:296

commit v7 on v6

--- a/solution.py
+++ b/solution.py
@@ -11,6 +11,7 @@
 LANES = 128
 PIECES = (0, 3, 5, 7, 8)
 EXTRA = 16
+SHORT = pl.CostEstimate(flops=1 << 16, bytes_accessed=1 << 12, transcendentals=0)
 HIDES = pl.CostEstimate(flops=1 << 35, bytes_accessed=1 << 25, transcendentals=0)
 
 
@@ -98,8 +99,7 @@
     )(*map(in_hbm, (own, grad, spare, evicted)))
 
 
-def reach_kernel(weight_ref, input_ref, gain_ref, first_ref, reach_ref):
-    del first_ref
+def reach_kernel(weight_ref, input_ref, gain_ref, reach_ref):
     tokens, features = input_ref.shape
     values = input_ref[...].astype(jnp.float32)
     reach_ref[tokens:, :] = jnp.zeros_like(reach_ref[tokens:, :])
@@ -110,15 +110,15 @@
     reach_ref[:tokens, :] = reach.astype(reach_ref.dtype)
 
 
-def reach_of(weights, inputs, gain, first):
+def reach_of(weights, inputs, gain):
     return pl.pallas_call(
         reach_kernel,
         out_shape=pltpu.VMEM((inputs.shape[0] + EXTRA, weights.shape[1]), jnp.bfloat16),
-        in_specs=vmem_specs(4),
+        in_specs=vmem_specs(3),
         out_specs=pl.BlockSpec(memory_space=pltpu.VMEM),
-        cost_estimate=HIDES,
+        cost_estimate=SHORT,
         compiler_params=pltpu.CompilerParams(vmem_limit_bytes=8 << 20),
-    )(*map(in_vmem, (weights, inputs, gain, first)))
+    )(*map(in_vmem, (weights, inputs, gain)))
 
 
 def mix_kernel(taken_ref, *refs):
@@ -193,7 +193,7 @@
         in_specs=vmem_specs(len(blocks) + 1),
         out_specs=pl.BlockSpec(memory_space=pltpu.VMEM),
         scratch_shapes=[pltpu.VMEM((tokens, weights.shape[1]), jnp.bfloat16)],
-        cost_estimate=pl.CostEstimate(flops=1 << 16, bytes_accessed=1 << 12, transcendentals=0),
+        cost_estimate=SHORT,
         compiler_params=pltpu.CompilerParams(vmem_limit_bytes=16 << 20),
     )(*map(in_vmem, (*blocks, weights)))
 
@@ -316,13 +316,17 @@
         spare = handed_over(spares, sections, count, sections // 2, mask)
         heads.append((swapped(packed, "tp", mask) if mask else packed, spare))
     weights, inputs = w_value[0], layer_input[0]
-    next_input = passed_along(inputs, "section", -1)
-    reach = reach_of(weights, inputs, gain, heads[-1][0])
+    reach = reach_of(weights, inputs, gain)
     if count == 8:
+        swap, spare = heads[1]
+        reach, sent, swap = lax.optimization_barrier((reach, inputs, swap))
+        heads[1] = swap, spare
         reaches = [reach, swapped(reach, "tp", SIDE)]
+        next_input = passed_along(sent, "section", -1)
         reaches[1], next_input = lax.optimization_barrier((reaches[1], next_input))
     else:
         reaches = [lax.psum(reach, "tp")]
+        next_input = passed_along(inputs, "section", -1)
     pair = value_gradients(taken, heads)
     blocks, head_of = gathered(pair, "tp")
     early = [project_early(head_of, blocks[:EARLY], weights)] if count == 8 else []

time: 27.8 us -> 28.1 us (1.011)
  waiting for transfers between devices: 6.36 us -> 7.41 us
  starting transfers between devices: 16.7 us -> 16.2 us
    ppermute x2, waiting for transfers between devices: 0.09 us -> 0.88 us  [passed_along(): return lax.ppermute(block, axis, route)]
    ppermute x5, waiting for transfers between devices: 2.15 us -> 2.62 us  [handed_over(): return lax.ppermute(block, ('section', 'tp'), route)]
    ppermute x2, starting transfers between devices: 3.14 us -> 2.84 us  [passed_along(): return lax.ppermute(block, axis, route)]
  transfers between devices with their start and end apart: 12 -> 12, of which waited for: 7 -> 5; matrix products, arithmetic and copies ran while one was open for 0% -> 0% of each run, Pallas kernels for 6% -> 5%
where the time goes in v7:
time: 28.1 us; the launch traced here: 28 us
  starting transfers between devices  16.2 us (58%)
  waiting for transfers between devices  7.41 us (26%)
  Pallas kernels  4.29 us (15%)
    ppermute x5, starting transfers between devices, swapped(): lax.ppermute(block, axis, [(i ^ mask, i) for i in range(lax.axis_size(axi...  7.49 us
    ppermute x5, starting transfers between devices, handed_over(): return lax.ppermute(block, ('section', 'tp'), route)  5.85 us
    ppermute x5, waiting for transfers between devices, swapped(): lax.ppermute(block, axis, [(i ^ mask, i) for i in range(lax.axis_size(axi...  3.92 us
    ppermute x2, starting transfers between devices, passed_along(): return lax.ppermute(block, axis, route)  2.84 us
    ppermute x5, waiting for transfers between devices, handed_over(): return lax.ppermute(block, ('section', 'tp'), route)  2.62 us
    pallas_call x1, Pallas kernels, finish(): pl.pallas_call(finish_kernel, out_shape=pltpu.HBM(inputs.shape, jnp.bfloa...  1.06 us
    pallas_call x1, Pallas kernels, pack(): pl.pallas_call(pack_kernel, out_shape=(pltpu.VMEM((2, *own.shape), own.dt...  0.98 us
    ppermute x2, waiting for transfers between devices, passed_along(): return lax.ppermute(block, axis, route)  0.88 us
  transfers between devices with their start and end apart: 12, of which 5 were waited for; matrix products, arithmetic and copies ran while one was open for 0% of the time, Pallas kernels for 5%

profile of v7, /device:TPU:1, one launch (start us, length us, event | category | flops | bytes accessed | tf_op | source)
XLA Modules:
  0.0 28.0 jit_solution(16451393174289195144)
XLA Ops:
  0.0 0.0 copy-start
  0.0 0.0 copy-start.1
  0.0 0.0 copy-start.2
  0.0 1.0 %shard_map.73 = (bf16[2,128,128]{2,1,0:T(8,128)(2,1)S(1)}, bf16[128,128]{1,0:T(8,128)(2,1)S(1)}, bf16[128,128]{1,0:T(8,128)(2,1)S(1)}) custom-call(bf16[128,128]{1,0:T(8,128)(2,1)} %bitcast.12, bf16[128,128]{1,0:T(8,128)(2,1)} %bitcast.13, bf16[128,128]{1,0:T(8,128)(2,1)} %bitcast.14, s32[1,4]{1,0:T(1,128)} %evicted_ref.1), custom_call_target="tpu_custom_call" | custom-call | flops 34359738368 | bytes 33554432 | tf_op jit(solution)/shard_map/pallas_call | solution.py:84
  1.0 2.1 %collective-permute-start.2 = (bf16[2,128,128]{2,1,0:T(8,128)(2,1)S(1)}, bf16[2,128,128]{2,1,0:T(8,128)(2,1)S(1)}, u32[]{:S(2)}, u32[]{:S(2)}) collective-permute-start(bf16[2,128,128]{2,1,0:T(8,128)(2,1)S(1)} %get-tuple-element.17.refs_3_), channel_id=1, source_target_pairs={{1,0},{0,1},{3,2},{2,3},{5,4},{4,5},{7,6},{6,7},{9,8},{8,9},{11,10... | collective-permute-start | bytes 196616 | tf_op jit(solution)/shard_map/ppermute | solution.py:25
  3.1 1.2 %collective-permute-start.1 = (bf16[128,128]{1,0:T(8,128)(2,1)S(1)}, bf16[128,128]{1,0:T(8,128)(2,1)S(1)}, u32[]{:S(2)}, u32[]{:S(2)}) collective-permute-start(bf16[128,128]{1,0:T(8,128)(2,1)S(1)} %get-tuple-element.16), channel_id=1, source_target_pairs={{17,0},{16,1},{19,2},{18,3},{21,4},{20,5},{23,6},{22,7},{25,8},{24... | collective-permute-start | bytes 98312 | tf_op jit(solution)/shard_map/ppermute | solution.py:296
  4.3 0.1 collective-permute-start
  4.4 0.0 copy-done
  4.4 0.0 copy-done.1
  4.4 0.0 copy-done.2
  4.4 0.6 %shard_map.74.refs_8_ = bf16[144,1024]{1,0:T(8,128)(2,1)S(1)} custom-call(bf16[1536,1024]{1,0:T(8,128)(2,1)S(1)} %bitcast.6, bf16[128,1536]{1,0:T(8,128)(2,1)S(1)} %bitcast.9, f32[1,1536]{1,0:T(1,128)S(1)} %copy-done.2), custom_call_target="tpu_custom_call" | custom-call | flops 65536 | bytes 4096 | tf_op jit(solution)/shard_map/pallas_call | solution.py:114
  5.0 0.0 collective-permute-done.2.refs_2_
  5.1 1.5 %collective-permute-start.6 = (bf16[144,1024]{1,0:T(8,128)(2,1)S(1)}, bf16[144,1024]{1,0:T(8,128)(2,1)S(1)}, u32[]{:S(2)}, u32[]{:S(2)}) collective-permute-start(bf16[144,1024]{1,0:T(8,128)(2,1)S(1)} %shard_map.74.refs_8_), channel_id=1, source_target_pairs={{1,0},{0,1},{3,2},{2,3},{5,4},{4,5},{7,6},{6,7},{9,8},{8,9},{11,10... | collective-permute-start | bytes 884744 | tf_op jit(solution)/shard_map/ppermute | solution.py:25
  6.5 2.0 %collective-permute-start.7 = (bf16[128,1536]{1,0:T(8,128)(2,1)S(1)}, bf16[128,1536]{1,0:T(8,128)(2,1)S(1)}, u32[]{:S(2)}, u32[]{:S(2)}) collective-permute-start(bf16[128,1536]{1,0:T(8,128)(2,1)S(1)} %bitcast.10), channel_id=1, source_target_pairs={{8,0},{16,8},{24,16},{0,24},{9,1},{17,9},{25,17},{1,25},{10,2},{18... | collective-permute-start | bytes 1179656 | tf_op jit(solution)/shard_map/ppermute | solution.py:21
  8.5 0.0 collective-permute-done.1.refs_1_
  8.5 0.0 collective-permute-done.refs_0_
  8.6 0.2 shard_map.75.refs_0_
  8.8 3.5 %collective-permute-start.3 = (bf16[2,128,128]{2,1,0:T(8,128)(2,1)S(1)}, bf16[2,128,128]{2,1,0:T(8,128)(2,1)S(1)}, u32[]{:S(2)}, u32[]{:S(2)}) collective-permute-start(bf16[2,128,128]{2,1,0:T(8,128)(2,1)S(1)} %shard_map.75.refs_0_), channel_id=1, source_target_pairs={{6,0},{7,1},{4,2},{5,3},{2,4},{3,5},{0,6},{1,7},{14,8},{15,9},{12,... | collective-permute-start | bytes 196616 | tf_op jit(solution)/shard_map/ppermute | solution.py:25
  12.3 0.0 collective-permute-start.5
  12.3 0.4 %collective-permute-start.4 = (bf16[2,128,128]{2,1,0:T(8,128)(2,1)S(1)}, bf16[2,128,128]{2,1,0:T(8,128)(2,1)S(1)}, u32[]{:S(2)}, u32[]{:S(2)}) collective-permute-start(bf16[2,128,128]{2,1,0:T(8,128)(2,1)S(1)} %shard_map.75.refs_0_), channel_id=1, source_target_pairs={{2,0},{3,1},{0,2},{1,3},{6,4},{7,5},{4,6},{5,7},{10,8},{11,9},{8,1... | collective-permute-start | bytes 196616 | tf_op jit(solution)/shard_map/ppermute | solution.py:25
  12.6 1.3 %collective-permute-done.3.refs_1_ = bf16[2,128,128]{2,1,0:T(8,128)(2,1)S(1)} collective-permute-done((bf16[2,128,128]{2,1,0:T(8,128)(2,1)S(1)}, bf16[2,128,128]{2,1,0:T(8,128)(2,1)S(1)}, u32[]{:S(2)}, u32[]{:S(2)}) %collective-permute-start.3) | collective-permute-done | bytes 65568 | tf_op jit(solution)/shard_map/ppermute | solution.py:25
  14.0 0.7 %shard_map.76.refs_4_ = f32[128,1536]{1,0:T(8,128)S(1)} custom-call(bf16[2,128,128]{2,1,0:T(8,128)(2,1)S(1)} %shard_map.75.refs_0_, bf16[2,128,128]{2,1,0:T(8,128)(2,1)S(1)} %collective-permute-done.3.refs_1_, bf16[1536,1024]{1,0:T(8,128)(2,1)S(1)} %bitcast.7), custom_call_target="tpu_custom_call" | custom-call | flops 65536 | bytes 4096 | tf_op jit(solution)/shard_map/pallas_call | solution.py:190
  14.7 0.0 collective-permute-done.6.refs_9_
  14.7 0.9 %collective-permute-done.7.input_ref = bf16[128,1536]{1,0:T(8,128)(2,1)S(1)} collective-permute-done((bf16[128,1536]{1,0:T(8,128)(2,1)S(1)}, bf16[128,1536]{1,0:T(8,128)(2,1)S(1)}, u32[]{:S(2)}, u32[]{:S(2)}) %collective-permute-start.7) | collective-permute-done | bytes 393248 | tf_op jit(solution)/shard_map/ppermute | solution.py:21
  15.5 2.6 %collective-permute-done.5.refs_3_ = bf16[2,128,128]{2,1,0:T(8,128)(2,1)S(1)} collective-permute-done((bf16[2,128,128]{2,1,0:T(8,128)(2,1)S(1)}, bf16[2,128,128]{2,1,0:T(8,128)(2,1)S(1)}, u32[]{:S(2)}, u32[]{:S(2)}) %collective-permute-start.5) | collective-permute-done | bytes 65568 | tf_op jit(solution)/shard_map/ppermute | solution.py:25
  18.1 0.0 collective-permute-done.4.refs_2_
  18.1 0.7 %shard_map.77 = (bf16[128,1664]{1,0:T(8,128)(2,1)S(1)}, f32[2,128]{1,0:T(2,128)S(1)}) custom-call(bf16[2,128,128]{2,1,0:T(8,128)(2,1)S(1)} %shard_map.75.refs_0_, bf16[2,128,128]{2,1,0:T(8,128)(2,1)S(1)} %collective-permute-done.3.refs_1_, bf16[2,128,128]{2,1,0:T(8,128)(2,1)S(1)} %collective-permute-done.4.refs_2_, ...), custom_call_target="tpu_custom_call" | custom-call | flops 34359738368 | bytes 33554432 | tf_op jit(solution)/shard_map/pallas_call | solution.py:231
  18.9 0.8 %collective-permute-start.8 = (bf16[128,1664]{1,0:T(8,128)(2,1)S(1)}, bf16[128,1664]{1,0:T(8,128)(2,1)S(1)}, u32[]{:S(2)}, u32[]{:S(2)}) collective-permute-start(bf16[128,1664]{1,0:T(8,128)(2,1)S(1)} %get-tuple-element.22), channel_id=1, source_target_pairs={{8,0},{16,8},{24,16},{0,24},{9,1},{17,9},{25,17},{1,25},{10,2},{18... | collective-permute-start | bytes 1277960 | tf_op jit(solution)/shard_map/ppermute | solution.py:21
  19.7 2.4 %collective-permute-start.11 = (f32[2,128]{1,0:T(2,128)S(1)}, f32[2,128]{1,0:T(2,128)S(1)}, u32[]{:S(2)}, u32[]{:S(2)}) collective-permute-start(f32[2,128]{1,0:T(2,128)S(1)} %get-tuple-element.24), channel_id=1, source_target_pairs={{14,0},{15,1},{12,2},{13,3},{10,4},{11,5},{8,6},{9,7},{22,8},{23,9... | collective-permute-start | bytes 3080 | tf_op jit(solution)/shard_map/ppermute | solution.py:296
  22.1 0.7 %collective-permute-start.10 = (f32[2,128]{1,0:T(2,128)S(1)}, f32[2,128]{1,0:T(2,128)S(1)}, u32[]{:S(2)}, u32[]{:S(2)}) collective-permute-start(f32[2,128]{1,0:T(2,128)S(1)} %get-tuple-element.24), channel_id=1, source_target_pairs={{12,0},{13,1},{14,2},{15,3},{8,4},{9,5},{10,6},{11,7},{20,8},{21,9... | collective-permute-start | bytes 3080 | tf_op jit(solution)/shard_map/ppermute | solution.py:296
  22.8 1.4 %collective-permute-start.9 = (f32[2,128]{1,0:T(2,128)S(1)}, f32[2,128]{1,0:T(2,128)S(1)}, u32[]{:S(2)}, u32[]{:S(2)}) collective-permute-start(f32[2,128]{1,0:T(2,128)S(1)} %get-tuple-element.24), channel_id=1, source_target_pairs={{10,0},{11,1},{8,2},{9,3},{14,4},{15,5},{12,6},{13,7},{18,8},{19,9... | collective-permute-start | bytes 3080 | tf_op jit(solution)/shard_map/ppermute | solution.py:296
  24.3 1.1 %collective-permute-done.11.refs_2_ = f32[2,128]{1,0:T(2,128)S(1)} collective-permute-done((f32[2,128]{1,0:T(2,128)S(1)}, f32[2,128]{1,0:T(2,128)S(1)}, u32[]{:S(2)}, u32[]{:S(2)}) %collective-permute-start.11) | collective-permute-done | bytes 1056 | tf_op jit(solution)/shard_map/ppermute | solution.py:296
  25.4 1.5 %collective-permute-done.10.refs_1_ = f32[2,128]{1,0:T(2,128)S(1)} collective-permute-done((f32[2,128]{1,0:T(2,128)S(1)}, f32[2,128]{1,0:T(2,128)S(1)}, u32[]{:S(2)}, u32[]{:S(2)}) %collective-permute-start.10) | collective-permute-done | bytes 1056 | tf_op jit(solution)/shard_map/ppermute | solution.py:296
  26.9 0.0 collective-permute-done.9.refs_0_
  26.9 0.0 collective-permute-done.8.scaled_ref
  26.9 1.1 %shard_map.78 = bf16[128,1536]{1,0:T(8,128)(2,1)} custom-call(bf16[128,1664]{1,0:T(8,128)(2,1)S(1)} %collective-permute-done.8.scaled_ref, bf16[128,1536]{1,0:T(8,128)(2,1)S(1)} %collective-permute-done.7.input_ref, f32[2,128]{1,0:T(2,128)S(1)} %collective-permute-done.9.refs_0_, f32[2,128]{1,0:T(2,128)S(1)} %collective-permute-done.10.refs_1_, ...), custom_call_target="tpu_custom_call" | custom-call | tf_op jit(solution)/shard_map/pallas_call | solution.py:272
Async XLA Ops:
  0.0 4.4 %copy-start = (bf16[1,1536,1024]{2,1,0:T(8,128)(2,1)S(1)}, bf16[1,1536,1024]{2,1,0:T(8,128)(2,1)}, u32[]{:S(2)}) copy-start(bf16[1,1536,1024]{2,1,0:T(8,128)(2,1)} %param.8) | copy-start | bytes 9437188
  0.0 4.4 %copy-start.1 = (bf16[1,128,1536]{2,1,0:T(8,128)(2,1)S(1)}, bf16[1,128,1536]{2,1,0:T(8,128)(2,1)}, u32[]{:S(2)}) copy-start(bf16[1,128,1536]{2,1,0:T(8,128)(2,1)} %param.12) | copy-start | bytes 1179652
  0.0 4.4 %copy-start.2 = (f32[1,1536]{1,0:T(1,128)S(1)}, f32[1,1536]{1,0:T(1,128)}, u32[]{:S(2)}) copy-start(f32[1,1536]{1,0:T(1,128)} %refs_7_.1) | copy-start | bytes 18436
  1.0 4.1 %collective-permute-start.2 = (bf16[2,128,128]{2,1,0:T(8,128)(2,1)S(1)}, bf16[2,128,128]{2,1,0:T(8,128)(2,1)S(1)}, u32[]{:S(2)}, u32[]{:S(2)}) collective-permute-start(bf16[2,128,128]{2,1,0:T(8,128)(2,1)S(1)} %get-tuple-element.17.refs_3_), channel_id=1, source_target_pairs={{1,0},{0,1},{3,2},{2,3},{5,4},{4,5},{7,6},{6,7},{9,8},{8,9},{11,10... | collective-permute-start | bytes 196616 | tf_op jit(solution)/shard_map/ppermute | solution.py:25
  3.1 5.4 %collective-permute-start.1 = (bf16[128,128]{1,0:T(8,128)(2,1)S(1)}, bf16[128,128]{1,0:T(8,128)(2,1)S(1)}, u32[]{:S(2)}, u32[]{:S(2)}) collective-permute-start(bf16[128,128]{1,0:T(8,128)(2,1)S(1)} %get-tuple-element.16), channel_id=1, source_target_pairs={{17,0},{16,1},{19,2},{18,3},{21,4},{20,5},{23,6},{22,7},{25,8},{24... | collective-permute-start | bytes 98312 | tf_op jit(solution)/shard_map/ppermute | solution.py:296
  4.3 4.3 %collective-permute-start = (bf16[128,128]{1,0:T(8,128)(2,1)S(1)}, bf16[128,128]{1,0:T(8,128)(2,1)S(1)}, u32[]{:S(2)}, u32[]{:S(2)}) collective-permute-start(bf16[128,128]{1,0:T(8,128)(2,1)S(1)} %get-tuple-element.16), channel_id=1, source_target_pairs={{16,0},{17,1},{18,2},{19,3},{20,4},{21,5},{22,6},{23,7},{24,8},{25... | collective-permute-start | bytes 98312 | tf_op jit(solution)/shard_map/ppermute | solution.py:296
  5.1 9.6 %collective-permute-start.6 = (bf16[144,1024]{1,0:T(8,128)(2,1)S(1)}, bf16[144,1024]{1,0:T(8,128)(2,1)S(1)}, u32[]{:S(2)}, u32[]{:S(2)}) collective-permute-start(bf16[144,1024]{1,0:T(8,128)(2,1)S(1)} %shard_map.74.refs_8_), channel_id=1, source_target_pairs={{1,0},{0,1},{3,2},{2,3},{5,4},{4,5},{7,6},{6,7},{9,8},{8,9},{11,10... | collective-permute-start | bytes 884744 | tf_op jit(solution)/shard_map/ppermute | solution.py:25
  6.5 9.0 %collective-permute-start.7 = (bf16[128,1536]{1,0:T(8,128)(2,1)S(1)}, bf16[128,1536]{1,0:T(8,128)(2,1)S(1)}, u32[]{:S(2)}, u32[]{:S(2)}) collective-permute-start(bf16[128,1536]{1,0:T(8,128)(2,1)S(1)} %bitcast.10), channel_id=1, source_target_pairs={{8,0},{16,8},{24,16},{0,24},{9,1},{17,9},{25,17},{1,25},{10,2},{18... | collective-permute-start | bytes 1179656 | tf_op jit(solution)/shard_map/ppermute | solution.py:21
  8.8 5.2 %collective-permute-start.3 = (bf16[2,128,128]{2,1,0:T(8,128)(2,1)S(1)}, bf16[2,128,128]{2,1,0:T(8,128)(2,1)S(1)}, u32[]{:S(2)}, u32[]{:S(2)}) collective-permute-start(bf16[2,128,128]{2,1,0:T(8,128)(2,1)S(1)} %shard_map.75.refs_0_), channel_id=1, source_target_pairs={{6,0},{7,1},{4,2},{5,3},{2,4},{3,5},{0,6},{1,7},{14,8},{15,9},{12,... | collective-permute-start | bytes 196616 | tf_op jit(solution)/shard_map/ppermute | solution.py:25
  12.3 5.8 %collective-permute-start.5 = (bf16[2,128,128]{2,1,0:T(8,128)(2,1)S(1)}, bf16[2,128,128]{2,1,0:T(8,128)(2,1)S(1)}, u32[]{:S(2)}, u32[]{:S(2)}) collective-permute-start(bf16[2,128,128]{2,1,0:T(8,128)(2,1)S(1)} %shard_map.75.refs_0_), channel_id=1, source_target_pairs={{4,0},{5,1},{6,2},{7,3},{0,4},{1,5},{2,6},{3,7},{12,8},{13,9},{14,... | collective-permute-start | bytes 196616 | tf_op jit(solution)/shard_map/ppermute | solution.py:25
  12.3 5.8 %collective-permute-start.4 = (bf16[2,128,128]{2,1,0:T(8,128)(2,1)S(1)}, bf16[2,128,128]{2,1,0:T(8,128)(2,1)S(1)}, u32[]{:S(2)}, u32[]{:S(2)}) collective-permute-start(bf16[2,128,128]{2,1,0:T(8,128)(2,1)S(1)} %shard_map.75.refs_0_), channel_id=1, source_target_pairs={{2,0},{3,1},{0,2},{1,3},{6,4},{7,5},{4,6},{5,7},{10,8},{11,9},{8,1... | collective-permute-start | bytes 196616 | tf_op jit(solution)/shard_map/ppermute | solution.py:25
  18.9 8.0 %collective-permute-start.8 = (bf16[128,1664]{1,0:T(8,128)(2,1)S(1)}, bf16[128,1664]{1,0:T(8,128)(2,1)S(1)}, u32[]{:S(2)}, u32[]{:S(2)}) collective-permute-start(bf16[128,1664]{1,0:T(8,128)(2,1)S(1)} %get-tuple-element.22), channel_id=1, source_target_pairs={{8,0},{16,8},{24,16},{0,24},{9,1},{17,9},{25,17},{1,25},{10,2},{18... | collective-permute-start | bytes 1277960 | tf_op jit(solution)/shard_map/ppermute | solution.py:21
  19.7 5.7 %collective-permute-start.11 = (f32[2,128]{1,0:T(2,128)S(1)}, f32[2,128]{1,0:T(2,128)S(1)}, u32[]{:S(2)}, u32[]{:S(2)}) collective-permute-start(f32[2,128]{1,0:T(2,128)S(1)} %get-tuple-element.24), channel_id=1, source_target_pairs={{14,0},{15,1},{12,2},{13,3},{10,4},{11,5},{8,6},{9,7},{22,8},{23,9... | collective-permute-start | bytes 3080 | tf_op jit(solution)/shard_map/ppermute | solution.py:296
  22.1 4.8 %collective-permute-start.10 = (f32[2,128]{1,0:T(2,128)S(1)}, f32[2,128]{1,0:T(2,128)S(1)}, u32[]{:S(2)}, u32[]{:S(2)}) collective-permute-start(f32[2,128]{1,0:T(2,128)S(1)} %get-tuple-element.24), channel_id=1, source_target_pairs={{12,0},{13,1},{14,2},{15,3},{8,4},{9,5},{10,6},{11,7},{20,8},{21,9... | collective-permute-start | bytes 3080 | tf_op jit(solution)/shard_map/ppermute | solution.py:296
  22.8 4.1 %collective-permute-start.9 = (f32[2,128]{1,0:T(2,128)S(1)}, f32[2,128]{1,0:T(2,128)S(1)}, u32[]{:S(2)}, u32[]{:S(2)}) collective-permute-start(f32[2,128]{1,0:T(2,128)S(1)} %get-tuple-element.24), channel_id=1, source_target_pairs={{10,0},{11,1},{8,2},{9,3},{14,4},{15,5},{12,6},{13,7},{18,8},{19,9... | collective-permute-start | bytes 3080 | tf_op jit(solution)/shard_map/ppermute | solution.py:296

commit v8 on v6

--- a/solution.py
+++ b/solution.py
@@ -40,9 +40,16 @@
     return jnp.broadcast_to(column, (column.shape[0], column.shape[0])).T[:1]
 
 
-def standing(rows):
-    tokens = rows.shape[1]
-    return jnp.concatenate([rows, jnp.zeros((tokens - rows.shape[0], tokens), rows.dtype)]).T
+def chosen(rows, lanes, pick):
+    row = lax.broadcasted_iota(jnp.int32, (rows, lanes), 0)
+    lane = lax.broadcasted_iota(jnp.int32, (rows, lanes), 1)
+    return pick(row, lane).astype(jnp.float32).astype(jnp.bfloat16)
+
+
+def product(left, right, left_dim, right_dim):
+    return lax.dot_general(
+        left, right, (((left_dim,), (right_dim,)), ((), ())), preferred_element_type=jnp.float32
+    )
 
 
 def split(values):
@@ -53,72 +60,74 @@
     return parts
 
 
-def as_parts(row):
-    rest = jnp.zeros((EXTRA - 3, row.shape[1]), jnp.float32)
-    return jnp.concatenate(split(row) + [rest]).astype(jnp.bfloat16)
-
-
-def pack_kernel(own_ref, grad_ref, spare_ref, evicted_ref, *refs):
-    out_ref, spare_out, taken_ref, flags, sems = refs
+def as_parts(row, rows):
+    rest = [jnp.zeros((rows - 3, row.shape[1]), jnp.float32)] if rows > 3 else []
+    return jnp.concatenate(split(row) + rest)
+
+
+def pack_kernel(own_ref, grad_ref, spare_ref, out_ref, spare_out, sems):
     copies = [
-        pltpu.make_async_copy(evicted_ref, flags, sems.at[0]),
-        pltpu.make_async_copy(own_ref, out_ref.at[0], sems.at[1]),
-        pltpu.make_async_copy(grad_ref, out_ref.at[1], sems.at[2]),
-        pltpu.make_async_copy(spare_ref, spare_out, sems.at[3]),
+        pltpu.make_async_copy(own_ref, out_ref.at[0], sems.at[0]),
+        pltpu.make_async_copy(grad_ref, out_ref.at[1], sems.at[1]),
+        pltpu.make_async_copy(spare_ref, spare_out, sems.at[2]),
     ]
     for copy in copies:
         copy.start()
-    copies[0].wait()
-    tiles = evicted_ref.shape[1]
-    rows = taken_ref.shape[0] // tiles
-    for tile in range(tiles):
-        part = pl.ds(tile * rows, rows)
-        taken = jnp.full((rows, taken_ref.shape[1]), flags[0, tile], jnp.int32)
-        taken_ref[part, :] = taken.astype(jnp.float32).astype(taken_ref.dtype)
-    for copy in copies[1:]:
+    for copy in copies:
         copy.wait()
 
 
-def pack(own, grad, spare, evicted):
+def pack(own, grad, spare):
     return pl.pallas_call(
         pack_kernel,
         out_shape=(
             pltpu.VMEM((2, *own.shape), own.dtype),
             pltpu.VMEM(spare.shape, spare.dtype),
-            pltpu.VMEM(own.shape, own.dtype),
         ),
-        in_specs=[pl.BlockSpec(memory_space=pltpu.HBM)] * 4,
-        out_specs=tuple(vmem_specs(3)),
-        scratch_shapes=[
-            pltpu.SMEM(evicted.shape, evicted.dtype),
-            pltpu.SemaphoreType.DMA((4,)),
-        ],
+        in_specs=[pl.BlockSpec(memory_space=pltpu.HBM)] * 3,
+        out_specs=tuple(vmem_specs(2)),
+        scratch_shapes=[pltpu.SemaphoreType.DMA((3,))],
         cost_estimate=HIDES,
         compiler_params=pltpu.CompilerParams(vmem_limit_bytes=4 << 20),
-    )(*map(in_hbm, (own, grad, spare, evicted)))
-
-
-def reach_kernel(weight_ref, input_ref, gain_ref, first_ref, reach_ref):
+    )(*map(in_hbm, (own, grad, spare)))
+
+
+def reach_kernel(weight_ref, input_ref, gain_ref, first_ref, evicted_ref, *refs):
     del first_ref
+    reach_ref, taken_ref, flags, sem = refs
+    copy = pltpu.make_async_copy(evicted_ref, flags, sem)
+    copy.start()
     tokens, features = input_ref.shape
     values = input_ref[...].astype(jnp.float32)
     reach_ref[tokens:, :] = jnp.zeros_like(reach_ref[tokens:, :])
     squares = as_row(jnp.sum(values * values, axis=1, keepdims=True))
-    reach_ref[tokens:, :tokens] = as_parts(squares)
+    reach_ref[tokens:, :tokens] = as_parts(squares, EXTRA).astype(reach_ref.dtype)
     gained = (values * gain_ref[...]).astype(jnp.bfloat16)
     reach = jnp.dot(gained, weight_ref[...], preferred_element_type=jnp.float32)
     reach_ref[:tokens, :] = reach.astype(reach_ref.dtype)
-
-
-def reach_of(weights, inputs, gain, first):
+    copy.wait()
+    tiles = evicted_ref.shape[1]
+    rows = tokens // tiles
+    for tile in range(tiles):
+        part = pl.ds(tile * rows, rows)
+        taken = jnp.full((rows, tokens), flags[0, tile], jnp.int32)
+        taken_ref[part, :] = taken.astype(jnp.float32).astype(taken_ref.dtype)
+
+
+def reach_of(weights, inputs, gain, first, evicted):
+    tokens = inputs.shape[0]
     return pl.pallas_call(
         reach_kernel,
-        out_shape=pltpu.VMEM((inputs.shape[0] + EXTRA, weights.shape[1]), jnp.bfloat16),
-        in_specs=vmem_specs(4),
-        out_specs=pl.BlockSpec(memory_space=pltpu.VMEM),
+        out_shape=(
+            pltpu.VMEM((tokens + EXTRA, weights.shape[1]), jnp.bfloat16),
+            pltpu.VMEM((tokens, tokens), jnp.bfloat16),
+        ),
+        in_specs=vmem_specs(4) + [pl.BlockSpec(memory_space=pltpu.HBM)],
+        out_specs=tuple(vmem_specs(2)),
+        scratch_shapes=[pltpu.SMEM(evicted.shape, evicted.dtype), pltpu.SemaphoreType.DMA(())],
         cost_estimate=HIDES,
         compiler_params=pltpu.CompilerParams(vmem_limit_bytes=8 << 20),
-    )(*map(in_vmem, (weights, inputs, gain, first)))
+    )(*map(in_vmem, (weights, inputs, gain, first)), in_hbm(evicted))
 
 
 def mix_kernel(taken_ref, *refs):
@@ -217,12 +226,19 @@
     reach = sum(ref[:tokens, :].astype(jnp.float32) for ref in reach_refs)
     squares = sum(ref[tokens:, :tokens].astype(jnp.float32) for ref in reach_refs)
     squares = jnp.sum(squares, axis=0, keepdims=True)
-    inner = jnp.sum(flat[...].astype(jnp.float32) * reach, axis=1, keepdims=True)
-    inner = as_row(inner)
+    products = flat[...].astype(jnp.float32) * reach
+    folded = products[:, :LANES]
+    for start in range(LANES, products.shape[1], LANES):
+        folded = folded + products[:, start : start + LANES]
+    ones = jnp.ones((EXTRA, LANES), jnp.bfloat16)
+    inner = sum(product(ones, part.astype(jnp.bfloat16), 1, 1) for part in split(folded))[:1]
     sums_ref[:1, :] = squares
     sums_ref[1:, :] = inner
-    rows = jnp.concatenate([*split(squares), *split(inner), jnp.zeros((2, tokens), jnp.float32)])
-    scaled_ref[:, features:] = standing(rows).astype(scaled_ref.dtype)
+    parts = jnp.concatenate([as_parts(squares, 3), as_parts(inner, EXTRA - 3)])
+    places = chosen(EXTRA, LANES, lambda row, lane: row == lane)
+    scaled_ref[:, features:] = product(parts.astype(jnp.bfloat16), places, 0, 0).astype(
+        scaled_ref.dtype
+    )
 
 
 def project(head_of, blocks, early, weights, inputs, gain, reaches):
@@ -245,23 +261,24 @@
 def finish_kernel(scaled_ref, input_ref, *refs):
     *sums_refs, out_ref, held, sems = refs
     tokens, features = input_ref.shape
-    extra = scaled_ref[:, features:].astype(jnp.float32).T
-    squares = extra[0:1] + extra[1:2] + extra[2:3]
-    inner = extra[3:4] + extra[4:5] + extra[5:6]
+    places = chosen(EXTRA, LANES, lambda row, lane: (lane < 6) & (lane // 3 == row))
+    sums = product(places, scaled_ref[:, features:], 1, 1)[:2]
     for ref in sums_refs:
-        squares = squares + ref[:1, :]
-        inner = inner + ref[1:, :]
-    inv = 1.0 / jnp.sqrt(squares / D + 1e-05)
-    factor = inner * (inv * inv * inv) / D
-    rows = jnp.concatenate([inv, factor, jnp.zeros((6, tokens), jnp.float32)])
-    columns = standing(rows)
-    inv, factor = columns[:, 0:1], columns[:, 1:2]
+        sums = sums + ref[...]
+    inv = 1.0 / jnp.sqrt(sums[:1] / D + 1e-05)
+    factor = sums[1:] * (inv * inv * inv) / D
+    parts = jnp.concatenate([as_parts(inv, 3), as_parts(factor, EXTRA - 3)])
+    spread = chosen(EXTRA, 2 * LANES, lambda row, lane: (row < 6) & (row // 3 == lane // LANES))
+    columns = product(parts.astype(jnp.bfloat16), spread, 0, 0)
+    inv, factor = columns[:, :LANES], columns[:, LANES:]
     copies = []
     for j in range(len(PIECES) - 1):
         part = slice(PIECES[j] * tokens // 8, PIECES[j + 1] * tokens // 8)
-        scaled = scaled_ref[part, :features].astype(jnp.float32)
-        values = input_ref[part, :].astype(jnp.float32)
-        held[part, :] = (scaled * inv[part] - values * factor[part]).astype(held.dtype)
+        for start in range(0, features, LANES):
+            lanes = slice(start, start + LANES)
+            scaled = scaled_ref[part, lanes].astype(jnp.float32)
+            values = input_ref[part, lanes].astype(jnp.float32)
+            held[part, lanes] = (scaled * inv[part] - values * factor[part]).astype(held.dtype)
         copies.append(pltpu.make_async_copy(held.at[part], out_ref.at[part], sems.at[j]))
         copies[-1].start()
     for copy in copies:
@@ -310,14 +327,14 @@
 
 def per_device(grad_attn, w_value, probs_own, probs_spare, evicted, layer_input, gain):
     sections, count = lax.axis_size("section"), lax.axis_size("tp")
-    packed, spares, taken = pack(probs_own[0, 0], grad_attn[0, 0], probs_spare[0, 0], evicted)
+    packed, spares = pack(probs_own[0, 0], grad_attn[0, 0], probs_spare[0, 0])
     heads = []
     for mask in (0, SIDE) if count == 8 else (0,):
         spare = handed_over(spares, sections, count, sections // 2, mask)
         heads.append((swapped(packed, "tp", mask) if mask else packed, spare))
     weights, inputs = w_value[0], layer_input[0]
     next_input = passed_along(inputs, "section", -1)
-    reach = reach_of(weights, inputs, gain, heads[-1][0])
+    reach, taken = reach_of(weights, inputs, gain, heads[-1][0], evicted)
     if count == 8:
         reaches = [reach, swapped(reach, "tp", SIDE)]
         reaches[1], next_input = lax.optimization_barrier((reaches[1], next_input))

time: 27.8 us -> 28.3 us (1.018)
  Pallas kernels: 4.3 us -> 4.69 us
  transfers between devices with their start and end apart: 12 -> 12, of which waited for: 7 -> 6; matrix products, arithmetic and copies ran while one was open for 0% -> 0% of each run, Pallas kernels for 6% -> 6%
where the time goes in v8:
time: 28.3 us; the launch traced here: 27.8 us
  starting transfers between devices  16.7 us (59%)
  waiting for transfers between devices  6.36 us (22%)
  Pallas kernels  4.69 us (17%)
    ppermute x5, starting transfers between devices, swapped(): lax.ppermute(block, axis, [(i ^ mask, i) for i in range(lax.axis_size(axi...  7.62 us
    ppermute x5, starting transfers between devices, handed_over(): return lax.ppermute(block, ('section', 'tp'), route)  5.96 us
    ppermute x5, waiting for transfers between devices, swapped(): lax.ppermute(block, axis, [(i ^ mask, i) for i in range(lax.axis_size(axi...  4.12 us
    ppermute x2, starting transfers between devices, passed_along(): return lax.ppermute(block, axis, route)  3.12 us
    ppermute x5, waiting for transfers between devices, handed_over(): return lax.ppermute(block, ('section', 'tp'), route)  2.19 us
    pallas_call x1, Pallas kernels, finish(): pl.pallas_call(finish_kernel, out_shape=pltpu.HBM(inputs.shape, jnp.bfloa...  1.18 us
    pallas_call x1, Pallas kernels, project(): pl.pallas_call(functools.partial(project_kernel, head_of, (len(blocks), l...  0.99 us
    pallas_call x1, Pallas kernels, pack(): pl.pallas_call(pack_kernel, out_shape=(pltpu.VMEM((2, *own.shape), own.dt...  0.97 us
  transfers between devices with their start and end apart: 12, of which 6 were waited for; matrix products, arithmetic and copies ran while one was open for 0% of the time, Pallas kernels for 6%

profile of v8, /device:TPU:1, one launch (start us, length us, event | category | flops | bytes accessed | tf_op | source)
XLA Modules:
  0.0 27.8 jit_solution(9282923338776256954)
XLA Ops:
  0.0 0.0 copy-start.1
  0.0 0.0 copy-start
  0.0 0.0 copy-start.2
  0.0 1.0 %shard_map.73 = (bf16[2,128,128]{2,1,0:T(8,128)(2,1)S(1)}, bf16[128,128]{1,0:T(8,128)(2,1)S(1)}) custom-call(bf16[128,128]{1,0:T(8,128)(2,1)} %bitcast.12, bf16[128,128]{1,0:T(8,128)(2,1)} %bitcast.13, bf16[128,128]{1,0:T(8,128)(2,1)} %bitcast.14), custom_call_target="tpu_custom_call" | custom-call | flops 34359738368 | bytes 33554432 | tf_op jit(solution)/shard_map/pallas_call | solution.py:81
  1.0 2.1 %collective-permute-start = (bf16[2,128,128]{2,1,0:T(8,128)(2,1)S(1)}, bf16[2,128,128]{2,1,0:T(8,128)(2,1)S(1)}, u32[]{:S(2)}, u32[]{:S(2)}) collective-permute-start(bf16[2,128,128]{2,1,0:T(8,128)(2,1)S(1)} %get-tuple-element.13.refs_3_), channel_id=1, source_target_pairs={{1,0},{0,1},{3,2},{2,3},{5,4},{4,5},{7,6},{6,7},{9,8},{8,9},{11,10... | collective-permute-start | bytes 196616 | tf_op jit(solution)/shard_map/ppermute | solution.py:24
  3.1 1.2 %collective-permute-start.2 = (bf16[128,128]{1,0:T(8,128)(2,1)S(1)}, bf16[128,128]{1,0:T(8,128)(2,1)S(1)}, u32[]{:S(2)}, u32[]{:S(2)}) collective-permute-start(bf16[128,128]{1,0:T(8,128)(2,1)S(1)} %get-tuple-element.15), channel_id=1, source_target_pairs={{17,0},{16,1},{19,2},{18,3},{21,4},{20,5},{23,6},{22,7},{25,8},{24... | collective-permute-start | bytes 98312 | tf_op jit(solution)/shard_map/ppermute | solution.py:313
  4.3 0.1 collective-permute-start.1
  4.4 0.0 copy-done.1
  4.4 1.2 %collective-permute-start.7 = (bf16[128,1536]{1,0:T(8,128)(2,1)S(1)}, bf16[128,1536]{1,0:T(8,128)(2,1)S(1)}, u32[]{:S(2)}, u32[]{:S(2)}) collective-permute-start(bf16[128,1536]{1,0:T(8,128)(2,1)S(1)} %bitcast.9), channel_id=1, source_target_pairs={{8,0},{16,8},{24,16},{0,24},{9,1},{17,9},{25,17},{1,25},{10,2},{18... | collective-permute-start | bytes 1179656 | tf_op jit(solution)/shard_map/ppermute | solution.py:20
  5.6 0.0 collective-permute-done.first_ref.refs_2_
  5.6 0.0 copy-done
  5.6 0.0 copy-done.2
  5.6 0.7 %shard_map.74 = (bf16[144,1024]{1,0:T(8,128)(2,1)S(1)}, bf16[128,128]{1,0:T(8,128)(2,1)S(1)}) custom-call(bf16[1536,1024]{1,0:T(8,128)(2,1)S(1)} %bitcast.6, bf16[128,1536]{1,0:T(8,128)(2,1)S(1)} %bitcast.10, f32[1,1536]{1,0:T(1,128)S(1)} %copy-done.2, bf16[2,128,128]{2,1,0:T(8,128)(2,1)S(1)} %collective-permute-done.first_ref.refs_2_, s32[1,4]{1,0:T(1,128)} %evicted_ref.1), custom_call_target="tpu_custom_call" | custom-call | flops 34359738368 | bytes 33554432 | tf_op jit(solution)/shard_map/pallas_call | solution.py:119
  6.3 1.7 %collective-permute-start.6 = (bf16[144,1024]{1,0:T(8,128)(2,1)S(1)}, bf16[144,1024]{1,0:T(8,128)(2,1)S(1)}, u32[]{:S(2)}, u32[]{:S(2)}) collective-permute-start(bf16[144,1024]{1,0:T(8,128)(2,1)S(1)} %get-tuple-element.16.refs_8_), channel_id=1, source_target_pairs={{1,0},{0,1},{3,2},{2,3},{5,4},{4,5},{7,6},{6,7},{9,8},{8,9},{11,10... | collective-permute-start | bytes 884744 | tf_op jit(solution)/shard_map/ppermute | solution.py:24
  8.1 0.0 collective-permute-done.2.refs_1_
  8.1 0.0 collective-permute-done.1.refs_0_
  8.1 0.2 shard_map.75.refs_0_
  8.3 3.4 %collective-permute-start.3 = (bf16[2,128,128]{2,1,0:T(8,128)(2,1)S(1)}, bf16[2,128,128]{2,1,0:T(8,128)(2,1)S(1)}, u32[]{:S(2)}, u32[]{:S(2)}) collective-permute-start(bf16[2,128,128]{2,1,0:T(8,128)(2,1)S(1)} %shard_map.75.refs_0_), channel_id=1, source_target_pairs={{6,0},{7,1},{4,2},{5,3},{2,4},{3,5},{0,6},{1,7},{14,8},{15,9},{12,... | collective-permute-start | bytes 196616 | tf_op jit(solution)/shard_map/ppermute | solution.py:24
  11.6 0.0 collective-permute-start.5
  11.6 0.4 %collective-permute-start.4 = (bf16[2,128,128]{2,1,0:T(8,128)(2,1)S(1)}, bf16[2,128,128]{2,1,0:T(8,128)(2,1)S(1)}, u32[]{:S(2)}, u32[]{:S(2)}) collective-permute-start(bf16[2,128,128]{2,1,0:T(8,128)(2,1)S(1)} %shard_map.75.refs_0_), channel_id=1, source_target_pairs={{2,0},{3,1},{0,2},{1,3},{6,4},{7,5},{4,6},{5,7},{10,8},{11,9},{8,1... | collective-permute-start | bytes 196616 | tf_op jit(solution)/shard_map/ppermute | solution.py:24
  12.0 1.3 %collective-permute-done.3.refs_1_ = bf16[2,128,128]{2,1,0:T(8,128)(2,1)S(1)} collective-permute-done((bf16[2,128,128]{2,1,0:T(8,128)(2,1)S(1)}, bf16[2,128,128]{2,1,0:T(8,128)(2,1)S(1)}, u32[]{:S(2)}, u32[]{:S(2)}) %collective-permute-start.3) | collective-permute-done | bytes 65568 | tf_op jit(solution)/shard_map/ppermute | solution.py:24
  13.3 0.7 %shard_map.76.refs_4_ = f32[128,1536]{1,0:T(8,128)S(1)} custom-call(bf16[2,128,128]{2,1,0:T(8,128)(2,1)S(1)} %shard_map.75.refs_0_, bf16[2,128,128]{2,1,0:T(8,128)(2,1)S(1)} %collective-permute-done.3.refs_1_, bf16[1536,1024]{1,0:T(8,128)(2,1)S(1)} %bitcast.7), custom_call_target="tpu_custom_call" | custom-call | flops 65536 | bytes 4096 | tf_op jit(solution)/shard_map/pallas_call | solution.py:199
  14.0 0.5 %collective-permute-done.6.refs_9_ = bf16[144,1024]{1,0:T(8,128)(2,1)S(1)} collective-permute-done((bf16[144,1024]{1,0:T(8,128)(2,1)S(1)}, bf16[144,1024]{1,0:T(8,128)(2,1)S(1)}, u32[]{:S(2)}, u32[]{:S(2)}) %collective-permute-start.6) | collective-permute-done | bytes 294944 | tf_op jit(solution)/shard_map/ppermute | solution.py:24
  14.5 0.0 collective-permute-done.7.input_ref
  14.5 2.3 %collective-permute-done.5.refs_3_ = bf16[2,128,128]{2,1,0:T(8,128)(2,1)S(1)} collective-permute-done((bf16[2,128,128]{2,1,0:T(8,128)(2,1)S(1)}, bf16[2,128,128]{2,1,0:T(8,128)(2,1)S(1)}, u32[]{:S(2)}, u32[]{:S(2)}) %collective-permute-start.5) | collective-permute-done | bytes 65568 | tf_op jit(solution)/shard_map/ppermute | solution.py:24
  16.8 0.0 collective-permute-done.4.refs_2_
  16.8 1.0 %shard_map.77 = (bf16[128,1664]{1,0:T(8,128)(2,1)S(1)}, f32[2,128]{1,0:T(2,128)S(1)}) custom-call(bf16[2,128,128]{2,1,0:T(8,128)(2,1)S(1)} %shard_map.75.refs_0_, bf16[2,128,128]{2,1,0:T(8,128)(2,1)S(1)} %collective-permute-done.3.refs_1_, bf16[2,128,128]{2,1,0:T(8,128)(2,1)S(1)} %collective-permute-done.4.refs_2_, ...), custom_call_target="tpu_custom_call" | custom-call | flops 34359738368 | bytes 33554432 | tf_op jit(solution)/shard_map/pallas_call | solution.py:247
  17.8 1.9 %collective-permute-start.8 = (bf16[128,1664]{1,0:T(8,128)(2,1)S(1)}, bf16[128,1664]{1,0:T(8,128)(2,1)S(1)}, u32[]{:S(2)}, u32[]{:S(2)}) collective-permute-start(bf16[128,1664]{1,0:T(8,128)(2,1)S(1)} %get-tuple-element.18), channel_id=1, source_target_pairs={{8,0},{16,8},{24,16},{0,24},{9,1},{17,9},{25,17},{1,25},{10,2},{18... | collective-permute-start | bytes 1277960 | tf_op jit(solution)/shard_map/ppermute | solution.py:20
  19.7 2.0 %collective-permute-start.11 = (f32[2,128]{1,0:T(2,128)S(1)}, f32[2,128]{1,0:T(2,128)S(1)}, u32[]{:S(2)}, u32[]{:S(2)}) collective-permute-start(f32[2,128]{1,0:T(2,128)S(1)} %get-tuple-element.20), channel_id=1, source_target_pairs={{14,0},{15,1},{12,2},{13,3},{10,4},{11,5},{8,6},{9,7},{22,8},{23,9... | collective-permute-start | bytes 3080 | tf_op jit(solution)/shard_map/ppermute | solution.py:313
  21.7 0.7 %collective-permute-start.10 = (f32[2,128]{1,0:T(2,128)S(1)}, f32[2,128]{1,0:T(2,128)S(1)}, u32[]{:S(2)}, u32[]{:S(2)}) collective-permute-start(f32[2,128]{1,0:T(2,128)S(1)} %get-tuple-element.20), channel_id=1, source_target_pairs={{12,0},{13,1},{14,2},{15,3},{8,4},{9,5},{10,6},{11,7},{20,8},{21,9... | collective-permute-start | bytes 3080 | tf_op jit(solution)/shard_map/ppermute | solution.py:313
  22.4 1.9 %collective-permute-start.9 = (f32[2,128]{1,0:T(2,128)S(1)}, f32[2,128]{1,0:T(2,128)S(1)}, u32[]{:S(2)}, u32[]{:S(2)}) collective-permute-start(f32[2,128]{1,0:T(2,128)S(1)} %get-tuple-element.20), channel_id=1, source_target_pairs={{10,0},{11,1},{8,2},{9,3},{14,4},{15,5},{12,6},{13,7},{18,8},{19,9... | collective-permute-start | bytes 3080 | tf_op jit(solution)/shard_map/ppermute | solution.py:313
  24.4 1.0 %collective-permute-done.11.refs_2_ = f32[2,128]{1,0:T(2,128)S(1)} collective-permute-done((f32[2,128]{1,0:T(2,128)S(1)}, f32[2,128]{1,0:T(2,128)S(1)}, u32[]{:S(2)}, u32[]{:S(2)}) %collective-permute-start.11) | collective-permute-done | bytes 1056 | tf_op jit(solution)/shard_map/ppermute | solution.py:313
  25.4 1.1 %collective-permute-done.10.refs_1_ = f32[2,128]{1,0:T(2,128)S(1)} collective-permute-done((f32[2,128]{1,0:T(2,128)S(1)}, f32[2,128]{1,0:T(2,128)S(1)}, u32[]{:S(2)}, u32[]{:S(2)}) %collective-permute-start.10) | collective-permute-done | bytes 1056 | tf_op jit(solution)/shard_map/ppermute | solution.py:313
  26.5 0.1 collective-permute-done.9.refs_0_
  26.6 0.0 collective-permute-done.8.scaled_ref
  26.6 1.2 %shard_map.78 = bf16[128,1536]{1,0:T(8,128)(2,1)} custom-call(bf16[128,1664]{1,0:T(8,128)(2,1)S(1)} %collective-permute-done.8.scaled_ref, bf16[128,1536]{1,0:T(8,128)(2,1)S(1)} %collective-permute-done.7.input_ref, f32[2,128]{1,0:T(2,128)S(1)} %collective-permute-done.9.refs_0_, f32[2,128]{1,0:T(2,128)S(1)} %collective-permute-done.10.refs_1_, ...), custom_call_target="tpu_custom_call" | custom-call | tf_op jit(solution)/shard_map/pallas_call | solution.py:289
Async XLA Ops:
  0.0 4.4 %copy-start.1 = (bf16[1,128,1536]{2,1,0:T(8,128)(2,1)S(1)}, bf16[1,128,1536]{2,1,0:T(8,128)(2,1)}, u32[]{:S(2)}) copy-start(bf16[1,128,1536]{2,1,0:T(8,128)(2,1)} %param.12) | copy-start | bytes 1179652
  0.0 5.6 %copy-start = (bf16[1,1536,1024]{2,1,0:T(8,128)(2,1)S(1)}, bf16[1,1536,1024]{2,1,0:T(8,128)(2,1)}, u32[]{:S(2)}) copy-start(bf16[1,1536,1024]{2,1,0:T(8,128)(2,1)} %param.8) | copy-start | bytes 9437188
  0.0 5.6 %copy-start.2 = (f32[1,1536]{1,0:T(1,128)S(1)}, f32[1,1536]{1,0:T(1,128)}, u32[]{:S(2)}) copy-start(f32[1,1536]{1,0:T(1,128)} %refs_7_.1) | copy-start | bytes 18436
  1.0 4.6 %collective-permute-start = (bf16[2,128,128]{2,1,0:T(8,128)(2,1)S(1)}, bf16[2,128,128]{2,1,0:T(8,128)(2,1)S(1)}, u32[]{:S(2)}, u32[]{:S(2)}) collective-permute-start(bf16[2,128,128]{2,1,0:T(8,128)(2,1)S(1)} %get-tuple-element.13.refs_3_), channel_id=1, source_target_pairs={{1,0},{0,1},{3,2},{2,3},{5,4},{4,5},{7,6},{6,7},{9,8},{8,9},{11,10... | collective-permute-start | bytes 196616 | tf_op jit(solution)/shard_map/ppermute | solution.py:24
  3.1 4.9 %collective-permute-start.2 = (bf16[128,128]{1,0:T(8,128)(2,1)S(1)}, bf16[128,128]{1,0:T(8,128)(2,1)S(1)}, u32[]{:S(2)}, u32[]{:S(2)}) collective-permute-start(bf16[128,128]{1,0:T(8,128)(2,1)S(1)} %get-tuple-element.15), channel_id=1, source_target_pairs={{17,0},{16,1},{19,2},{18,3},{21,4},{20,5},{23,6},{22,7},{25,8},{24... | collective-permute-start | bytes 98312 | tf_op jit(solution)/shard_map/ppermute | solution.py:313
  4.3 3.8 %collective-permute-start.1 = (bf16[128,128]{1,0:T(8,128)(2,1)S(1)}, bf16[128,128]{1,0:T(8,128)(2,1)S(1)}, u32[]{:S(2)}, u32[]{:S(2)}) collective-permute-start(bf16[128,128]{1,0:T(8,128)(2,1)S(1)} %get-tuple-element.15), channel_id=1, source_target_pairs={{16,0},{17,1},{18,2},{19,3},{20,4},{21,5},{22,6},{23,7},{24,8},{25... | collective-permute-start | bytes 98312 | tf_op jit(solution)/shard_map/ppermute | solution.py:313
  4.4 10.1 %collective-permute-start.7 = (bf16[128,1536]{1,0:T(8,128)(2,1)S(1)}, bf16[128,1536]{1,0:T(8,128)(2,1)S(1)}, u32[]{:S(2)}, u32[]{:S(2)}) collective-permute-start(bf16[128,1536]{1,0:T(8,128)(2,1)S(1)} %bitcast.9), channel_id=1, source_target_pairs={{8,0},{16,8},{24,16},{0,24},{9,1},{17,9},{25,17},{1,25},{10,2},{18... | collective-permute-start | bytes 1179656 | tf_op jit(solution)/shard_map/ppermute | solution.py:20
  6.3 8.1 %collective-permute-start.6 = (bf16[144,1024]{1,0:T(8,128)(2,1)S(1)}, bf16[144,1024]{1,0:T(8,128)(2,1)S(1)}, u32[]{:S(2)}, u32[]{:S(2)}) collective-permute-start(bf16[144,1024]{1,0:T(8,128)(2,1)S(1)} %get-tuple-element.16.refs_8_), channel_id=1, source_target_pairs={{1,0},{0,1},{3,2},{2,3},{5,4},{4,5},{7,6},{6,7},{9,8},{8,9},{11,10... | collective-permute-start | bytes 884744 | tf_op jit(solution)/shard_map/ppermute | solution.py:24
  8.3 5.0 %collective-permute-start.3 = (bf16[2,128,128]{2,1,0:T(8,128)(2,1)S(1)}, bf16[2,128,128]{2,1,0:T(8,128)(2,1)S(1)}, u32[]{:S(2)}, u32[]{:S(2)}) collective-permute-start(bf16[2,128,128]{2,1,0:T(8,128)(2,1)S(1)} %shard_map.75.refs_0_), channel_id=1, source_target_pairs={{6,0},{7,1},{4,2},{5,3},{2,4},{3,5},{0,6},{1,7},{14,8},{15,9},{12,... | collective-permute-start | bytes 196616 | tf_op jit(solution)/shard_map/ppermute | solution.py:24
  11.6 5.2 %collective-permute-start.5 = (bf16[2,128,128]{2,1,0:T(8,128)(2,1)S(1)}, bf16[2,128,128]{2,1,0:T(8,128)(2,1)S(1)}, u32[]{:S(2)}, u32[]{:S(2)}) collective-permute-start(bf16[2,128,128]{2,1,0:T(8,128)(2,1)S(1)} %shard_map.75.refs_0_), channel_id=1, source_target_pairs={{4,0},{5,1},{6,2},{7,3},{0,4},{1,5},{2,6},{3,7},{12,8},{13,9},{14,... | collective-permute-start | bytes 196616 | tf_op jit(solution)/shard_map/ppermute | solution.py:24
  11.6 5.2 %collective-permute-start.4 = (bf16[2,128,128]{2,1,0:T(8,128)(2,1)S(1)}, bf16[2,128,128]{2,1,0:T(8,128)(2,1)S(1)}, u32[]{:S(2)}, u32[]{:S(2)}) collective-permute-start(bf16[2,128,128]{2,1,0:T(8,128)(2,1)S(1)} %shard_map.75.refs_0_), channel_id=1, source_target_pairs={{2,0},{3,1},{0,2},{1,3},{6,4},{7,5},{4,6},{5,7},{10,8},{11,9},{8,1... | collective-permute-start | bytes 196616 | tf_op jit(solution)/shard_map/ppermute | solution.py:24
  17.8 8.8 %collective-permute-start.8 = (bf16[128,1664]{1,0:T(8,128)(2,1)S(1)}, bf16[128,1664]{1,0:T(8,128)(2,1)S(1)}, u32[]{:S(2)}, u32[]{:S(2)}) collective-permute-start(bf16[128,1664]{1,0:T(8,128)(2,1)S(1)} %get-tuple-element.18), channel_id=1, source_target_pairs={{8,0},{16,8},{24,16},{0,24},{9,1},{17,9},{25,17},{1,25},{10,2},{18... | collective-permute-start | bytes 1277960 | tf_op jit(solution)/shard_map/ppermute | solution.py:20
  19.7 5.7 %collective-permute-start.11 = (f32[2,128]{1,0:T(2,128)S(1)}, f32[2,128]{1,0:T(2,128)S(1)}, u32[]{:S(2)}, u32[]{:S(2)}) collective-permute-start(f32[2,128]{1,0:T(2,128)S(1)} %get-tuple-element.20), channel_id=1, source_target_pairs={{14,0},{15,1},{12,2},{13,3},{10,4},{11,5},{8,6},{9,7},{22,8},{23,9... | collective-permute-start | bytes 3080 | tf_op jit(solution)/shard_map/ppermute | solution.py:313
  21.7 4.8 %collective-permute-start.10 = (f32[2,128]{1,0:T(2,128)S(1)}, f32[2,128]{1,0:T(2,128)S(1)}, u32[]{:S(2)}, u32[]{:S(2)}) collective-permute-start(f32[2,128]{1,0:T(2,128)S(1)} %get-tuple-element.20), channel_id=1, source_target_pairs={{12,0},{13,1},{14,2},{15,3},{8,4},{9,5},{10,6},{11,7},{20,8},{21,9... | collective-permute-start | bytes 3080 | tf_op jit(solution)/shard_map/ppermute | solution.py:313
  22.4 4.1 %collective-permute-start.9 = (f32[2,128]{1,0:T(2,128)S(1)}, f32[2,128]{1,0:T(2,128)S(1)}, u32[]{:S(2)}, u32[]{:S(2)}) collective-permute-start(f32[2,128]{1,0:T(2,128)S(1)} %get-tuple-element.20), channel_id=1, source_target_pairs={{10,0},{11,1},{8,2},{9,3},{14,4},{15,5},{12,6},{13,7},{18,8},{19,9... | collective-permute-start | bytes 3080 | tf_op jit(solution)/shard_map/ppermute | solution.py:313

commit v9 on v6

--- a/solution.py
+++ b/solution.py
@@ -124,20 +124,22 @@
 def mix_kernel(taken_ref, *refs):
     out_ref = refs[-1]
     taken = taken_ref[...]
-    for j in range(out_ref.shape[0]):
+    for j in range(out_ref.shape[1]):
         packed_ref, spare_ref = refs[len(refs) - 2 - j], refs[j]
-        out_ref[j] = lax.dot_general(
+        value = lax.dot_general(
             packed_ref[0] * (1 - taken) + spare_ref[...] * taken,
             packed_ref[1],
             (((0,), (0,)), ((), ())),
             preferred_element_type=jnp.float32,
         ).astype(out_ref.dtype)
-
-
-def value_gradients(taken, heads):
+        for copy in range(out_ref.shape[0]):
+            out_ref[copy, j] = value
+
+
+def value_gradients(taken, heads, copies):
     return pl.pallas_call(
         mix_kernel,
-        out_shape=pltpu.VMEM((len(heads), *heads[0][1].shape), jnp.bfloat16),
+        out_shape=pltpu.VMEM((copies, len(heads), *heads[0][1].shape), jnp.bfloat16),
         in_specs=vmem_specs(1 + 2 * len(heads)),
         out_specs=pl.BlockSpec(memory_space=pltpu.VMEM),
         cost_estimate=HIDES,
@@ -296,16 +298,17 @@
     return lax.ppermute(block, ("section", "tp"), route)
 
 
-def gathered(pair, axis):
-    if lax.axis_size(axis) != 8:
-        return [lax.all_gather(pair[0], axis)], lambda place: place
-    blocks = [pair] + [swapped(pair, axis, mask) for mask in LINE]
-    masks = [far | side for far in (0, *LINE) for side in (0, SIDE)]
+def gathered(pairs, axis):
+    if pairs.shape[0] == 1:
+        return [lax.all_gather(pairs[0, 0], axis)], lambda place: place
+    count = lax.axis_size(axis)
+    groups = [[i for i in range(count) if i % 2 == side] for side in range(2)]
+    blocks = lax.all_to_all(pairs, axis, 0, 0, axis_index_groups=groups, tiled=True)
 
     def head_of(place):
-        return lax.axis_index(axis) ^ masks[place]
-
-    return blocks, head_of
+        return (place - place % 2) + (lax.rem(lax.axis_index(axis), 2) ^ (place % 2))
+
+    return [blocks.reshape(count, *blocks.shape[2:])], head_of
 
 
 def per_device(grad_attn, w_value, probs_own, probs_spare, evicted, layer_input, gain):
@@ -323,9 +326,9 @@
         reaches[1], next_input = lax.optimization_barrier((reaches[1], next_input))
     else:
         reaches = [lax.psum(reach, "tp")]
-    pair = value_gradients(taken, heads)
-    blocks, head_of = gathered(pair, "tp")
-    early = [project_early(head_of, blocks[:EARLY], weights)] if count == 8 else []
+    pairs = value_gradients(taken, heads, count // 2 if count == 8 else 1)
+    blocks, head_of = gathered(pairs, "tp")
+    early = []
     scaled, sums = project(head_of, blocks, early, weights, inputs, gain, reaches)
     next_scaled = passed_along(scaled, "section", -1)
     next_sums = []

time: 27.8 us -> 37.2 us (1.34)
  local copies, waits for them, and re-layouts: 0.01 us -> 3.79 us
  waiting for transfers between devices: 6.36 us -> 9.88 us
  starting transfers between devices: 16.7 us -> 18.5 us
    all_to_all x0 -> x1, starting transfers between devices: none -> 4.61 us  [gathered(): lax.all_to_all(pairs, axis, 0, 0, axis_index_groups=groups, tiled=True)]
    ppermute x5 -> x2, starting transfers between devices: 7.61 us -> 3.73 us  [swapped(): lax.ppermute(block, axis, [(i ^ mask, i) for i in range(lax.axis_size(axi...]
    unnamed x6 -> x8, local copies, waits for them, and re-layouts: 0.01 us -> 3.79 us
    ppermute x5, waiting for transfers between devices: 2.15 us -> 5.29 us  [handed_over(): return lax.ppermute(block, ('section', 'tp'), route)]
    ppermute x2, starting transfers between devices: 3.14 us -> 4.65 us  [passed_along(): return lax.ppermute(block, axis, route)]
    ppermute x5 -> x2, waiting for transfers between devices: 4.12 us -> 4.59 us  [swapped(): lax.ppermute(block, axis, [(i ^ mask, i) for i in range(lax.axis_size(axi...]
    pallas_call x1, Pallas kernels: 0.75 us -> 1.2 us  [project(): pl.pallas_call(functools.partial(project_kernel, head_of, (len(blocks), l...]
    ppermute x5, starting transfers between devices: 5.96 us -> 5.56 us  [handed_over(): return lax.ppermute(block, ('section', 'tp'), route)]
  transfers between devices with their start and end apart: 12 -> 10, of which waited for: 7 -> 5; matrix products, arithmetic and copies ran while one was open for 0% -> 0% of each run, Pallas kernels for 6% -> 4%
where the time goes in v9:
time: 37.2 us; the launch traced here: 36.9 us
  starting transfers between devices  18.5 us (50%)
  waiting for transfers between devices  9.88 us (27%)
  Pallas kernels  4.65 us (12%)
  local copies, waits for them, and re-layouts  3.79 us (10%)
    ppermute x5, starting transfers between devices, handed_over(): return lax.ppermute(block, ('section', 'tp'), route)  5.56 us
    ppermute x5, waiting for transfers between devices, handed_over(): return lax.ppermute(block, ('section', 'tp'), route)  5.29 us
    ppermute x2, starting transfers between devices, passed_along(): return lax.ppermute(block, axis, route)  4.65 us
    all_to_all x1, starting transfers between devices, gathered(): lax.all_to_all(pairs, axis, 0, 0, axis_index_groups=groups, tiled=True)  4.61 us
    ppermute x2, waiting for transfers between devices, swapped(): lax.ppermute(block, axis, [(i ^ mask, i) for i in range(lax.axis_size(axi...  4.59 us
    unnamed x8, local copies, waits for them, and re-layouts  3.79 us
    ppermute x2, starting transfers between devices, swapped(): lax.ppermute(block, axis, [(i ^ mask, i) for i in range(lax.axis_size(axi...  3.73 us
    pallas_call x1, Pallas kernels, project(): pl.pallas_call(functools.partial(project_kernel, head_of, (len(blocks), l...  1.2 us
  transfers between devices with their start and end apart: 10, of which 5 were waited for; matrix products, arithmetic and copies ran while one was open for 0% of the time, Pallas kernels for 4%

profile of v9, /device:TPU:1, one launch (start us, length us, event | category | flops | bytes accessed | tf_op | source)
XLA Modules:
  0.0 36.9 jit_solution(16072214495161289326)
XLA Ops:
  0.0 0.0 copy-start.2
  0.0 0.9 %shard_map.73 = (bf16[2,128,128]{2,1,0:T(8,128)(2,1)S(1)}, bf16[128,128]{1,0:T(8,128)(2,1)S(1)}, bf16[128,128]{1,0:T(8,128)(2,1)S(1)}) custom-call(bf16[128,128]{1,0:T(8,128)(2,1)} %bitcast.13, bf16[128,128]{1,0:T(8,128)(2,1)} %bitcast.14, bf16[128,128]{1,0:T(8,128)(2,1)} %bitcast.15, s32[1,4]{1,0:T(1,128)} %evicted_ref.1), custom_call_target="tpu_custom_call" | custom-call | flops 34359738368 | bytes 33554432 | tf_op jit(solution)/shard_map/pallas_call | solution.py:83
  0.9 2.1 %collective-permute-start.2 = (bf16[2,128,128]{2,1,0:T(8,128)(2,1)S(1)}, bf16[2,128,128]{2,1,0:T(8,128)(2,1)S(1)}, u32[]{:S(2)}, u32[]{:S(2)}) collective-permute-start(bf16[2,128,128]{2,1,0:T(8,128)(2,1)S(1)} %get-tuple-element.14.refs_3_), channel_id=1, source_target_pairs={{1,0},{0,1},{3,2},{2,3},{5,4},{4,5},{7,6},{6,7},{9,8},{8,9},{11,10... | collective-permute-start | bytes 196616 | tf_op jit(solution)/shard_map/ppermute | solution.py:24
  3.0 1.2 %collective-permute-start.1 = (bf16[128,128]{1,0:T(8,128)(2,1)S(1)}, bf16[128,128]{1,0:T(8,128)(2,1)S(1)}, u32[]{:S(2)}, u32[]{:S(2)}) collective-permute-start(bf16[128,128]{1,0:T(8,128)(2,1)S(1)} %get-tuple-element.13), channel_id=1, source_target_pairs={{17,0},{16,1},{19,2},{18,3},{21,4},{20,5},{23,6},{22,7},{25,8},{24... | collective-permute-start | bytes 98312 | tf_op jit(solution)/shard_map/ppermute | solution.py:298
  4.2 0.1 collective-permute-start
  4.3 0.0 copy-done.2
  4.3 1.2 %collective-permute-start.4 = (bf16[128,1536]{1,0:T(8,128)(2,1)S(1)}, bf16[128,1536]{1,0:T(8,128)(2,1)S(1)}, u32[]{:S(2)}, u32[]{:S(2)}) collective-permute-start(bf16[128,1536]{1,0:T(8,128)(2,1)S(1)} %bitcast.10), channel_id=1, source_target_pairs={{8,0},{16,8},{24,16},{0,24},{9,1},{17,9},{25,17},{1,25},{10,2},{18... | collective-permute-start | bytes 1179656 | tf_op jit(solution)/shard_map/ppermute | solution.py:20
  5.5 1.2 %collective-permute-done.1.refs_1_ = bf16[128,128]{1,0:T(8,128)(2,1)S(1)} collective-permute-done((bf16[128,128]{1,0:T(8,128)(2,1)S(1)}, bf16[128,128]{1,0:T(8,128)(2,1)S(1)}, u32[]{:S(2)}, u32[]{:S(2)}) %collective-permute-start.1) | collective-permute-done | bytes 32800 | tf_op jit(solution)/shard_map/ppermute | solution.py:298
  6.7 0.4 %collective-permute-done.refs_0_ = bf16[128,128]{1,0:T(8,128)(2,1)S(1)} collective-permute-done((bf16[128,128]{1,0:T(8,128)(2,1)S(1)}, bf16[128,128]{1,0:T(8,128)(2,1)S(1)}, u32[]{:S(2)}, u32[]{:S(2)}) %collective-permute-start) | collective-permute-done | bytes 32800 | tf_op jit(solution)/shard_map/ppermute | solution.py:298
  7.1 0.0 collective-permute-done.2.refs_2_.first_ref
  7.1 0.0 copy-start.3
  7.1 0.9 %shard_map.74 = bf16[4,2,128,128]{3,2,1,0:T(8,128)(2,1)} custom-call(bf16[128,128]{1,0:T(8,128)(2,1)S(1)} %get-tuple-element.12.taken_ref, bf16[128,128]{1,0:T(8,128)(2,1)S(1)} %collective-permute-done.refs_0_, bf16[128,128]{1,0:T(8,128)(2,1)S(1)} %collective-permute-done.1.refs_1_, bf16[2,128,128]{2,1,0:T(8,128)(2,1)S(1)} %collective-permute-done.2.refs_2_.first_ref, ...), custom_call_target="tpu_custom_call" | custom-call | flops 34359738368 | bytes 33554432 | tf_op jit(solution)/shard_map/pallas_call | solution.py:140
  8.0 4.6 %all-to-all-start = ((bf16[4,2,128,128]{3,2,1,0:T(8,128)(2,1)}), bf16[4,2,128,128]{3,2,1,0:T(8,128)(2,1)S(1)}, u32[]{:S(2)}, u32[]{:S(2)}) async-start(bf16[4,2,128,128]{3,2,1,0:T(8,128)(2,1)} %shard_map.74), calls=%async_computation | async-start | bytes 524288 | tf_op jit(solution)/shard_map/all_to_all | solution.py:306
  12.6 0.0 copy-done.3
  12.6 0.0 copy-start
  12.6 1.9 %copy-done = bf16[1,1536,1024]{2,1,0:T(8,128)(2,1)S(1)} copy-done((bf16[1,1536,1024]{2,1,0:T(8,128)(2,1)S(1)}, bf16[1,1536,1024]{2,1,0:T(8,128)(2,1)}, u32[]{:S(2)}) %copy-start) | copy-done | bytes 3145752
  14.5 0.6 %shard_map.75.refs_4_ = bf16[144,1024]{1,0:T(8,128)(2,1)S(1)} custom-call(bf16[1536,1024]{1,0:T(8,128)(2,1)S(1)} %bitcast.8, bf16[128,1536]{1,0:T(8,128)(2,1)S(1)} %bitcast.11, f32[1,1536]{1,0:T(1,128)S(1)} %copy-done.3, bf16[2,128,128]{2,1,0:T(8,128)(2,1)S(1)} %collective-permute-done.2.refs_2_.first_ref), custom_call_target="tpu_custom_call" | custom-call | flops 34359738368 | bytes 33554432 | tf_op jit(solution)/shard_map/pallas_call | solution.py:114
  15.1 1.6 %collective-permute-start.3 = (bf16[144,1024]{1,0:T(8,128)(2,1)S(1)}, bf16[144,1024]{1,0:T(8,128)(2,1)S(1)}, u32[]{:S(2)}, u32[]{:S(2)}) collective-permute-start(bf16[144,1024]{1,0:T(8,128)(2,1)S(1)} %shard_map.75.refs_4_), channel_id=1, source_target_pairs={{1,0},{0,1},{3,2},{2,3},{5,4},{4,5},{7,6},{6,7},{9,8},{8,9},{11,10... | collective-permute-start | bytes 884744 | tf_op jit(solution)/shard_map/ppermute | solution.py:24
  16.7 4.6 %collective-permute-done.3.refs_5_ = bf16[144,1024]{1,0:T(8,128)(2,1)S(1)} collective-permute-done((bf16[144,1024]{1,0:T(8,128)(2,1)S(1)}, bf16[144,1024]{1,0:T(8,128)(2,1)S(1)}, u32[]{:S(2)}, u32[]{:S(2)}) %collective-permute-start.3) | collective-permute-done | bytes 294944 | tf_op jit(solution)/shard_map/ppermute | solution.py:24
  21.3 0.0 collective-permute-done.4.input_ref
  21.3 0.0 all-to-all-done
  21.3 0.0 copy-start.1
  21.3 1.9 %copy-done.1 = bf16[1,1536,1024]{2,1,0:T(8,128)(2,1)S(1)} copy-done((bf16[1,1536,1024]{2,1,0:T(8,128)(2,1)S(1)}, bf16[1,1536,1024]{2,1,0:T(8,128)(2,1)}, u32[]{:S(2)}) %copy-start.1) | copy-done | bytes 3145752
  23.2 1.2 %shard_map.76 = (bf16[128,1664]{1,0:T(8,128)(2,1)S(1)}, f32[2,128]{1,0:T(2,128)S(1)}) custom-call(bf16[8,128,128]{2,1,0:T(8,128)(2,1)S(1)} %bitcast.7, bf16[1536,1024]{1,0:T(8,128)(2,1)S(1)} %bitcast.9, bf16[128,1536]{1,0:T(8,128)(2,1)S(1)} %bitcast.12, f32[1,1536]{1,0:T(1,128)S(1)} %copy-done.3, bf16[144,1024]{1,0:T(8,128)(2,1)S(1)} %shard_map.75.refs_4_, ...), custom_call_target="tpu_custom_call" | custom-call | flops 34359738368 | bytes 33554432 | tf_op jit(solution)/shard_map/pallas_call | solution.py:233
  24.4 3.4 %collective-permute-start.5 = (bf16[128,1664]{1,0:T(8,128)(2,1)S(1)}, bf16[128,1664]{1,0:T(8,128)(2,1)S(1)}, u32[]{:S(2)}, u32[]{:S(2)}) collective-permute-start(bf16[128,1664]{1,0:T(8,128)(2,1)S(1)} %get-tuple-element.16), channel_id=1, source_target_pairs={{8,0},{16,8},{24,16},{0,24},{9,1},{17,9},{25,17},{1,25},{10,2},{18... | collective-permute-start | bytes 1277960 | tf_op jit(solution)/shard_map/ppermute | solution.py:20
  27.8 3.2 %collective-permute-start.8 = (f32[2,128]{1,0:T(2,128)S(1)}, f32[2,128]{1,0:T(2,128)S(1)}, u32[]{:S(2)}, u32[]{:S(2)}) collective-permute-start(f32[2,128]{1,0:T(2,128)S(1)} %get-tuple-element.18), channel_id=1, source_target_pairs={{14,0},{15,1},{12,2},{13,3},{10,4},{11,5},{8,6},{9,7},{22,8},{23,9... | collective-permute-start | bytes 3080 | tf_op jit(solution)/shard_map/ppermute | solution.py:298
  31.0 0.2 collective-permute-start.7
  31.2 0.9 %collective-permute-start.6 = (f32[2,128]{1,0:T(2,128)S(1)}, f32[2,128]{1,0:T(2,128)S(1)}, u32[]{:S(2)}, u32[]{:S(2)}) collective-permute-start(f32[2,128]{1,0:T(2,128)S(1)} %get-tuple-element.18), channel_id=1, source_target_pairs={{10,0},{11,1},{8,2},{9,3},{14,4},{15,5},{12,6},{13,7},{18,8},{19,9... | collective-permute-start | bytes 3080 | tf_op jit(solution)/shard_map/ppermute | solution.py:298
  32.1 1.4 %collective-permute-done.8.refs_2_ = f32[2,128]{1,0:T(2,128)S(1)} collective-permute-done((f32[2,128]{1,0:T(2,128)S(1)}, f32[2,128]{1,0:T(2,128)S(1)}, u32[]{:S(2)}, u32[]{:S(2)}) %collective-permute-start.8) | collective-permute-done | bytes 1056 | tf_op jit(solution)/shard_map/ppermute | solution.py:298
  33.5 2.3 %collective-permute-done.7.refs_1_ = f32[2,128]{1,0:T(2,128)S(1)} collective-permute-done((f32[2,128]{1,0:T(2,128)S(1)}, f32[2,128]{1,0:T(2,128)S(1)}, u32[]{:S(2)}, u32[]{:S(2)}) %collective-permute-start.7) | collective-permute-done | bytes 1056 | tf_op jit(solution)/shard_map/ppermute | solution.py:298
  35.8 0.0 collective-permute-done.6.refs_0_
  35.8 0.0 collective-permute-done.5.scaled_ref
  35.8 1.1 %shard_map.77 = bf16[128,1536]{1,0:T(8,128)(2,1)} custom-call(bf16[128,1664]{1,0:T(8,128)(2,1)S(1)} %collective-permute-done.5.scaled_ref, bf16[128,1536]{1,0:T(8,128)(2,1)S(1)} %collective-permute-done.4.input_ref, f32[2,128]{1,0:T(2,128)S(1)} %collective-permute-done.6.refs_0_, f32[2,128]{1,0:T(2,128)S(1)} %collective-permute-done.7.refs_1_, ...), custom_call_target="tpu_custom_call" | custom-call | tf_op jit(solution)/shard_map/pallas_call | solution.py:274
Async XLA Ops:
  0.0 4.3 %copy-start.2 = (bf16[1,128,1536]{2,1,0:T(8,128)(2,1)S(1)}, bf16[1,128,1536]{2,1,0:T(8,128)(2,1)}, u32[]{:S(2)}) copy-start(bf16[1,128,1536]{2,1,0:T(8,128)(2,1)} %param.12) | copy-start | bytes 1179652
  0.9 6.2 %collective-permute-start.2 = (bf16[2,128,128]{2,1,0:T(8,128)(2,1)S(1)}, bf16[2,128,128]{2,1,0:T(8,128)(2,1)S(1)}, u32[]{:S(2)}, u32[]{:S(2)}) collective-permute-start(bf16[2,128,128]{2,1,0:T(8,128)(2,1)S(1)} %get-tuple-element.14.refs_3_), channel_id=1, source_target_pairs={{1,0},{0,1},{3,2},{2,3},{5,4},{4,5},{7,6},{6,7},{9,8},{8,9},{11,10... | collective-permute-start | bytes 196616 | tf_op jit(solution)/shard_map/ppermute | solution.py:24
  3.0 3.7 %collective-permute-start.1 = (bf16[128,128]{1,0:T(8,128)(2,1)S(1)}, bf16[128,128]{1,0:T(8,128)(2,1)S(1)}, u32[]{:S(2)}, u32[]{:S(2)}) collective-permute-start(bf16[128,128]{1,0:T(8,128)(2,1)S(1)} %get-tuple-element.13), channel_id=1, source_target_pairs={{17,0},{16,1},{19,2},{18,3},{21,4},{20,5},{23,6},{22,7},{25,8},{24... | collective-permute-start | bytes 98312 | tf_op jit(solution)/shard_map/ppermute | solution.py:298
  4.2 2.9 %collective-permute-start = (bf16[128,128]{1,0:T(8,128)(2,1)S(1)}, bf16[128,128]{1,0:T(8,128)(2,1)S(1)}, u32[]{:S(2)}, u32[]{:S(2)}) collective-permute-start(bf16[128,128]{1,0:T(8,128)(2,1)S(1)} %get-tuple-element.13), channel_id=1, source_target_pairs={{16,0},{17,1},{18,2},{19,3},{20,4},{21,5},{22,6},{23,7},{24,8},{25... | collective-permute-start | bytes 98312 | tf_op jit(solution)/shard_map/ppermute | solution.py:298
  4.3 17.0 %collective-permute-start.4 = (bf16[128,1536]{1,0:T(8,128)(2,1)S(1)}, bf16[128,1536]{1,0:T(8,128)(2,1)S(1)}, u32[]{:S(2)}, u32[]{:S(2)}) collective-permute-start(bf16[128,1536]{1,0:T(8,128)(2,1)S(1)} %bitcast.10), channel_id=1, source_target_pairs={{8,0},{16,8},{24,16},{0,24},{9,1},{17,9},{25,17},{1,25},{10,2},{18... | collective-permute-start | bytes 1179656 | tf_op jit(solution)/shard_map/ppermute | solution.py:20
  7.1 5.5 %copy-start.3 = (f32[1,1536]{1,0:T(1,128)S(1)}, f32[1,1536]{1,0:T(1,128)}, u32[]{:S(2)}) copy-start(f32[1,1536]{1,0:T(1,128)} %refs_3_.1) | copy-start | bytes 18436
  8.0 13.3 %all-to-all-start = ((bf16[4,2,128,128]{3,2,1,0:T(8,128)(2,1)}), bf16[4,2,128,128]{3,2,1,0:T(8,128)(2,1)S(1)}, u32[]{:S(2)}, u32[]{:S(2)}) async-start(bf16[4,2,128,128]{3,2,1,0:T(8,128)(2,1)} %shard_map.74), calls=%async_computation | async-start | bytes 524288 | tf_op jit(solution)/shard_map/all_to_all | solution.py:306
  12.6 1.9 %copy-start = (bf16[1,1536,1024]{2,1,0:T(8,128)(2,1)S(1)}, bf16[1,1536,1024]{2,1,0:T(8,128)(2,1)}, u32[]{:S(2)}) copy-start(bf16[1,1536,1024]{2,1,0:T(8,128)(2,1)} %param.8) | copy-start | bytes 9437188
  15.1 6.2 %collective-permute-start.3 = (bf16[144,1024]{1,0:T(8,128)(2,1)S(1)}, bf16[144,1024]{1,0:T(8,128)(2,1)S(1)}, u32[]{:S(2)}, u32[]{:S(2)}) collective-permute-start(bf16[144,1024]{1,0:T(8,128)(2,1)S(1)} %shard_map.75.refs_4_), channel_id=1, source_target_pairs={{1,0},{0,1},{3,2},{2,3},{5,4},{4,5},{7,6},{6,7},{9,8},{8,9},{11,10... | collective-permute-start | bytes 884744 | tf_op jit(solution)/shard_map/ppermute | solution.py:24
  21.3 1.9 %copy-start.1 = (bf16[1,1536,1024]{2,1,0:T(8,128)(2,1)S(1)}, bf16[1,1536,1024]{2,1,0:T(8,128)(2,1)}, u32[]{:S(2)}) copy-start(bf16[1,1536,1024]{2,1,0:T(8,128)(2,1)} %param.8) | copy-start | bytes 9437188
  24.4 11.5 %collective-permute-start.5 = (bf16[128,1664]{1,0:T(8,128)(2,1)S(1)}, bf16[128,1664]{1,0:T(8,128)(2,1)S(1)}, u32[]{:S(2)}, u32[]{:S(2)}) collective-permute-start(bf16[128,1664]{1,0:T(8,128)(2,1)S(1)} %get-tuple-element.16), channel_id=1, source_target_pairs={{8,0},{16,8},{24,16},{0,24},{9,1},{17,9},{25,17},{1,25},{10,2},{18... | collective-permute-start | bytes 1277960 | tf_op jit(solution)/shard_map/ppermute | solution.py:20
  27.8 5.7 %collective-permute-start.8 = (f32[2,128]{1,0:T(2,128)S(1)}, f32[2,128]{1,0:T(2,128)S(1)}, u32[]{:S(2)}, u32[]{:S(2)}) collective-permute-start(f32[2,128]{1,0:T(2,128)S(1)} %get-tuple-element.18), channel_id=1, source_target_pairs={{14,0},{15,1},{12,2},{13,3},{10,4},{11,5},{8,6},{9,7},{22,8},{23,9... | collective-permute-start | bytes 3080 | tf_op jit(solution)/shard_map/ppermute | solution.py:298
  31.0 4.8 %collective-permute-start.7 = (f32[2,128]{1,0:T(2,128)S(1)}, f32[2,128]{1,0:T(2,128)S(1)}, u32[]{:S(2)}, u32[]{:S(2)}) collective-permute-start(f32[2,128]{1,0:T(2,128)S(1)} %get-tuple-element.18), channel_id=1, source_target_pairs={{12,0},{13,1},{14,2},{15,3},{8,4},{9,5},{10,6},{11,7},{20,8},{21,9... | collective-permute-start | bytes 3080 | tf_op jit(solution)/shard_map/ppermute | solution.py:298
  31.2 4.6 %collective-permute-start.6 = (f32[2,128]{1,0:T(2,128)S(1)}, f32[2,128]{1,0:T(2,128)S(1)}, u32[]{:S(2)}, u32[]{:S(2)}) collective-permute-start(f32[2,128]{1,0:T(2,128)S(1)} %get-tuple-element.18), channel_id=1, source_target_pairs={{10,0},{11,1},{8,2},{9,3},{14,4},{15,5},{12,6},{13,7},{18,8},{19,9... | collective-permute-start | bytes 3080 | tf_op jit(solution)/shard_map/ppermute | solution.py:298

commit v10 on v6

--- a/solution.py
+++ b/solution.py
@@ -51,6 +51,10 @@
         parts.append(values.astype(jnp.bfloat16).astype(jnp.float32))
         values = values - parts[-1]
     return parts
+
+
+def own_ratio(squares, inner):
+    return inner / jnp.maximum(squares, 1e-30)
 
 
 def as_parts(row):
@@ -98,7 +102,7 @@
     )(*map(in_hbm, (own, grad, spare, evicted)))
 
 
-def reach_kernel(weight_ref, input_ref, gain_ref, first_ref, reach_ref):
+def reach_kernel(weight_ref, input_ref, gain_ref, first_ref, reach_ref, own_ref):
     del first_ref
     tokens, features = input_ref.shape
     values = input_ref[...].astype(jnp.float32)
@@ -108,14 +112,19 @@
     gained = (values * gain_ref[...]).astype(jnp.bfloat16)
     reach = jnp.dot(gained, weight_ref[...], preferred_element_type=jnp.float32)
     reach_ref[:tokens, :] = reach.astype(reach_ref.dtype)
+    own_ref[:tokens, :] = reach
+    own_ref[tokens:, :] = reach_ref[tokens:, :].astype(own_ref.dtype)
 
 
 def reach_of(weights, inputs, gain, first):
     return pl.pallas_call(
         reach_kernel,
-        out_shape=pltpu.VMEM((inputs.shape[0] + EXTRA, weights.shape[1]), jnp.bfloat16),
+        out_shape=tuple(
+            pltpu.VMEM((inputs.shape[0] + EXTRA, weights.shape[1]), dtype)
+            for dtype in (jnp.bfloat16, jnp.float32)
+        ),
         in_specs=vmem_specs(4),
-        out_specs=pl.BlockSpec(memory_space=pltpu.VMEM),
+        out_specs=tuple(vmem_specs(2)),
         cost_estimate=HIDES,
         compiler_params=pltpu.CompilerParams(vmem_limit_bytes=8 << 20),
     )(*map(in_vmem, (weights, inputs, gain, first)))
@@ -207,22 +216,27 @@
     groups = fill(flat, blocks, head_of, 0)
     if early_refs:
         groups = groups[EARLY:]
+    reach = sum(ref[:tokens, :].astype(jnp.float32) for ref in reach_refs)
+    squares = sum(ref[tokens:, :tokens].astype(jnp.float32) for ref in reach_refs)
+    squares = jnp.sum(squares, axis=0, keepdims=True)
+    inner = as_row(jnp.sum(flat[...].astype(jnp.float32) * reach, axis=1, keepdims=True))
+    sums_ref[:1, :] = squares
+    sums_ref[1:, :] = inner
+    rho = own_ratio(squares, inner)
+    rows = [*split(squares), *split(inner), rho, jnp.zeros((1, tokens), jnp.float32)]
+    columns = standing(jnp.concatenate(rows))
+    scaled_ref[:, features:] = columns.astype(scaled_ref.dtype)
+    rho = columns[:, 6:7]
     tile = column_tile(features)
     for start in range(0, features, tile):
         part = pl.ds(start, tile)
         grad_normed = times_weights(flat, groups, weight_ref, part)
         for ref in early_refs:
             grad_normed = grad_normed + ref[:, part]
-        scaled_ref[:, part] = (grad_normed * gain_ref[:, part]).astype(scaled_ref.dtype)
-    reach = sum(ref[:tokens, :].astype(jnp.float32) for ref in reach_refs)
-    squares = sum(ref[tokens:, :tokens].astype(jnp.float32) for ref in reach_refs)
-    squares = jnp.sum(squares, axis=0, keepdims=True)
-    inner = jnp.sum(flat[...].astype(jnp.float32) * reach, axis=1, keepdims=True)
-    inner = as_row(inner)
-    sums_ref[:1, :] = squares
-    sums_ref[1:, :] = inner
-    rows = jnp.concatenate([*split(squares), *split(inner), jnp.zeros((2, tokens), jnp.float32)])
-    scaled_ref[:, features:] = standing(rows).astype(scaled_ref.dtype)
+        values = input_ref[:, part].astype(jnp.float32)
+        scaled_ref[:, part] = (grad_normed * gain_ref[:, part] - values * rho).astype(
+            scaled_ref.dtype
+        )
 
 
 def project(head_of, blocks, early, weights, inputs, gain, reaches):
@@ -248,11 +262,12 @@
     extra = scaled_ref[:, features:].astype(jnp.float32).T
     squares = extra[0:1] + extra[1:2] + extra[2:3]
     inner = extra[3:4] + extra[4:5] + extra[5:6]
+    rho = own_ratio(squares, inner)
     for ref in sums_refs:
         squares = squares + ref[:1, :]
         inner = inner + ref[1:, :]
     inv = 1.0 / jnp.sqrt(squares / D + 1e-05)
-    factor = inner * (inv * inv * inv) / D
+    factor = inner * (inv * inv * inv) / D - inv * rho
     rows = jnp.concatenate([inv, factor, jnp.zeros((6, tokens), jnp.float32)])
     columns = standing(rows)
     inv, factor = columns[:, 0:1], columns[:, 1:2]
@@ -317,12 +332,12 @@
         heads.append((swapped(packed, "tp", mask) if mask else packed, spare))
     weights, inputs = w_value[0], layer_input[0]
     next_input = passed_along(inputs, "section", -1)
-    reach = reach_of(weights, inputs, gain, heads[-1][0])
+    reach, own_reach = reach_of(weights, inputs, gain, heads[-1][0])
     if count == 8:
-        reaches = [reach, swapped(reach, "tp", SIDE)]
+        reaches = [own_reach, swapped(reach, "tp", SIDE)]
         reaches[1], next_input = lax.optimization_barrier((reaches[1], next_input))
     else:
-        reaches = [lax.psum(reach, "tp")]
+        reaches = [lax.psum(own_reach, "tp")]
     pair = value_gradients(taken, heads)
     blocks, head_of = gathered(pair, "tp")
     early = [project_early(head_of, blocks[:EARLY], weights)] if count == 8 else []

time: 27.8 us -> 27.9 us (level)
  transfers between devices with their start and end apart: 12 -> 12, of which waited for: 7 -> 7; matrix products, arithmetic and copies ran while one was open for 0% -> 0% of each run, Pallas kernels for 6% -> 5%
where the time goes in v10:
time: 27.9 us; the launch traced here: 27.5 us
  starting transfers between devices  16.7 us (60%)
  waiting for transfers between devices  6.36 us (23%)
  Pallas kernels  4.36 us (16%)
    ppermute x5, starting transfers between devices, swapped(): lax.ppermute(block, axis, [(i ^ mask, i) for i in range(lax.axis_size(axi...  7.62 us
    ppermute x5, starting transfers between devices, handed_over(): return lax.ppermute(block, ('section', 'tp'), route)  5.95 us
    ppermute x5, waiting for transfers between devices, swapped(): lax.ppermute(block, axis, [(i ^ mask, i) for i in range(lax.axis_size(axi...  4.11 us
    ppermute x2, starting transfers between devices, passed_along(): return lax.ppermute(block, axis, route)  3.15 us
    ppermute x5, waiting for transfers between devices, handed_over(): return lax.ppermute(block, ('section', 'tp'), route)  2.17 us
    pallas_call x1, Pallas kernels, finish(): pl.pallas_call(finish_kernel, out_shape=pltpu.HBM(inputs.shape, jnp.bfloa...  1.06 us
    pallas_call x1, Pallas kernels, pack(): pl.pallas_call(pack_kernel, out_shape=(pltpu.VMEM((2, *own.shape), own.dt...  0.98 us
    pallas_call x1, Pallas kernels, project(): pl.pallas_call(functools.partial(project_kernel, head_of, (len(blocks), l...  0.83 us
  transfers between devices with their start and end apart: 12, of which 7 were waited for; matrix products, arithmetic and copies ran while one was open for 0% of the time, Pallas kernels for 5%

profile of v10, /device:TPU:1, one launch (start us, length us, event | category | flops | bytes accessed | tf_op | source)
XLA Modules:
  0.0 27.5 jit_solution(9214546621763983344)
XLA Ops:
  0.0 0.0 copy-start.1
  0.0 0.0 copy-start
  0.0 0.0 copy-start.2
  0.0 1.0 %shard_map.73 = (bf16[2,128,128]{2,1,0:T(8,128)(2,1)S(1)}, bf16[128,128]{1,0:T(8,128)(2,1)S(1)}, bf16[128,128]{1,0:T(8,128)(2,1)S(1)}) custom-call(bf16[128,128]{1,0:T(8,128)(2,1)} %bitcast.12, bf16[128,128]{1,0:T(8,128)(2,1)} %bitcast.13, bf16[128,128]{1,0:T(8,128)(2,1)} %bitcast.14, s32[1,4]{1,0:T(1,128)} %evicted_ref.1), custom_call_target="tpu_custom_call" | custom-call | flops 34359738368 | bytes 33554432 | tf_op jit(solution)/shard_map/pallas_call | solution.py:87
  1.0 2.1 %collective-permute-start.2 = (bf16[2,128,128]{2,1,0:T(8,128)(2,1)S(1)}, bf16[2,128,128]{2,1,0:T(8,128)(2,1)S(1)}, u32[]{:S(2)}, u32[]{:S(2)}) collective-permute-start(bf16[2,128,128]{2,1,0:T(8,128)(2,1)S(1)} %get-tuple-element.16.refs_3_), channel_id=1, source_target_pairs={{1,0},{0,1},{3,2},{2,3},{5,4},{4,5},{7,6},{6,7},{9,8},{8,9},{11,10... | collective-permute-start | bytes 196616 | tf_op jit(solution)/shard_map/ppermute | solution.py:24
  3.1 1.2 %collective-permute-start.1 = (bf16[128,128]{1,0:T(8,128)(2,1)S(1)}, bf16[128,128]{1,0:T(8,128)(2,1)S(1)}, u32[]{:S(2)}, u32[]{:S(2)}) collective-permute-start(bf16[128,128]{1,0:T(8,128)(2,1)S(1)} %get-tuple-element.15), channel_id=1, source_target_pairs={{17,0},{16,1},{19,2},{18,3},{21,4},{20,5},{23,6},{22,7},{25,8},{24... | collective-permute-start | bytes 98312 | tf_op jit(solution)/shard_map/ppermute | solution.py:311
  4.3 0.1 collective-permute-start
  4.4 0.0 copy-done.1
  4.4 1.2 %collective-permute-start.7 = (bf16[128,1536]{1,0:T(8,128)(2,1)S(1)}, bf16[128,1536]{1,0:T(8,128)(2,1)S(1)}, u32[]{:S(2)}, u32[]{:S(2)}) collective-permute-start(bf16[128,1536]{1,0:T(8,128)(2,1)S(1)} %bitcast.9), channel_id=1, source_target_pairs={{8,0},{16,8},{24,16},{0,24},{9,1},{17,9},{25,17},{1,25},{10,2},{18... | collective-permute-start | bytes 1179656 | tf_op jit(solution)/shard_map/ppermute | solution.py:20
  5.6 0.0 collective-permute-done.2.refs_2_.first_ref
  5.6 0.0 copy-done
  5.6 0.0 copy-done.2
  5.6 0.6 %shard_map.76 = (bf16[144,1024]{1,0:T(8,128)(2,1)S(1)}, f32[144,1024]{1,0:T(8,128)S(1)}) custom-call(bf16[1536,1024]{1,0:T(8,128)(2,1)S(1)} %bitcast.6, bf16[128,1536]{1,0:T(8,128)(2,1)S(1)} %bitcast.10, f32[1,1536]{1,0:T(1,128)S(1)} %copy-done.2, bf16[2,128,128]{2,1,0:T(8,128)(2,1)S(1)} %collective-permute-done.2.refs_2_.first_ref), custom_call_target="tpu_custom_call" | custom-call | flops 34359738368 | bytes 33554432 | tf_op jit(solution)/shard_map/pallas_call | solution.py:120
  6.3 1.7 %collective-permute-start.6 = (bf16[144,1024]{1,0:T(8,128)(2,1)S(1)}, bf16[144,1024]{1,0:T(8,128)(2,1)S(1)}, u32[]{:S(2)}, u32[]{:S(2)}) collective-permute-start(bf16[144,1024]{1,0:T(8,128)(2,1)S(1)} %get-tuple-element.18), channel_id=1, source_target_pairs={{1,0},{0,1},{3,2},{2,3},{5,4},{4,5},{7,6},{6,7},{9,8},{8,9},{11,10... | collective-permute-start | bytes 884744 | tf_op jit(solution)/shard_map/ppermute | solution.py:24
  8.0 0.0 collective-permute-done.1.refs_1_
  8.0 0.0 collective-permute-done.refs_0_
  8.0 0.2 shard_map.74.refs_0_
  8.2 3.4 %collective-permute-start.3 = (bf16[2,128,128]{2,1,0:T(8,128)(2,1)S(1)}, bf16[2,128,128]{2,1,0:T(8,128)(2,1)S(1)}, u32[]{:S(2)}, u32[]{:S(2)}) collective-permute-start(bf16[2,128,128]{2,1,0:T(8,128)(2,1)S(1)} %shard_map.74.refs_0_), channel_id=1, source_target_pairs={{6,0},{7,1},{4,2},{5,3},{2,4},{3,5},{0,6},{1,7},{14,8},{15,9},{12,... | collective-permute-start | bytes 196616 | tf_op jit(solution)/shard_map/ppermute | solution.py:24
  11.6 0.0 collective-permute-start.5
  11.6 0.4 %collective-permute-start.4 = (bf16[2,128,128]{2,1,0:T(8,128)(2,1)S(1)}, bf16[2,128,128]{2,1,0:T(8,128)(2,1)S(1)}, u32[]{:S(2)}, u32[]{:S(2)}) collective-permute-start(bf16[2,128,128]{2,1,0:T(8,128)(2,1)S(1)} %shard_map.74.refs_0_), channel_id=1, source_target_pairs={{2,0},{3,1},{0,2},{1,3},{6,4},{7,5},{4,6},{5,7},{10,8},{11,9},{8,1... | collective-permute-start | bytes 196616 | tf_op jit(solution)/shard_map/ppermute | solution.py:24
  12.0 1.3 %collective-permute-done.3.refs_1_ = bf16[2,128,128]{2,1,0:T(8,128)(2,1)S(1)} collective-permute-done((bf16[2,128,128]{2,1,0:T(8,128)(2,1)S(1)}, bf16[2,128,128]{2,1,0:T(8,128)(2,1)S(1)}, u32[]{:S(2)}, u32[]{:S(2)}) %collective-permute-start.3) | collective-permute-done | bytes 65568 | tf_op jit(solution)/shard_map/ppermute | solution.py:24
  13.3 0.7 %shard_map.75.refs_4_ = f32[128,1536]{1,0:T(8,128)S(1)} custom-call(bf16[2,128,128]{2,1,0:T(8,128)(2,1)S(1)} %shard_map.74.refs_0_, bf16[2,128,128]{2,1,0:T(8,128)(2,1)S(1)} %collective-permute-done.3.refs_1_, bf16[1536,1024]{1,0:T(8,128)(2,1)S(1)} %bitcast.7), custom_call_target="tpu_custom_call" | custom-call | flops 65536 | bytes 4096 | tf_op jit(solution)/shard_map/pallas_call | solution.py:199
  14.0 0.5 %collective-permute-done.6.refs_9_ = bf16[144,1024]{1,0:T(8,128)(2,1)S(1)} collective-permute-done((bf16[144,1024]{1,0:T(8,128)(2,1)S(1)}, bf16[144,1024]{1,0:T(8,128)(2,1)S(1)}, u32[]{:S(2)}, u32[]{:S(2)}) %collective-permute-start.6) | collective-permute-done | bytes 294944 | tf_op jit(solution)/shard_map/ppermute | solution.py:24
  14.4 0.0 collective-permute-done.7.input_ref
  14.4 2.3 %collective-permute-done.5.refs_3_ = bf16[2,128,128]{2,1,0:T(8,128)(2,1)S(1)} collective-permute-done((bf16[2,128,128]{2,1,0:T(8,128)(2,1)S(1)}, bf16[2,128,128]{2,1,0:T(8,128)(2,1)S(1)}, u32[]{:S(2)}, u32[]{:S(2)}) %collective-permute-start.5) | collective-permute-done | bytes 65568 | tf_op jit(solution)/shard_map/ppermute | solution.py:24
  16.8 0.0 collective-permute-done.4.refs_2_
  16.8 0.8 %shard_map.77 = (bf16[128,1664]{1,0:T(8,128)(2,1)S(1)}, f32[2,128]{1,0:T(2,128)S(1)}) custom-call(bf16[2,128,128]{2,1,0:T(8,128)(2,1)S(1)} %shard_map.74.refs_0_, bf16[2,128,128]{2,1,0:T(8,128)(2,1)S(1)} %collective-permute-done.3.refs_1_, bf16[2,128,128]{2,1,0:T(8,128)(2,1)S(1)} %collective-permute-done.4.refs_2_, ...), custom_call_target="tpu_custom_call" | custom-call | flops 34359738368 | bytes 33554432 | tf_op jit(solution)/shard_map/pallas_call | solution.py:245
  17.6 1.9 %collective-permute-start.8 = (bf16[128,1664]{1,0:T(8,128)(2,1)S(1)}, bf16[128,1664]{1,0:T(8,128)(2,1)S(1)}, u32[]{:S(2)}, u32[]{:S(2)}) collective-permute-start(bf16[128,1664]{1,0:T(8,128)(2,1)S(1)} %get-tuple-element.20), channel_id=1, source_target_pairs={{8,0},{16,8},{24,16},{0,24},{9,1},{17,9},{25,17},{1,25},{10,2},{18... | collective-permute-start | bytes 1277960 | tf_op jit(solution)/shard_map/ppermute | solution.py:20
  19.5 2.0 %collective-permute-start.11 = (f32[2,128]{1,0:T(2,128)S(1)}, f32[2,128]{1,0:T(2,128)S(1)}, u32[]{:S(2)}, u32[]{:S(2)}) collective-permute-start(f32[2,128]{1,0:T(2,128)S(1)} %get-tuple-element.22), channel_id=1, source_target_pairs={{14,0},{15,1},{12,2},{13,3},{10,4},{11,5},{8,6},{9,7},{22,8},{23,9... | collective-permute-start | bytes 3080 | tf_op jit(solution)/shard_map/ppermute | solution.py:311
  21.5 0.7 %collective-permute-start.10 = (f32[2,128]{1,0:T(2,128)S(1)}, f32[2,128]{1,0:T(2,128)S(1)}, u32[]{:S(2)}, u32[]{:S(2)}) collective-permute-start(f32[2,128]{1,0:T(2,128)S(1)} %get-tuple-element.22), channel_id=1, source_target_pairs={{12,0},{13,1},{14,2},{15,3},{8,4},{9,5},{10,6},{11,7},{20,8},{21,9... | collective-permute-start | bytes 3080 | tf_op jit(solution)/shard_map/ppermute | solution.py:311
  22.2 2.0 %collective-permute-start.9 = (f32[2,128]{1,0:T(2,128)S(1)}, f32[2,128]{1,0:T(2,128)S(1)}, u32[]{:S(2)}, u32[]{:S(2)}) collective-permute-start(f32[2,128]{1,0:T(2,128)S(1)} %get-tuple-element.22), channel_id=1, source_target_pairs={{10,0},{11,1},{8,2},{9,3},{14,4},{15,5},{12,6},{13,7},{18,8},{19,9... | collective-permute-start | bytes 3080 | tf_op jit(solution)/shard_map/ppermute | solution.py:311
  24.2 1.0 %collective-permute-done.11.refs_2_ = f32[2,128]{1,0:T(2,128)S(1)} collective-permute-done((f32[2,128]{1,0:T(2,128)S(1)}, f32[2,128]{1,0:T(2,128)S(1)}, u32[]{:S(2)}, u32[]{:S(2)}) %collective-permute-start.11) | collective-permute-done | bytes 1056 | tf_op jit(solution)/shard_map/ppermute | solution.py:311
  25.2 1.1 %collective-permute-done.10.refs_1_ = f32[2,128]{1,0:T(2,128)S(1)} collective-permute-done((f32[2,128]{1,0:T(2,128)S(1)}, f32[2,128]{1,0:T(2,128)S(1)}, u32[]{:S(2)}, u32[]{:S(2)}) %collective-permute-start.10) | collective-permute-done | bytes 1056 | tf_op jit(solution)/shard_map/ppermute | solution.py:311
  26.3 0.1 collective-permute-done.9.refs_0_
  26.4 0.1 collective-permute-done.8.scaled_ref
  26.5 1.1 %shard_map.78 = bf16[128,1536]{1,0:T(8,128)(2,1)} custom-call(bf16[128,1664]{1,0:T(8,128)(2,1)S(1)} %collective-permute-done.8.scaled_ref, bf16[128,1536]{1,0:T(8,128)(2,1)S(1)} %collective-permute-done.7.input_ref, f32[2,128]{1,0:T(2,128)S(1)} %collective-permute-done.9.refs_0_, f32[2,128]{1,0:T(2,128)S(1)} %collective-permute-done.10.refs_1_, ...), custom_call_target="tpu_custom_call" | custom-call | tf_op jit(solution)/shard_map/pallas_call | solution.py:287
Async XLA Ops:
  0.0 4.4 %copy-start.1 = (bf16[1,128,1536]{2,1,0:T(8,128)(2,1)S(1)}, bf16[1,128,1536]{2,1,0:T(8,128)(2,1)}, u32[]{:S(2)}) copy-start(bf16[1,128,1536]{2,1,0:T(8,128)(2,1)} %param.12) | copy-start | bytes 1179652
  0.0 5.6 %copy-start = (bf16[1,1536,1024]{2,1,0:T(8,128)(2,1)S(1)}, bf16[1,1536,1024]{2,1,0:T(8,128)(2,1)}, u32[]{:S(2)}) copy-start(bf16[1,1536,1024]{2,1,0:T(8,128)(2,1)} %param.8) | copy-start | bytes 9437188
  0.0 5.6 %copy-start.2 = (f32[1,1536]{1,0:T(1,128)S(1)}, f32[1,1536]{1,0:T(1,128)}, u32[]{:S(2)}) copy-start(f32[1,1536]{1,0:T(1,128)} %refs_7_.1) | copy-start | bytes 18436
  1.0 4.6 %collective-permute-start.2 = (bf16[2,128,128]{2,1,0:T(8,128)(2,1)S(1)}, bf16[2,128,128]{2,1,0:T(8,128)(2,1)S(1)}, u32[]{:S(2)}, u32[]{:S(2)}) collective-permute-start(bf16[2,128,128]{2,1,0:T(8,128)(2,1)S(1)} %get-tuple-element.16.refs_3_), channel_id=1, source_target_pairs={{1,0},{0,1},{3,2},{2,3},{5,4},{4,5},{7,6},{6,7},{9,8},{8,9},{11,10... | collective-permute-start | bytes 196616 | tf_op jit(solution)/shard_map/ppermute | solution.py:24
  3.1 4.9 %collective-permute-start.1 = (bf16[128,128]{1,0:T(8,128)(2,1)S(1)}, bf16[128,128]{1,0:T(8,128)(2,1)S(1)}, u32[]{:S(2)}, u32[]{:S(2)}) collective-permute-start(bf16[128,128]{1,0:T(8,128)(2,1)S(1)} %get-tuple-element.15), channel_id=1, source_target_pairs={{17,0},{16,1},{19,2},{18,3},{21,4},{20,5},{23,6},{22,7},{25,8},{24... | collective-permute-start | bytes 98312 | tf_op jit(solution)/shard_map/ppermute | solution.py:311
  4.3 3.7 %collective-permute-start = (bf16[128,128]{1,0:T(8,128)(2,1)S(1)}, bf16[128,128]{1,0:T(8,128)(2,1)S(1)}, u32[]{:S(2)}, u32[]{:S(2)}) collective-permute-start(bf16[128,128]{1,0:T(8,128)(2,1)S(1)} %get-tuple-element.15), channel_id=1, source_target_pairs={{16,0},{17,1},{18,2},{19,3},{20,4},{21,5},{22,6},{23,7},{24,8},{25... | collective-permute-start | bytes 98312 | tf_op jit(solution)/shard_map/ppermute | solution.py:311
  4.4 10.0 %collective-permute-start.7 = (bf16[128,1536]{1,0:T(8,128)(2,1)S(1)}, bf16[128,1536]{1,0:T(8,128)(2,1)S(1)}, u32[]{:S(2)}, u32[]{:S(2)}) collective-permute-start(bf16[128,1536]{1,0:T(8,128)(2,1)S(1)} %bitcast.9), channel_id=1, source_target_pairs={{8,0},{16,8},{24,16},{0,24},{9,1},{17,9},{25,17},{1,25},{10,2},{18... | collective-permute-start | bytes 1179656 | tf_op jit(solution)/shard_map/ppermute | solution.py:20
  6.3 8.1 %collective-permute-start.6 = (bf16[144,1024]{1,0:T(8,128)(2,1)S(1)}, bf16[144,1024]{1,0:T(8,128)(2,1)S(1)}, u32[]{:S(2)}, u32[]{:S(2)}) collective-permute-start(bf16[144,1024]{1,0:T(8,128)(2,1)S(1)} %get-tuple-element.18), channel_id=1, source_target_pairs={{1,0},{0,1},{3,2},{2,3},{5,4},{4,5},{7,6},{6,7},{9,8},{8,9},{11,10... | collective-permute-start | bytes 884744 | tf_op jit(solution)/shard_map/ppermute | solution.py:24
  8.2 5.0 %collective-permute-start.3 = (bf16[2,128,128]{2,1,0:T(8,128)(2,1)S(1)}, bf16[2,128,128]{2,1,0:T(8,128)(2,1)S(1)}, u32[]{:S(2)}, u32[]{:S(2)}) collective-permute-start(bf16[2,128,128]{2,1,0:T(8,128)(2,1)S(1)} %shard_map.74.refs_0_), channel_id=1, source_target_pairs={{6,0},{7,1},{4,2},{5,3},{2,4},{3,5},{0,6},{1,7},{14,8},{15,9},{12,... | collective-permute-start | bytes 196616 | tf_op jit(solution)/shard_map/ppermute | solution.py:24
  11.6 5.2 %collective-permute-start.5 = (bf16[2,128,128]{2,1,0:T(8,128)(2,1)S(1)}, bf16[2,128,128]{2,1,0:T(8,128)(2,1)S(1)}, u32[]{:S(2)}, u32[]{:S(2)}) collective-permute-start(bf16[2,128,128]{2,1,0:T(8,128)(2,1)S(1)} %shard_map.74.refs_0_), channel_id=1, source_target_pairs={{4,0},{5,1},{6,2},{7,3},{0,4},{1,5},{2,6},{3,7},{12,8},{13,9},{14,... | collective-permute-start | bytes 196616 | tf_op jit(solution)/shard_map/ppermute | solution.py:24
  11.6 5.2 %collective-permute-start.4 = (bf16[2,128,128]{2,1,0:T(8,128)(2,1)S(1)}, bf16[2,128,128]{2,1,0:T(8,128)(2,1)S(1)}, u32[]{:S(2)}, u32[]{:S(2)}) collective-permute-start(bf16[2,128,128]{2,1,0:T(8,128)(2,1)S(1)} %shard_map.74.refs_0_), channel_id=1, source_target_pairs={{2,0},{3,1},{0,2},{1,3},{6,4},{7,5},{4,6},{5,7},{10,8},{11,9},{8,1... | collective-permute-start | bytes 196616 | tf_op jit(solution)/shard_map/ppermute | solution.py:24
  17.6 8.8 %collective-permute-start.8 = (bf16[128,1664]{1,0:T(8,128)(2,1)S(1)}, bf16[128,1664]{1,0:T(8,128)(2,1)S(1)}, u32[]{:S(2)}, u32[]{:S(2)}) collective-permute-start(bf16[128,1664]{1,0:T(8,128)(2,1)S(1)} %get-tuple-element.20), channel_id=1, source_target_pairs={{8,0},{16,8},{24,16},{0,24},{9,1},{17,9},{25,17},{1,25},{10,2},{18... | collective-permute-start | bytes 1277960 | tf_op jit(solution)/shard_map/ppermute | solution.py:20
  19.5 5.7 %collective-permute-start.11 = (f32[2,128]{1,0:T(2,128)S(1)}, f32[2,128]{1,0:T(2,128)S(1)}, u32[]{:S(2)}, u32[]{:S(2)}) collective-permute-start(f32[2,128]{1,0:T(2,128)S(1)} %get-tuple-element.22), channel_id=1, source_target_pairs={{14,0},{15,1},{12,2},{13,3},{10,4},{11,5},{8,6},{9,7},{22,8},{23,9... | collective-permute-start | bytes 3080 | tf_op jit(solution)/shard_map/ppermute | solution.py:311
  21.5 4.8 %collective-permute-start.10 = (f32[2,128]{1,0:T(2,128)S(1)}, f32[2,128]{1,0:T(2,128)S(1)}, u32[]{:S(2)}, u32[]{:S(2)}) collective-permute-start(f32[2,128]{1,0:T(2,128)S(1)} %get-tuple-element.22), channel_id=1, source_target_pairs={{12,0},{13,1},{14,2},{15,3},{8,4},{9,5},{10,6},{11,7},{20,8},{21,9... | collective-permute-start | bytes 3080 | tf_op jit(solution)/shard_map/ppermute | solution.py:311
  22.2 4.1 %collective-permute-start.9 = (f32[2,128]{1,0:T(2,128)S(1)}, f32[2,128]{1,0:T(2,128)S(1)}, u32[]{:S(2)}, u32[]{:S(2)}) collective-permute-start(f32[2,128]{1,0:T(2,128)S(1)} %get-tuple-element.22), channel_id=1, source_target_pairs={{10,0},{11,1},{8,2},{9,3},{14,4},{15,5},{12,6},{13,7},{18,8},{19,9... | collective-permute-start | bytes 3080 | tf_op jit(solution)/shard_map/ppermute | solution.py:311

commit v11 on v10

--- a/solution.py
+++ b/solution.py
@@ -11,6 +11,8 @@
 LANES = 128
 PIECES = (0, 3, 5, 7, 8)
 EXTRA = 16
+SHORT = pl.CostEstimate(flops=1 << 16, bytes_accessed=1 << 12, transcendentals=0)
+HALF = pl.CostEstimate(flops=1 << 31, bytes_accessed=1 << 16, transcendentals=0)
 HIDES = pl.CostEstimate(flops=1 << 35, bytes_accessed=1 << 25, transcendentals=0)
 
 
@@ -102,8 +104,7 @@
     )(*map(in_hbm, (own, grad, spare, evicted)))
 
 
-def reach_kernel(weight_ref, input_ref, gain_ref, first_ref, reach_ref, own_ref):
-    del first_ref
+def reach_kernel(weight_ref, input_ref, gain_ref, reach_ref, own_ref):
     tokens, features = input_ref.shape
     values = input_ref[...].astype(jnp.float32)
     reach_ref[tokens:, :] = jnp.zeros_like(reach_ref[tokens:, :])
@@ -123,11 +124,11 @@
             pltpu.VMEM((inputs.shape[0] + EXTRA, weights.shape[1]), dtype)
             for dtype in (jnp.bfloat16, jnp.float32)
         ),
-        in_specs=vmem_specs(4),
+        in_specs=vmem_specs(3),
         out_specs=tuple(vmem_specs(2)),
-        cost_estimate=HIDES,
+        cost_estimate=SHORT,
         compiler_params=pltpu.CompilerParams(vmem_limit_bytes=8 << 20),
-    )(*map(in_vmem, (weights, inputs, gain, first)))
+    )(*map(in_vmem, (weights, inputs, gain)))
 
 
 def mix_kernel(taken_ref, *refs):
@@ -149,7 +150,7 @@
         out_shape=pltpu.VMEM((len(heads), *heads[0][1].shape), jnp.bfloat16),
         in_specs=vmem_specs(1 + 2 * len(heads)),
         out_specs=pl.BlockSpec(memory_space=pltpu.VMEM),
-        cost_estimate=HIDES,
+        cost_estimate=HALF,
         compiler_params=pltpu.CompilerParams(vmem_limit_bytes=4 << 20),
     )(*map(in_vmem, (taken, *[spare for _, spare in heads], *[packed for packed, _ in heads[::-1]])))
 
@@ -202,7 +203,7 @@
         in_specs=vmem_specs(len(blocks) + 1),
         out_specs=pl.BlockSpec(memory_space=pltpu.VMEM),
         scratch_shapes=[pltpu.VMEM((tokens, weights.shape[1]), jnp.bfloat16)],
-        cost_estimate=pl.CostEstimate(flops=1 << 16, bytes_accessed=1 << 12, transcendentals=0),
+        cost_estimate=SHORT,
         compiler_params=pltpu.CompilerParams(vmem_limit_bytes=16 << 20),
     )(*map(in_vmem, (*blocks, weights)))
 
@@ -334,6 +335,8 @@
     next_input = passed_along(inputs, "section", -1)
     reach, own_reach = reach_of(weights, inputs, gain, heads[-1][0])
     if count == 8:
+        reach, swap = lax.optimization_barrier((reach, heads[1][0]))
+        heads[1] = (swap, heads[1][1])
         reaches = [own_reach, swapped(reach, "tp", SIDE)]
         reaches[1], next_input = lax.optimization_barrier((reaches[1], next_input))
     else:

time: 27.9 us -> 29.1 us (1.043)
  waiting for transfers between devices: 6.36 us -> 7.36 us
  starting transfers between devices: 16.7 us -> 17.2 us
    ppermute x5, waiting for transfers between devices: 2.17 us -> 2.75 us  [handed_over(): return lax.ppermute(block, ('section', 'tp'), route)]
    ppermute x2, waiting for transfers between devices: 0.07 us -> 0.44 us  [passed_along(): return lax.ppermute(block, axis, route)]
    ppermute x5, starting transfers between devices: 7.62 us -> 7.94 us  [swapped(): lax.ppermute(block, axis, [(i ^ mask, i) for i in range(lax.axis_size(axi...]
  transfers between devices with their start and end apart: 12 -> 12, of which waited for: 7 -> 8; matrix products, arithmetic and copies ran while one was open for 0% -> 0% of each run, Pallas kernels for 5% -> 9%
where the time goes in v11:
time: 29.1 us; the launch traced here: 29 us
  starting transfers between devices  17.2 us (59%)
  waiting for transfers between devices  7.36 us (25%)
  Pallas kernels  4.37 us (15%)
    ppermute x5, starting transfers between devices, swapped(): lax.ppermute(block, axis, [(i ^ mask, i) for i in range(lax.axis_size(axi...  7.94 us
    ppermute x5, starting transfers between devices, handed_over(): return lax.ppermute(block, ('section', 'tp'), route)  5.94 us
    ppermute x5, waiting for transfers between devices, swapped(): lax.ppermute(block, axis, [(i ^ mask, i) for i in range(lax.axis_size(axi...  4.18 us
    ppermute x2, starting transfers between devices, passed_along(): return lax.ppermute(block, axis, route)  3.28 us
    ppermute x5, waiting for transfers between devices, handed_over(): return lax.ppermute(block, ('section', 'tp'), route)  2.75 us
    pallas_call x1, Pallas kernels, finish(): pl.pallas_call(finish_kernel, out_shape=pltpu.HBM(inputs.shape, jnp.bfloa...  1.06 us
    pallas_call x1, Pallas kernels, pack(): pl.pallas_call(pack_kernel, out_shape=(pltpu.VMEM((2, *own.shape), own.dt...  0.97 us
    pallas_call x1, Pallas kernels, project(): pl.pallas_call(functools.partial(project_kernel, head_of, (len(blocks), l...  0.82 us
  transfers between devices with their start and end apart: 12, of which 8 were waited for; matrix products, arithmetic and copies ran while one was open for 0% of the time, Pallas kernels for 9%

profile of v11, /device:TPU:1, one launch (start us, length us, event | category | flops | bytes accessed | tf_op | source)
XLA Modules:
  0.0 29.0 jit_solution(16017769123912488494)
XLA Ops:
  0.0 0.1 collective-permute-start.7
  0.1 0.0 copy-start
  0.1 0.0 copy-start.1
  0.1 0.0 copy-start.2
  0.1 1.0 %shard_map.73 = (bf16[2,128,128]{2,1,0:T(8,128)(2,1)S(1)}, bf16[128,128]{1,0:T(8,128)(2,1)S(1)}, bf16[128,128]{1,0:T(8,128)(2,1)S(1)}) custom-call(bf16[128,128]{1,0:T(8,128)(2,1)} %bitcast.12, bf16[128,128]{1,0:T(8,128)(2,1)} %bitcast.13, bf16[128,128]{1,0:T(8,128)(2,1)} %bitcast.14, s32[1,4]{1,0:T(1,128)} %evicted_ref.1), custom_call_target="tpu_custom_call" | custom-call | flops 34359738368 | bytes 33554432 | tf_op jit(solution)/shard_map/pallas_call | solution.py:89
  1.0 2.8 %collective-permute-start.2 = (bf16[2,128,128]{2,1,0:T(8,128)(2,1)S(1)}, bf16[2,128,128]{2,1,0:T(8,128)(2,1)S(1)}, u32[]{:S(2)}, u32[]{:S(2)}) collective-permute-start(bf16[2,128,128]{2,1,0:T(8,128)(2,1)S(1)} %get-tuple-element.19.refs_3_), channel_id=1, source_target_pairs={{1,0},{0,1},{3,2},{2,3},{5,4},{4,5},{7,6},{6,7},{9,8},{8,9},{11,10... | collective-permute-start | bytes 196616 | tf_op jit(solution)/shard_map/ppermute | solution.py:26
  3.8 1.2 %collective-permute-start.1 = (bf16[128,128]{1,0:T(8,128)(2,1)S(1)}, bf16[128,128]{1,0:T(8,128)(2,1)S(1)}, u32[]{:S(2)}, u32[]{:S(2)}) collective-permute-start(bf16[128,128]{1,0:T(8,128)(2,1)S(1)} %get-tuple-element.17), channel_id=1, source_target_pairs={{17,0},{16,1},{19,2},{18,3},{21,4},{20,5},{23,6},{22,7},{25,8},{24... | collective-permute-start | bytes 98312 | tf_op jit(solution)/shard_map/ppermute | solution.py:312
  5.0 0.1 collective-permute-start
  5.1 0.0 copy-done
  5.1 0.0 copy-done.1
  5.1 0.0 copy-done.2
  5.1 0.6 %shard_map.74 = (bf16[144,1024]{1,0:T(8,128)(2,1)S(1)}, f32[144,1024]{1,0:T(8,128)S(1)}) custom-call(bf16[1536,1024]{1,0:T(8,128)(2,1)S(1)} %bitcast.6, bf16[128,1536]{1,0:T(8,128)(2,1)S(1)} %bitcast.10, f32[1,1536]{1,0:T(1,128)S(1)} %copy-done.2), custom_call_target="tpu_custom_call" | custom-call | flops 65536 | bytes 4096 | tf_op jit(solution)/shard_map/pallas_call | solution.py:121
  5.7 0.0 collective-permute-done.2.refs_2_
  5.7 1.4 %collective-permute-start.6 = (bf16[144,1024]{1,0:T(8,128)(2,1)S(1)}, bf16[144,1024]{1,0:T(8,128)(2,1)S(1)}, u32[]{:S(2)}, u32[]{:S(2)}) collective-permute-start(bf16[144,1024]{1,0:T(8,128)(2,1)S(1)} %get-tuple-element.22), channel_id=1, source_target_pairs={{1,0},{0,1},{3,2},{2,3},{5,4},{4,5},{7,6},{6,7},{9,8},{8,9},{11,10... | collective-permute-start | bytes 884744 | tf_op jit(solution)/shard_map/ppermute | solution.py:26
  7.2 0.7 %collective-permute-done.1.refs_1_ = bf16[128,128]{1,0:T(8,128)(2,1)S(1)} collective-permute-done((bf16[128,128]{1,0:T(8,128)(2,1)S(1)}, bf16[128,128]{1,0:T(8,128)(2,1)S(1)}, u32[]{:S(2)}, u32[]{:S(2)}) %collective-permute-start.1) | collective-permute-done | bytes 32800 | tf_op jit(solution)/shard_map/ppermute | solution.py:312
  7.9 0.3 collective-permute-done.refs_0_
  8.1 0.2 shard_map.75.refs_0_
  8.3 3.4 %collective-permute-start.3 = (bf16[2,128,128]{2,1,0:T(8,128)(2,1)S(1)}, bf16[2,128,128]{2,1,0:T(8,128)(2,1)S(1)}, u32[]{:S(2)}, u32[]{:S(2)}) collective-permute-start(bf16[2,128,128]{2,1,0:T(8,128)(2,1)S(1)} %shard_map.75.refs_0_), channel_id=1, source_target_pairs={{6,0},{7,1},{4,2},{5,3},{2,4},{3,5},{0,6},{1,7},{14,8},{15,9},{12,... | collective-permute-start | bytes 196616 | tf_op jit(solution)/shard_map/ppermute | solution.py:26
  11.7 0.0 collective-permute-start.5
  11.7 0.4 %collective-permute-start.4 = (bf16[2,128,128]{2,1,0:T(8,128)(2,1)S(1)}, bf16[2,128,128]{2,1,0:T(8,128)(2,1)S(1)}, u32[]{:S(2)}, u32[]{:S(2)}) collective-permute-start(bf16[2,128,128]{2,1,0:T(8,128)(2,1)S(1)} %shard_map.75.refs_0_), channel_id=1, source_target_pairs={{2,0},{3,1},{0,2},{1,3},{6,4},{7,5},{4,6},{5,7},{10,8},{11,9},{8,1... | collective-permute-start | bytes 196616 | tf_op jit(solution)/shard_map/ppermute | solution.py:26
  12.1 1.3 %collective-permute-done.3.refs_1_ = bf16[2,128,128]{2,1,0:T(8,128)(2,1)S(1)} collective-permute-done((bf16[2,128,128]{2,1,0:T(8,128)(2,1)S(1)}, bf16[2,128,128]{2,1,0:T(8,128)(2,1)S(1)}, u32[]{:S(2)}, u32[]{:S(2)}) %collective-permute-start.3) | collective-permute-done | bytes 65568 | tf_op jit(solution)/shard_map/ppermute | solution.py:26
  13.4 0.7 %shard_map.76.refs_4_ = f32[128,1536]{1,0:T(8,128)S(1)} custom-call(bf16[2,128,128]{2,1,0:T(8,128)(2,1)S(1)} %shard_map.75.refs_0_, bf16[2,128,128]{2,1,0:T(8,128)(2,1)S(1)} %collective-permute-done.3.refs_1_, bf16[1536,1024]{1,0:T(8,128)(2,1)S(1)} %bitcast.7), custom_call_target="tpu_custom_call" | custom-call | flops 65536 | bytes 4096 | tf_op jit(solution)/shard_map/pallas_call | solution.py:200
  14.1 0.0 collective-permute-done.6.refs_9_
  14.1 0.0 collective-permute-done.7.input_ref
  14.1 2.9 %collective-permute-done.5.refs_3_ = bf16[2,128,128]{2,1,0:T(8,128)(2,1)S(1)} collective-permute-done((bf16[2,128,128]{2,1,0:T(8,128)(2,1)S(1)}, bf16[2,128,128]{2,1,0:T(8,128)(2,1)S(1)}, u32[]{:S(2)}, u32[]{:S(2)}) %collective-permute-start.5) | collective-permute-done | bytes 65568 | tf_op jit(solution)/shard_map/ppermute | solution.py:26
  16.9 0.0 collective-permute-done.4.refs_2_
  17.0 0.8 %shard_map.77 = (bf16[128,1664]{1,0:T(8,128)(2,1)S(1)}, f32[2,128]{1,0:T(2,128)S(1)}) custom-call(bf16[2,128,128]{2,1,0:T(8,128)(2,1)S(1)} %shard_map.75.refs_0_, bf16[2,128,128]{2,1,0:T(8,128)(2,1)S(1)} %collective-permute-done.3.refs_1_, bf16[2,128,128]{2,1,0:T(8,128)(2,1)S(1)} %collective-permute-done.4.refs_2_, ...), custom_call_target="tpu_custom_call" | custom-call | flops 34359738368 | bytes 33554432 | tf_op jit(solution)/shard_map/pallas_call | solution.py:246
  17.8 3.2 %collective-permute-start.8 = (bf16[128,1664]{1,0:T(8,128)(2,1)S(1)}, bf16[128,1664]{1,0:T(8,128)(2,1)S(1)}, u32[]{:S(2)}, u32[]{:S(2)}) collective-permute-start(bf16[128,1664]{1,0:T(8,128)(2,1)S(1)} %get-tuple-element.24), channel_id=1, source_target_pairs={{8,0},{16,8},{24,16},{0,24},{9,1},{17,9},{25,17},{1,25},{10,2},{18... | collective-permute-start | bytes 1277960 | tf_op jit(solution)/shard_map/ppermute | solution.py:22
  21.0 1.3 %collective-permute-start.11 = (f32[2,128]{1,0:T(2,128)S(1)}, f32[2,128]{1,0:T(2,128)S(1)}, u32[]{:S(2)}, u32[]{:S(2)}) collective-permute-start(f32[2,128]{1,0:T(2,128)S(1)} %get-tuple-element.26), channel_id=1, source_target_pairs={{14,0},{15,1},{12,2},{13,3},{10,4},{11,5},{8,6},{9,7},{22,8},{23,9... | collective-permute-start | bytes 3080 | tf_op jit(solution)/shard_map/ppermute | solution.py:312
  22.3 1.3 %collective-permute-start.10 = (f32[2,128]{1,0:T(2,128)S(1)}, f32[2,128]{1,0:T(2,128)S(1)}, u32[]{:S(2)}, u32[]{:S(2)}) collective-permute-start(f32[2,128]{1,0:T(2,128)S(1)} %get-tuple-element.26), channel_id=1, source_target_pairs={{12,0},{13,1},{14,2},{15,3},{8,4},{9,5},{10,6},{11,7},{20,8},{21,9... | collective-permute-start | bytes 3080 | tf_op jit(solution)/shard_map/ppermute | solution.py:312
  23.6 2.1 %collective-permute-start.9 = (f32[2,128]{1,0:T(2,128)S(1)}, f32[2,128]{1,0:T(2,128)S(1)}, u32[]{:S(2)}, u32[]{:S(2)}) collective-permute-start(f32[2,128]{1,0:T(2,128)S(1)} %get-tuple-element.26), channel_id=1, source_target_pairs={{10,0},{11,1},{8,2},{9,3},{14,4},{15,5},{12,6},{13,7},{18,8},{19,9... | collective-permute-start | bytes 3080 | tf_op jit(solution)/shard_map/ppermute | solution.py:312
  25.7 1.0 %collective-permute-done.11.refs_2_ = f32[2,128]{1,0:T(2,128)S(1)} collective-permute-done((f32[2,128]{1,0:T(2,128)S(1)}, f32[2,128]{1,0:T(2,128)S(1)}, u32[]{:S(2)}, u32[]{:S(2)}) %collective-permute-start.11) | collective-permute-done | bytes 1056 | tf_op jit(solution)/shard_map/ppermute | solution.py:312
  26.7 0.4 %collective-permute-done.10.refs_1_ = f32[2,128]{1,0:T(2,128)S(1)} collective-permute-done((f32[2,128]{1,0:T(2,128)S(1)}, f32[2,128]{1,0:T(2,128)S(1)}, u32[]{:S(2)}, u32[]{:S(2)}) %collective-permute-start.10) | collective-permute-done | bytes 1056 | tf_op jit(solution)/shard_map/ppermute | solution.py:312
  27.1 0.4 %collective-permute-done.9.refs_0_ = f32[2,128]{1,0:T(2,128)S(1)} collective-permute-done((f32[2,128]{1,0:T(2,128)S(1)}, f32[2,128]{1,0:T(2,128)S(1)}, u32[]{:S(2)}, u32[]{:S(2)}) %collective-permute-start.9) | collective-permute-done | bytes 1056 | tf_op jit(solution)/shard_map/ppermute | solution.py:312
  27.5 0.4 %collective-permute-done.8.scaled_ref = bf16[128,1664]{1,0:T(8,128)(2,1)S(1)} collective-permute-done((bf16[128,1664]{1,0:T(8,128)(2,1)S(1)}, bf16[128,1664]{1,0:T(8,128)(2,1)S(1)}, u32[]{:S(2)}, u32[]{:S(2)}) %collective-permute-start.8) | collective-permute-done | bytes 426016 | tf_op jit(solution)/shard_map/ppermute | solution.py:22
  27.9 1.1 %shard_map.78 = bf16[128,1536]{1,0:T(8,128)(2,1)} custom-call(bf16[128,1664]{1,0:T(8,128)(2,1)S(1)} %collective-permute-done.8.scaled_ref, bf16[128,1536]{1,0:T(8,128)(2,1)S(1)} %collective-permute-done.7.input_ref, f32[2,128]{1,0:T(2,128)S(1)} %collective-permute-done.9.refs_0_, f32[2,128]{1,0:T(2,128)S(1)} %collective-permute-done.10.refs_1_, ...), custom_call_target="tpu_custom_call" | custom-call | tf_op jit(solution)/shard_map/pallas_call | solution.py:288
Async XLA Ops:
  0.0 14.1 %collective-permute-start.7 = (bf16[128,1536]{1,0:T(8,128)(2,1)}, bf16[128,1536]{1,0:T(8,128)(2,1)S(1)}, u32[]{:S(2)}, u32[]{:S(2)}) collective-permute-start(bf16[128,1536]{1,0:T(8,128)(2,1)} %bitcast.9), channel_id=1, source_target_pairs={{8,0},{16,8},{24,16},{0,24},{9,1},{17,9},{25,17},{1,25},{10,2},{18... | collective-permute-start | bytes 1179656 | tf_op jit(solution)/shard_map/ppermute | solution.py:22
  0.1 5.0 %copy-start = (bf16[1,1536,1024]{2,1,0:T(8,128)(2,1)S(1)}, bf16[1,1536,1024]{2,1,0:T(8,128)(2,1)}, u32[]{:S(2)}) copy-start(bf16[1,1536,1024]{2,1,0:T(8,128)(2,1)} %param.8) | copy-start | bytes 9437188
  0.1 5.0 %copy-start.1 = (bf16[1,128,1536]{2,1,0:T(8,128)(2,1)S(1)}, bf16[1,128,1536]{2,1,0:T(8,128)(2,1)}, u32[]{:S(2)}) copy-start(bf16[1,128,1536]{2,1,0:T(8,128)(2,1)} %param.12) | copy-start | bytes 1179652
  0.1 5.0 %copy-start.2 = (f32[1,1536]{1,0:T(1,128)S(1)}, f32[1,1536]{1,0:T(1,128)}, u32[]{:S(2)}) copy-start(f32[1,1536]{1,0:T(1,128)} %refs_7_.1) | copy-start | bytes 18436
  1.0 4.7 %collective-permute-start.2 = (bf16[2,128,128]{2,1,0:T(8,128)(2,1)S(1)}, bf16[2,128,128]{2,1,0:T(8,128)(2,1)S(1)}, u32[]{:S(2)}, u32[]{:S(2)}) collective-permute-start(bf16[2,128,128]{2,1,0:T(8,128)(2,1)S(1)} %get-tuple-element.19.refs_3_), channel_id=1, source_target_pairs={{1,0},{0,1},{3,2},{2,3},{5,4},{4,5},{7,6},{6,7},{9,8},{8,9},{11,10... | collective-permute-start | bytes 196616 | tf_op jit(solution)/shard_map/ppermute | solution.py:26
  3.8 4.1 %collective-permute-start.1 = (bf16[128,128]{1,0:T(8,128)(2,1)S(1)}, bf16[128,128]{1,0:T(8,128)(2,1)S(1)}, u32[]{:S(2)}, u32[]{:S(2)}) collective-permute-start(bf16[128,128]{1,0:T(8,128)(2,1)S(1)} %get-tuple-element.17), channel_id=1, source_target_pairs={{17,0},{16,1},{19,2},{18,3},{21,4},{20,5},{23,6},{22,7},{25,8},{24... | collective-permute-start | bytes 98312 | tf_op jit(solution)/shard_map/ppermute | solution.py:312
  5.0 3.2 %collective-permute-start = (bf16[128,128]{1,0:T(8,128)(2,1)S(1)}, bf16[128,128]{1,0:T(8,128)(2,1)S(1)}, u32[]{:S(2)}, u32[]{:S(2)}) collective-permute-start(bf16[128,128]{1,0:T(8,128)(2,1)S(1)} %get-tuple-element.17), channel_id=1, source_target_pairs={{16,0},{17,1},{18,2},{19,3},{20,4},{21,5},{22,6},{23,7},{24,8},{25... | collective-permute-start | bytes 98312 | tf_op jit(solution)/shard_map/ppermute | solution.py:312
  5.7 8.3 %collective-permute-start.6 = (bf16[144,1024]{1,0:T(8,128)(2,1)S(1)}, bf16[144,1024]{1,0:T(8,128)(2,1)S(1)}, u32[]{:S(2)}, u32[]{:S(2)}) collective-permute-start(bf16[144,1024]{1,0:T(8,128)(2,1)S(1)} %get-tuple-element.22), channel_id=1, source_target_pairs={{1,0},{0,1},{3,2},{2,3},{5,4},{4,5},{7,6},{6,7},{9,8},{8,9},{11,10... | collective-permute-start | bytes 884744 | tf_op jit(solution)/shard_map/ppermute | solution.py:26
  8.3 5.0 %collective-permute-start.3 = (bf16[2,128,128]{2,1,0:T(8,128)(2,1)S(1)}, bf16[2,128,128]{2,1,0:T(8,128)(2,1)S(1)}, u32[]{:S(2)}, u32[]{:S(2)}) collective-permute-start(bf16[2,128,128]{2,1,0:T(8,128)(2,1)S(1)} %shard_map.75.refs_0_), channel_id=1, source_target_pairs={{6,0},{7,1},{4,2},{5,3},{2,4},{3,5},{0,6},{1,7},{14,8},{15,9},{12,... | collective-permute-start | bytes 196616 | tf_op jit(solution)/shard_map/ppermute | solution.py:26
  11.7 5.2 %collective-permute-start.5 = (bf16[2,128,128]{2,1,0:T(8,128)(2,1)S(1)}, bf16[2,128,128]{2,1,0:T(8,128)(2,1)S(1)}, u32[]{:S(2)}, u32[]{:S(2)}) collective-permute-start(bf16[2,128,128]{2,1,0:T(8,128)(2,1)S(1)} %shard_map.75.refs_0_), channel_id=1, source_target_pairs={{4,0},{5,1},{6,2},{7,3},{0,4},{1,5},{2,6},{3,7},{12,8},{13,9},{14,... | collective-permute-start | bytes 196616 | tf_op jit(solution)/shard_map/ppermute | solution.py:26
  11.7 5.2 %collective-permute-start.4 = (bf16[2,128,128]{2,1,0:T(8,128)(2,1)S(1)}, bf16[2,128,128]{2,1,0:T(8,128)(2,1)S(1)}, u32[]{:S(2)}, u32[]{:S(2)}) collective-permute-start(bf16[2,128,128]{2,1,0:T(8,128)(2,1)S(1)} %shard_map.75.refs_0_), channel_id=1, source_target_pairs={{2,0},{3,1},{0,2},{1,3},{6,4},{7,5},{4,6},{5,7},{10,8},{11,9},{8,1... | collective-permute-start | bytes 196616 | tf_op jit(solution)/shard_map/ppermute | solution.py:26
  17.8 10.1 %collective-permute-start.8 = (bf16[128,1664]{1,0:T(8,128)(2,1)S(1)}, bf16[128,1664]{1,0:T(8,128)(2,1)S(1)}, u32[]{:S(2)}, u32[]{:S(2)}) collective-permute-start(bf16[128,1664]{1,0:T(8,128)(2,1)S(1)} %get-tuple-element.24), channel_id=1, source_target_pairs={{8,0},{16,8},{24,16},{0,24},{9,1},{17,9},{25,17},{1,25},{10,2},{18... | collective-permute-start | bytes 1277960 | tf_op jit(solution)/shard_map/ppermute | solution.py:22
  21.0 5.7 %collective-permute-start.11 = (f32[2,128]{1,0:T(2,128)S(1)}, f32[2,128]{1,0:T(2,128)S(1)}, u32[]{:S(2)}, u32[]{:S(2)}) collective-permute-start(f32[2,128]{1,0:T(2,128)S(1)} %get-tuple-element.26), channel_id=1, source_target_pairs={{14,0},{15,1},{12,2},{13,3},{10,4},{11,5},{8,6},{9,7},{22,8},{23,9... | collective-permute-start | bytes 3080 | tf_op jit(solution)/shard_map/ppermute | solution.py:312
  22.3 4.8 %collective-permute-start.10 = (f32[2,128]{1,0:T(2,128)S(1)}, f32[2,128]{1,0:T(2,128)S(1)}, u32[]{:S(2)}, u32[]{:S(2)}) collective-permute-start(f32[2,128]{1,0:T(2,128)S(1)} %get-tuple-element.26), channel_id=1, source_target_pairs={{12,0},{13,1},{14,2},{15,3},{8,4},{9,5},{10,6},{11,7},{20,8},{21,9... | collective-permute-start | bytes 3080 | tf_op jit(solution)/shard_map/ppermute | solution.py:312
  23.6 3.9 %collective-permute-start.9 = (f32[2,128]{1,0:T(2,128)S(1)}, f32[2,128]{1,0:T(2,128)S(1)}, u32[]{:S(2)}, u32[]{:S(2)}) collective-permute-start(f32[2,128]{1,0:T(2,128)S(1)} %get-tuple-element.26), channel_id=1, source_target_pairs={{10,0},{11,1},{8,2},{9,3},{14,4},{15,5},{12,6},{13,7},{18,8},{19,9... | collective-permute-start | bytes 3080 | tf_op jit(solution)/shard_map/ppermute | solution.py:312
